TPU v7x, 128 devices: a whole 4x4x4 slice. The times are simulated.
128 devices in a mesh: wide: 16 (over x, z), narrow: 8 (over y, core).
Axes of the slice: x: 4, y: 4, z: 4, core: 2. Of those that a mesh axis runs over, the one named last changes fastest.
Arguments:
- activations: bfloat16 [4096, 16384], P('wide', 'narrow'), may hold values from -6 to 6
- grad_out: bfloat16 [4096, 8192], P('narrow', 'wide'), may hold values from -0.09375 to 0.09375
- momentum: float32 [8192, 16384], P('wide', 'narrow'), may hold values from -90 to 90
- right_factor: float32 [16384, 512], P('narrow'), may hold values from -0.046875 to 0.046875
Outputs:
- new_momentum: float32 [8192, 16384], P('wide', 'narrow')
- new_right: float32 [16384, 512], P('narrow')
- update: bfloat16 [8192, 16384], P('wide', 'narrow')
All inputs are finite; a program needn't handle non-finite values.
Results may differ from a plain program's by a relative error of at most 0.0012.
Values may be sent and summed in bfloat16 or wider, within the bound.
A program may use at most 128 MiB of HBM per device.

v0:
```python
import math

import jax
import jax.numpy as jnp
from jax import lax
from jax.sharding import Mesh
from jax.sharding import PartitionSpec as P

DOUT = 8192
DIN = 16384
RANK = 512
NARROW = ("narrow_0", "narrow_1")
WIDE = ("wide_0", "wide_1")


FEEDBACK = 0.05
EPSILON = 1e-06


def sent_to_all(array, axis):
    devices = lax.axis_size(axis)
    return lax.all_to_all(
        jnp.broadcast_to(array[None], (devices, *array.shape)), axis, 0, 0, tiled=True
    )


def laid_out(tiles, dim):
    tiles = jnp.moveaxis(tiles, 0, dim)
    lengths = tiles.shape
    return tiles.reshape(*lengths[:dim], lengths[dim] * lengths[dim + 1], *lengths[dim + 2 :])


def gathered_by_axis(array, axes, dim):
    far, near = axes
    tiles = sent_to_all(sent_to_all(array, far), near)
    return laid_out(tiles.swapaxes(0, 1).reshape(-1, *array.shape), dim)


def split_up(array, dim, devices):
    before, after = (array.shape[:dim], array.shape[dim + 1 :])
    return jnp.moveaxis(array.reshape(*before, devices, -1, *after), dim, 0)


def summed_on_arrival(array, axis, dim):
    tiles = split_up(array, dim, lax.axis_size(axis))
    arrived = lax.all_to_all(tiles, axis, split_axis=0, concat_axis=0, tiled=True)
    return arrived.sum(axis=0)


def padded_to(lines, devices):
    spare = -len(lines) % devices
    return jnp.pad(lines, [(0, spare)] + [(0, 0)] * (lines.ndim - 1))


def summed_rows(array, axes, dim):
    far, near = axes
    own = summed_on_arrival(split_up(array, dim, lax.axis_size(far)), near, dim + 1)
    return jnp.sum(lax.all_to_all(own, far, 0, 0, tiled=True), axis=0)


def total_of(array, axes):
    lines = array.reshape(-1, array.shape[-1])
    padded = padded_to(lines, lax.axis_size(axes[0]) * lax.axis_size(axes[1]))
    whole = gathered_by_axis(summed_rows(padded, axes, 0), axes, 0)
    return lax.slice_in_dim(whole, 0, len(lines)).reshape(array.shape)


def gathered_copies(array, axis, dim):
    return laid_out(sent_to_all(array, axis), dim)


def own_rows(total, axes):
    for axis in axes:
        total = lax.psum_scatter(total, axis, scatter_dimension=0, tiled=True)
    return total


def taken_together(array, axis):
    return sent_to_all(array, axis).sum(axis=0)


def over_axes(array, axes):
    far, near = axes
    nearer = taken_together(array, near)
    return taken_together(nearer, far)


def body(activations, grad_out, momentum, right_factor):
    highest = lax.Precision.HIGHEST
    out_rows = gathered_by_axis(grad_out, ("narrow_0", "narrow_1"), 0)
    gradient = lax.dot_general(
        out_rows,
        lax.all_gather(activations, WIDE, axis=0, tiled=True),
        (((0,), (0,)), ((), ())),
        preferred_element_type=jnp.float32,
    )
    buffer = momentum + gradient
    left_share = summed_on_arrival(
        jnp.dot(buffer, right_factor, precision=highest, preferred_element_type=jnp.float32),
        NARROW,
        0,
    )
    gram_local = jnp.dot(
        left_share.T, left_share, precision=highest, preferred_element_type=jnp.float32
    )
    gram_matrix = total_of(gram_local, (("wide_0", "wide_1", "narrow_0"), "narrow_1"))
    lower_factor = jnp.linalg.cholesky(gram_matrix)
    ortho_share = jax.scipy.linalg.solve_triangular(lower_factor, left_share.T, lower=True).T
    ortho_left = gathered_copies(ortho_share, NARROW, 0)
    right_share = own_rows(
        lax.dot_general(
            buffer,
            ortho_left,
            (((0,), (0,)), ((), ())),
            precision=highest,
            preferred_element_type=jnp.float32,
        ),
        WIDE,
    )
    col_squares = over_axes(
        jnp.sum(right_share * right_share, axis=0), (("wide_0", "wide_1", "narrow_0"), "narrow_1")
    )
    right_raw = lax.all_gather(right_share, WIDE, axis=0, tiled=True)
    feedback = lax.dot_general(
        ortho_left,
        right_raw,
        (((1,), (1,)), ((), ())),
        precision=highest,
        preferred_element_type=jnp.float32,
    )
    new_momentum = buffer - FEEDBACK * feedback
    new_right = right_raw / (jnp.sqrt(col_squares) + EPSILON)
    update_scale = math.sqrt(DOUT * DIN / RANK)
    product = lax.dot_general(
        ortho_left,
        new_right,
        (((1,), (1,)), ((), ())),
        precision=highest,
        preferred_element_type=jnp.float32,
    )
    update = (update_scale * product).astype(jnp.bfloat16)
    return (new_momentum, new_right, update)


def solution(mesh):
    finer = Mesh(mesh.devices.reshape(4, 4, 4, 2), ("wide_0", "wide_1", "narrow_0", "narrow_1"))
    in_specs = (P(WIDE, NARROW), P(NARROW, WIDE), P(WIDE, NARROW), P(NARROW, None))
    out_specs = (P(WIDE, NARROW), P(NARROW, None), P(WIDE, NARROW))
    return jax.shard_map(body, mesh=finer, in_specs=in_specs, out_specs=out_specs, check_vma=False)
```

profile of v0, /device:TPU:1, one launch (start us, length us, event | category | flops | bytes accessed | tf_op | source)
XLA Modules:
  0.0 525.0 jit_solution(6163401556393695659)
XLA Ops:
  7.2 0.7 all-gather.3.cloned.1.call-update
  7.9 1.2 broadcast_in_dim.15
  9.1 30.2 %all_to_all.52 = bf16[4,512,512]{2,1,0:T(8,128)(2,1)S(1)} all-to-all(bf16[4,512,512]{2,1,0:T(8,128)(2,1)S(1)} %broadcast_in_dim.15), channel_id=1, replica_groups=mesh['wide_0'=4,'wide_1'=4,'narrow_0'=4,'narrow_1'=2] {'narrow_0'}, dimensions={0} | all-to-all | bytes 4194304 | tf_op jit(solution)/shard_map/all_to_all | solution.py:22
  39.3 0.4 broadcast_in_dim.16
  39.7 8.6 %all_to_all.53 = bf16[2,4,512,512]{3,2,1,0:T(8,128)(2,1)S(1)} all-to-all(bf16[2,4,512,512]{3,2,1,0:T(8,128)(2,1)S(1)} %broadcast_in_dim.16), channel_id=1, replica_groups=mesh['wide_0'=4,'wide_1'=4,'narrow_0'=4,'narrow_1'=2] {'narrow_1'}, dimensions={0} | all-to-all | bytes 8388608 | tf_op jit(solution)/shard_map/all_to_all | solution.py:22
  48.3 2.5 copy.28
  50.8 74.0 %all-gather.3.cloned.1.call-done = bf16[4096,2048]{1,0:T(8,128)(2,1)} async-done(((bf16[256,2048]{1,0:T(8,128)(2,1)}), bf16[4096,2048]{1,0:T(8,128)(2,1)}) %all-gather.3.cloned.1.call-update) | async-done | bytes 16777232 | tf_op jit(solution)/shard_map/all_gather | solution.py:93
  124.8 14.4 %convolution_add_fusion = f32[512,2048]{1,0:T(8,128)S(1)} fusion(f32[512,2048]{1,0:T(8,128)} %param.6, bf16[4096,512]{1,0:T(8,128)(2,1)} %bitcast.79, bf16[4096,2048]{1,0:T(8,128)(2,1)} %all-gather.3.cloned.1.call-done), kind=kOutput, calls=%fused_computation.4 | convolution fusion | flops 8590983168 | bytes 29360128 | tf_op jit(solution)/shard_map/dot_general | solution.py:91
  139.2 6.9 %fusion.33 = f32[512,512]{1,0:T(8,128)S(1)} fusion(f32[512,2048]{1,0:T(8,128)S(1)} %convolution_add_fusion, f32[2048,512]{1,0:T(8,128)S(1)} %copy-done.4), kind=kOutput, calls=%fused_computation.76 | convolution fusion | flops 6442450944 | bytes 9437184 | tf_op jit(solution)/shard_map/dot_general | solution.py:99
  146.1 19.9 %all_to_all.54 = f32[8,64,512]{2,1,0:T(8,128)S(1)} all-to-all(f32[8,64,512]{2,1,0:T(8,128)S(1)} %bitcast.78), channel_id=1, replica_groups=mesh['wide_0'=4,'wide_1'=4,'narrow_0'=4,'narrow_1'=2] {'narrow_0','narro..., dimensions={0} | all-to-all | bytes 2097152 | tf_op jit(solution)/shard_map/all_to_all | solution.py:46
  166.2 1.0 convolution_bitcast_fusion
  167.2 5.2 all_to_all.55
  172.5 0.3 copy.31
  172.9 18.3 %all_to_all.56 = f32[64,4,512]{2,1,0:T(4,128)S(1)} all-to-all(f32[64,4,512]{2,1,0:T(4,128)S(1)} %copy.31), channel_id=1, replica_groups=mesh['wide_0'=4,'wide_1'=4,'narrow_0'=4,'narrow_1'=2] {'wide_0','wide_1'..., dimensions={0} | all-to-all | bytes 1048576 | tf_op jit(solution)/shard_map/all_to_all | solution.py:58
  191.2 0.9 broadcast_in_dim.18
  192.1 4.9 all-to-all-start.5
  197.1 10.7 %all-to-all-done.5 = f32[64,4,512]{2,1,0:T(4,128)S(1)} async-done(((f32[64,4,512]{2,1,0:T(4,128)}), f32[64,4,512]{2,1,0:T(4,128)S(1)}, u32[]{:S(2)}, u32[]{:S(2)}) %all-to-all-start.5) | async-done | bytes 524320 | tf_op jit(solution)/shard_map/all_to_all | solution.py:22
  208.0 7.4 %all_to_all.57 = f32[2,64,4,512]{3,2,1,0:T(4,128)S(1)} all-to-all(f32[2,64,4,512]{3,2,1,0:T(4,128)S(1)} %broadcast_in_dim.19), channel_id=1, replica_groups=mesh['wide_0'=4,'wide_1'=4,'narrow_0'=4,'narrow_1'=2] {'narrow_1'}, dimensions={0} | all-to-all | bytes 2097152 | tf_op jit(solution)/shard_map/all_to_all | solution.py:22
  215.6 0.4 reshape_reshape.8
  216.0 0.3 copy.33
  216.3 0.2 fusion
  216.5 11.7 %cholesky.104 = f32[128,128]{1,0:T(8,128)S(1)} custom-call(f32[128,128]{1,0:T(8,128)S(1)} %cholesky.266), custom_call_target="Cholesky" | custom-call | tf_op jit(solution)/shard_map/jit(cholesky)/cholesky | solution.py:107
  228.4 9.8 %custom-call.31 = f32[1,128,128]{1,2,0:T(8,128)S(1)} custom-call(f32[1,128,128]{2,1,0:T(8,128)S(1)} %get-tuple-element.30), custom_call_target="InvertDiagBlocksLowerTriangular" | custom-call | tf_op jit(solution)/shard_map/jit(cholesky)/cholesky | solution.py:107
  238.2 0.3 constant_dynamic-update-slice_fusion.3
  238.6 0.3 convolution_subtract_fusion
  238.9 11.7 %cholesky.217 = f32[128,128]{1,0:T(8,128)S(1)} custom-call(f32[128,128]{1,0:T(8,128)S(1)} %cholesky.270), custom_call_target="Cholesky" | custom-call | tf_op jit(solution)/shard_map/jit(cholesky)/cholesky | solution.py:107
  250.7 10.0 %custom-call.32 = f32[1,128,128]{1,2,0:T(8,128)S(1)} custom-call(f32[1,128,128]{2,1,0:T(8,128)S(1)} %get-tuple-element.27), custom_call_target="InvertDiagBlocksLowerTriangular" | custom-call | tf_op jit(solution)/shard_map/jit(cholesky)/cholesky | solution.py:107
  260.6 0.3 convolution_dynamic-update-slice_fusion
  260.9 0.4 convolution_subtract_fusion.1
  261.3 11.7 %cholesky.238 = f32[128,128]{1,0:T(8,128)S(1)} custom-call(f32[128,128]{1,0:T(8,128)S(1)} %cholesky.275), custom_call_target="Cholesky" | custom-call | tf_op jit(solution)/shard_map/jit(cholesky)/cholesky | solution.py:107
  273.0 0.7 compare_reduce_fusion.1
  273.8 9.8 %custom-call.33 = f32[1,128,128]{1,2,0:T(8,128)S(1)} custom-call(f32[1,128,128]{2,1,0:T(8,128)S(1)} %get-tuple-element.24), custom_call_target="InvertDiagBlocksLowerTriangular" | custom-call | tf_op jit(solution)/shard_map/jit(cholesky)/cholesky | solution.py:107
  283.6 0.2 convolution_dynamic-update-slice_fusion.1
  283.8 0.4 convolution_subtract_fusion.2
  284.2 11.9 %cholesky.255 = f32[128,128]{1,0:T(8,128)S(1)} custom-call(f32[128,128]{1,0:T(8,128)S(1)} %convolution_subtract_fusion.2), custom_call_target="Cholesky" | custom-call | tf_op jit(solution)/shard_map/jit(cholesky)/cholesky | solution.py:107
  296.1 0.6 compare_reduce_fusion
  296.7 0.7 compare_reduce_fusion.2
  300.1 8.5 %while.1 = (s32[]{:T(128)}, f32[512,512]{1,0:T(8,128)S(1)}, s32[4,2]{0,1:T(2,128)S(1)}, f32[4,128,128]{2,1,0:T(8,128)S(1)}, s32[]{:T(128)}) while((s32[]{:T(128)}, f32[512,512]{1,0:T(8,128)S(1)}, s32[4,2]{0,1:T(2,128)S(1)}, f32[4,128,128]{2,1,0:T(8,128)S(1)}, s32[]{:T(128)}) %tuple.31), condition=%wide.while_cond, body=%wide.while_body.sunk | while | flops 2 | bytes 131181 | solution.py:108
  300.2 0.6 fusion.51
  300.8 1.4 bitcast_dynamic-update-slice_fusion.2
  302.3 0.6 fusion.51
  302.9 1.4 bitcast_dynamic-update-slice_fusion.2
  304.4 0.6 fusion.51
  305.0 1.4 bitcast_dynamic-update-slice_fusion.2
  306.5 0.6 fusion.51
  307.1 1.4 bitcast_dynamic-update-slice_fusion.2
  308.6 39.3 %custom-call.34 = f32[4,128,128]{1,2,0:T(8,128)S(1)} custom-call(f32[4,128,128]{2,1,0:T(8,128)S(1)} %get-tuple-element.10), custom_call_target="InvertDiagBlocksLowerTriangular" | custom-call | tf_op jit(solution)/shard_map/jit(_solve_triangular)/triangular_solve | solution.py:108
  347.9 0.2 fusion.20
  348.1 0.2 convolution_subtract_fusion.5
  348.5 0.3 convolution_subtract_fusion.4
  348.8 0.2 fusion.17
  349.0 0.4 convolution_subtract_fusion.3
  349.4 0.2 fusion.16
  349.7 17.9 %all_to_all.58 = f32[8,64,512]{2,1,0:T(8,128)S(1)} all-to-all(f32[8,64,512]{2,1,0:T(8,128)S(1)} %broadcast_in_dim.20), channel_id=1, replica_groups=mesh['wide_0'=4,'wide_1'=4,'narrow_0'=4,'narrow_1'=2] {'narrow_0','narro..., dimensions={0} | all-to-all | bytes 2097152 | tf_op jit(solution)/shard_map/all_to_all | solution.py:22
  367.6 8.4 %fusion.34 = f32[2048,512]{1,0:T(8,128)} fusion(f32[512,2048]{1,0:T(8,128)S(1)} %copy-done.1, f32[512,512]{1,0:T(8,128)S(1)} %bitcast.75), kind=kOutput, calls=%fused_computation.77 | convolution fusion | flops 6442450944 | bytes 9437184 | tf_op jit(solution)/shard_map/dot_general | solution.py:111
  376.0 43.0 %reduce-scatter.3.cloned.1.call-done = f32[512,512]{1,0:T(8,128)} async-done(((f32[2048,512]{1,0:T(8,128)}), f32[512,512]{1,0:T(8,128)}) %reduce-scatter.3.cloned.1.call-update) | async-done | bytes 1048592 | tf_op jit(solution)/shard_map/reduce_scatter | solution.py:74
  419.1 24.2 %reduce-scatter.5.cloned.1.call-done = f32[128,512]{1,0:T(8,128)} async-done(((f32[512,512]{1,0:T(8,128)}), f32[128,512]{1,0:T(8,128)}) %reduce-scatter.5.cloned.1.call-update) | async-done | bytes 262160 | tf_op jit(solution)/shard_map/reduce_scatter | solution.py:74
  443.3 1.0 multiply_reduce_fusion
  444.3 5.8 %all_to_all.59 = f32[2,1,512]{2,1,0:T(1,128)S(1)} all-to-all(f32[2,1,512]{2,1,0:T(1,128)S(1)} %broadcast_in_dim.21), channel_id=1, replica_groups=mesh['wide_0'=4,'wide_1'=4,'narrow_0'=4,'narrow_1'=2] {'narrow_1'}, dimensions={0} | all-to-all | bytes 8192 | tf_op jit(solution)/shard_map/all_to_all | solution.py:22
  450.2 17.3 %all_to_all.60 = f32[64,1,512]{2,1,0:T(1,128)S(1)} all-to-all(f32[64,1,512]{2,1,0:T(1,128)S(1)} %broadcast_in_dim.22), channel_id=1, replica_groups=mesh['wide_0'=4,'wide_1'=4,'narrow_0'=4,'narrow_1'=2] {'wide_0','wide_1'..., dimensions={0} | all-to-all | bytes 262144 | tf_op jit(solution)/shard_map/all_to_all | solution.py:22
  467.6 31.0 %all-gather.5.cloned.1.call-done = f32[2048,512]{1,0:T(8,128)} async-done(((f32[128,512]{1,0:T(8,128)}), f32[2048,512]{1,0:T(8,128)}) %all-gather.5.cloned.1.call-update) | async-done | bytes 4194320 | tf_op jit(solution)/shard_map/all_gather | solution.py:123
  498.6 2.7 broadcast_divide_fusion
  501.4 8.1 %multiply_convert_fusion = bf16[512,2048]{1,0:T(8,128)(2,1)} fusion(f32[512,512]{1,0:T(8,128)S(1)} %bitcast.76, f32[2048,512]{1,0:T(8,128)S(1)} %broadcast_divide_fusion), kind=kOutput, calls=%fused_computation.2 | convolution fusion | flops 6444548096 | bytes 7340032 | tf_op jit(solution)/shard_map/dot_general | solution.py:134
  509.5 8.5 %multiply_subtract_fusion = f32[512,2048]{1,0:T(8,128)} fusion(f32[512,2048]{1,0:T(8,128)S(1)} %copy-done.2, f32[512,512]{1,0:T(8,128)S(1)} %bitcast.77, f32[2048,512]{1,0:T(8,128)S(1)} %copy-done.3), kind=kOutput, calls=%fused_computation.3 | convolution fusion | flops 6444548096 | bytes 13631488 | tf_op jit(solution)/shard_map/dot_general | solution.py:124
  (49 shorter events, 2.2 us)
Async XLA Ops:
  7.2 117.7 %all-gather.3.cloned.1.call-start = ((), (), s32[]{:S(2)}) async-start(), calls=%async_computation.12 | async-start | bytes 17825792 | tf_op jit(solution)/shard_map/all_gather | solution.py:93
  124.8 14.4 %copy-start.4 = (f32[2048,512]{1,0:T(8,128)S(1)}, f32[2048,512]{1,0:T(8,128)}, u32[]{:S(2)}) copy-start(f32[2048,512]{1,0:T(8,128)} %param.7) | copy-start | bytes 12582916
  139.2 6.9 %copy-start = (f32[512,2048]{1,0:T(8,128)}, f32[512,2048]{1,0:T(8,128)S(1)}, u32[]{:S(2)}) copy-start(f32[512,2048]{1,0:T(8,128)S(1)} %convolution_add_fusion) | copy-start | bytes 12582916
  192.1 15.8 %all-to-all-start.5 = ((f32[64,4,512]{2,1,0:T(4,128)}), f32[64,4,512]{2,1,0:T(4,128)S(1)}, u32[]{:S(2)}, u32[]{:S(2)}) async-start(f32[64,4,512]{2,1,0:T(4,128)} %broadcast_in_dim.18), calls=%async_computation.5 | async-start | bytes 1048576 | tf_op jit(solution)/shard_map/all_to_all | solution.py:22
  197.0 222.0 %reduce-scatter.3.cloned.1.call-start = ((), (), s32[]{:S(2)}) async-start(), calls=%async_computation.13 | async-start | bytes 5242880 | tf_op jit(solution)/shard_map/reduce_scatter | solution.py:74
  347.9 19.7 %copy-start.1 = (f32[512,2048]{1,0:T(8,128)S(1)}, f32[512,2048]{1,0:T(8,128)}, u32[]{:S(2)}) copy-start(f32[512,2048]{1,0:T(8,128)} %copy-done) | copy-start | bytes 12582916
  376.0 67.3 %reduce-scatter.5.cloned.1.call-start = ((), (), s32[]{:S(2)}) async-start(), calls=%async_computation.14 | async-start | bytes 1310720 | tf_op jit(solution)/shard_map/reduce_scatter | solution.py:74
  419.1 79.6 %all-gather.5.cloned.1.call-start = ((), (), s32[]{:S(2)}) async-start(), calls=%async_computation.15 | async-start | bytes 4456448 | tf_op jit(solution)/shard_map/all_gather | solution.py:123
  501.4 8.2 %copy-start.5 = (f32[2048,512]{1,0:T(8,128)}, f32[2048,512]{1,0:T(8,128)S(1)}, u32[]{:S(2)}) copy-start(f32[2048,512]{1,0:T(8,128)S(1)} %broadcast_divide_fusion) | copy-start | bytes 12582916
  501.4 8.2 %copy-start.2 = (f32[512,2048]{1,0:T(8,128)S(1)}, f32[512,2048]{1,0:T(8,128)}, u32[]{:S(2)}) copy-start(f32[512,2048]{1,0:T(8,128)} %copy-done) | copy-start | bytes 12582916
  501.4 8.2 %copy-start.3 = (f32[2048,512]{1,0:T(8,128)S(1)}, f32[2048,512]{1,0:T(8,128)}, u32[]{:S(2)}) copy-start(f32[2048,512]{1,0:T(8,128)} %all-gather.5.cloned.1.call-done) | copy-start | bytes 12582916
Sparse Core Ops, SparseCore 0:
  10.1 114.6 all-gather.2
  376.1 42.8 reduce-scatter.2
  421.6 21.6 reduce-scatter.4
  445.3 53.2 all-gather.4
where the time goes:
time: 536 us; the launch traced here: 525 us
  waiting for transfers between devices  184 us (34%)
  blocking collectives  131 us (24%)
  other arithmetic  123 us (23%)
  matrix products  50.7 us (9%)
  between operations  17.1 us (3%)
  local copies, waits for them, and re-layouts  15.1 us (3%)
    all_to_all x6, blocking collectives, sent_to_all(): lax.all_to_all(jnp.broadcast_to(array[None], (devices, *array.shape)), ax...  87.2 us
    another operation x14, other arithmetic, body(): lower_factor = jnp.linalg.cholesky(gram_matrix)  78.8 us
    all_gather x1, waiting for transfers between devices, body(): lax.all_gather(activations, WIDE, axis=0, tiled=True)  74 us
    reduce_scatter x2, waiting for transfers between devices, own_rows(): total = lax.psum_scatter(total, axis, scatter_dimension=0, tiled=True)  67.2 us
    another operation x3, other arithmetic, body(): jax.scipy.linalg.solve_triangular(lower_factor, left_share.T, lower=True)  39.4 us
    all_gather x1, waiting for transfers between devices, body(): right_raw = lax.all_gather(right_share, WIDE, axis=0, tiled=True)  31 us
    all_to_all x2, blocking collectives, summed_on_arrival(): lax.all_to_all(tiles, axis, split_axis=0, concat_axis=0, tiled=True)  25.1 us
    all_to_all x1, blocking collectives, summed_rows(): return jnp.sum(lax.all_to_all(own, far, 0, 0, tiled=True), axis=0)  18.3 us
  transfers between devices with their start and end apart: 5, of which 5 were waited for; matrix products, arithmetic and copies ran while one was open for 1% of the time, Pallas kernels for 0%

commit v1 on v0

v1 whole, which is shorter than its diff:
```python
import math

import jax
import jax.numpy as jnp
from jax import lax
from jax.experimental import pallas as pl
from jax.experimental.pallas import tpu as pltpu
from jax.sharding import Mesh
from jax.sharding import PartitionSpec as P

DOUT = 8192
DIN = 16384
RANK = 512
X, Z, Y, C = "wide_0", "wide_1", "narrow_0", "narrow_1"
NARROW = (Y, C)
WIDE = (X, Z)
FEEDBACK = 0.05
EPSILON = 1e-06
F32 = jnp.float32
BF16 = jnp.bfloat16
VMEM = pl.BlockSpec(memory_space=pltpu.VMEM)
MESH = pl.DeviceIdType.MESH

def eliminated(rows):
    lane = lax.broadcasted_iota(jnp.int32, (8, 128), 1)
    sub = lax.broadcasted_iota(jnp.int32, (8, 128), 0)
    groups = len(rows)
    for p in range(groups):
        here = rows[p]
        cols = [jnp.broadcast_to(here[:, 8 * p + k : 8 * p + k + 1], (8, 128)) for k in range(8)]
        a = [[jnp.broadcast_to(cols[k][i : i + 1, :], (8, 128)) if k <= i else None for k in range(8)] for i in range(8)]
        low = [[None] * 8 for _ in range(8)]
        root = [None] * 8
        for k in range(8):
            root[k] = lax.rsqrt(a[k][k])
            for i in range(k + 1, 8):
                low[i][k] = a[i][k] * root[k]
            for i in range(k + 1, 8):
                for j in range(k + 1, i + 1):
                    a[i][j] = a[i][j] - low[i][k] * low[j][k]
        inside = (lane >= 8 * p) & (lane < 8 * p + 8)
        unit = jnp.where(lane == sub + 8 * p, 1.0, 0.0).astype(F32)
        source = jnp.where(inside, unit, here)
        y = []
        for k in range(8):
            value = jnp.broadcast_to(source[k : k + 1, :], (8, 128))
            for m in range(k):
                value = value - low[k][m] * y[m]
            y.append(value * root[k])
        done = y[0]
        for k in range(1, 8):
            done = jnp.where(sub == k, y[k], done)
        rows[p] = done
        for g in range(p + 1, groups):
            c = []
            total = jnp.where(inside, 0.0, rows[g])
            for k in range(8):
                value = jnp.broadcast_to(rows[g][:, 8 * p + k : 8 * p + k + 1], (8, 128))
                for m in range(k):
                    value = value - low[k][m] * c[m]
                c.append(value * root[k])
                total = total - c[k] * y[k]
            rows[g] = total
    return rows

def factor_kernel(c_ref, out_ref, s_ref):
    hi = lax.Precision.HIGHEST
    s_ref[...] = c_ref[...]
    row = lax.broadcasted_iota(jnp.int32, (128, 128), 0)
    col = lax.broadcasted_iota(jnp.int32, (128, 128), 1)
    for b in range(4):
        o = 128 * b
        rows = [s_ref[o + 8 * g : o + 8 * g + 8, o : o + 128] for g in range(16)]
        inv = jnp.concatenate(eliminated(rows), axis=0)
        inv = jnp.where(row >= col, inv, 0.0)
        s_ref[o : o + 128, o : o + 128] = jnp.where(row == col, 1.0, 0.0).astype(F32)
        y = jnp.dot(inv, s_ref[o : o + 128, :], precision=hi, preferred_element_type=F32)
        s_ref[o : o + 128, :] = y
        if b < 3:
            rest = y[:, o + 128 :]
            s_ref[o + 128 :, o : o + 128] = jnp.zeros((384 - o, 128), F32)
            s_ref[o + 128 :, :] = s_ref[o + 128 :, :] - lax.dot_general(
                rest, y, (((0,), (0,)), ((), ())), precision=hi, preferred_element_type=F32)
    row = lax.broadcasted_iota(jnp.int32, (512, 512), 0)
    col = lax.broadcasted_iota(jnp.int32, (512, 512), 1)
    out_ref[...] = jnp.where(row >= col, s_ref[...], 0.0)

def inverse_factor(c):
    return pl.pallas_call(factor_kernel, out_shape=jax.ShapeDtypeStruct((512,512),F32),
        in_specs=[pl.BlockSpec(memory_space=pltpu.VMEM)], out_specs=pl.BlockSpec(memory_space=pltpu.VMEM),
        scratch_shapes=[pltpu.VMEM((512,512),F32)],
        compiler_params=pltpu.CompilerParams(vmem_limit_bytes=32<<20))(c)


def halves(value):
    high = value.astype(BF16)
    return high, (value - high.astype(F32)).astype(BF16)


def dot3(left, right, dims):
    a, b = halves(left)
    c, d = halves(right)
    one = lambda u, v: lax.dot_general(u, v, (dims, ((), ())), preferred_element_type=F32)
    return one(a, c) + (one(a, d) + one(b, c))


def partner(axis, step):
    size = 2 if axis == C else 4
    return lax.rem(lax.axis_index(axis) + step, size)


def greet(peers):
    barrier = pltpu.get_barrier_semaphore()
    for peer in peers:
        pl.semaphore_signal(barrier, inc=1, device_id=peer, device_id_type=MESH)
    pl.semaphore_wait(barrier, len(peers))


def line_peers(axes):
    peers = []
    for axis in axes:
        for step in range(1, 2 if axis == C else 4):
            peers.append({axis: partner(axis, step)})
    return peers


def sent(send, recv, phase, axis, source, target):
    copies = []
    for step in range(1, 2 if axis == C else 4):
        to = partner(axis, step)
        copy = pltpu.make_async_remote_copy(
            src_ref=source(to),
            dst_ref=target(to),
            send_sem=send.at[phase, step - 1],
            recv_sem=recv.at[phase, step - 1],
            device_id={axis: to},
            device_id_type=MESH,
        )
        copy.start()
        copies.append(copy)
    return copies


def all_of(copies):
    for copy in copies:
        copy.wait()


def left_kernel(part, left, gram, pair, half, share, block, gx, gz, send, recv):
    x, z, y, c = (lax.axis_index(a) for a in (X, Z, Y, C))
    greet(line_peers((X, Z, Y, C)))
    all_of(sent(send, recv, 0, C, lambda to: part.at[to], lambda to: pair))
    half[...] = part[c] + pair[...]
    copies = sent(send, recv, 1, Y, lambda to: half.at[to], lambda to: share.at[y])
    share[y] = half[y]
    all_of(copies)
    left[c, y] = (share[0] + share[1]) + (share[2] + share[3])
    all_of(sent(send, recv, 2, Y, lambda to: left.at[c, y], lambda to: left.at[c, y]))
    all_of(sent(send, recv, 3, C, lambda to: left.at[c], lambda to: left.at[c]))
    whole = left[...].reshape(RANK, RANK)
    for index in range(4):
        @pl.when(y == index)
        def _():
            own = whole[:, 128 * index : 128 * index + 128]
            block[...] = dot3(own, whole, ((0,), (0,))).reshape(2, 4, 16, RANK)
    copies = sent(send, recv, 4, X, lambda to: block.at[c, to], lambda to: gx.at[x])
    gx[x] = block[c, x]
    all_of(copies)
    gz[z] = (gx[0] + gx[1]) + (gx[2] + gx[3])
    all_of(sent(send, recv, 5, Z, lambda to: gz.at[z], lambda to: gz.at[z]))
    gram[y, c, x] = (gz[0] + gz[1]) + (gz[2] + gz[3])
    all_of(sent(send, recv, 6, X, lambda to: gram.at[y, c, x], lambda to: gram.at[y, c, x]))
    all_of(sent(send, recv, 7, Y, lambda to: gram.at[y, c], lambda to: gram.at[y, c]))
    all_of(sent(send, recv, 8, C, lambda to: gram.at[:, c], lambda to: gram.at[:, c]))


def left_and_gram(part):
    left, gram = pl.pallas_call(
        left_kernel,
        out_shape=(
            jax.ShapeDtypeStruct((2, 4, 64, RANK), F32),
            jax.ShapeDtypeStruct((4, 2, 4, 16, RANK), F32),
        ),
        in_specs=[VMEM],
        out_specs=(VMEM, VMEM),
        scratch_shapes=[
            pltpu.VMEM((4, 64, RANK), F32),
            pltpu.VMEM((4, 64, RANK), F32),
            pltpu.VMEM((4, 64, RANK), F32),
            pltpu.VMEM((2, 4, 16, RANK), F32),
            pltpu.VMEM((4, 16, RANK), F32),
            pltpu.VMEM((4, 16, RANK), F32),
            pltpu.SemaphoreType.DMA((9, 3)),
            pltpu.SemaphoreType.DMA((9, 3)),
        ],
        compiler_params=pltpu.CompilerParams(
            collective_id=1, has_side_effects=True, vmem_limit_bytes=40 << 20
        ),
        cost_estimate=pl.CostEstimate(flops=1 << 26, bytes_accessed=64 << 20, transcendentals=0),
    )(part.reshape(2, 4, 64, RANK))
    return left.reshape(RANK, RANK), gram.reshape(RANK, RANK)


def right_kernel(part, out, from_x, from_z, sum_x, sum_z, end_x, end_z, send, recv):
    x, z = lax.axis_index(X), lax.axis_index(Z)
    greet(line_peers((X, Z)))
    a = sent(send, recv, 0, X, lambda to: part.at[to, :, 0], lambda to: from_x.at[x])
    b = sent(send, recv, 1, Z, lambda to: part.at[:, to, 1], lambda to: from_z.at[z])
    from_x[x] = part[x, :, 0]
    from_z[z] = part[:, z, 1]
    all_of(a)
    sum_x[...] = (from_x[0] + from_x[1]) + (from_x[2] + from_x[3])
    a = sent(send, recv, 2, Z, lambda to: sum_x.at[to], lambda to: end_z.at[z])
    all_of(b)
    sum_z[...] = (from_z[0] + from_z[1]) + (from_z[2] + from_z[3])
    b = sent(send, recv, 3, X, lambda to: sum_z.at[to], lambda to: end_x.at[x])
    end_z[z] = sum_x[z]
    end_x[x] = sum_z[x]
    all_of(a)
    out[x, z, 0] = (end_z[0] + end_z[1]) + (end_z[2] + end_z[3])
    a = sent(send, recv, 4, Z, lambda to: out.at[x, z, 0], lambda to: out.at[x, z, 0])
    all_of(b)
    out[x, z, 1] = (end_x[0] + end_x[1]) + (end_x[2] + end_x[3])
    b = sent(send, recv, 5, X, lambda to: out.at[x, z, 1], lambda to: out.at[x, z, 1])
    all_of(a)
    a = sent(send, recv, 6, X, lambda to: out.at[x, :, 0], lambda to: out.at[x, :, 0])
    all_of(b)
    b = sent(send, recv, 7, Z, lambda to: out.at[:, z, 1], lambda to: out.at[:, z, 1])
    all_of(a)
    all_of(b)


def right_sum(part):
    out = pl.pallas_call(
        right_kernel,
        out_shape=jax.ShapeDtypeStruct((4, 4, 2, 64, RANK), F32),
        in_specs=[VMEM],
        out_specs=VMEM,
        scratch_shapes=[
            pltpu.VMEM((4, 4, 64, RANK), F32),
            pltpu.VMEM((4, 4, 64, RANK), F32),
            pltpu.VMEM((4, 64, RANK), F32),
            pltpu.VMEM((4, 64, RANK), F32),
            pltpu.VMEM((4, 64, RANK), F32),
            pltpu.VMEM((4, 64, RANK), F32),
            pltpu.SemaphoreType.DMA((8, 3)),
            pltpu.SemaphoreType.DMA((8, 3)),
        ],
        compiler_params=pltpu.CompilerParams(
            collective_id=2, has_side_effects=True, vmem_limit_bytes=40 << 20
        ),
        cost_estimate=pl.CostEstimate(flops=1 << 22, bytes_accessed=128 << 20, transcendentals=0),
    )(part.reshape(4, 4, 2, 64, RANK))
    return out.reshape(-1, RANK)


def raw_kernel(w_ref, p_ref, inv_ref, right, left, scale, seen, send, recv):
    y, c = lax.axis_index(Y), lax.axis_index(C)
    greet(line_peers((Y, C)))
    right[...] = dot3(w_ref[...], inv_ref[...], ((1,), (1,)))
    squares = right[...] * right[...]
    seen[4 + c] = jnp.sum(squares.reshape(-1, 8, RANK), axis=0)
    all_of(sent(send, recv, 0, C, lambda to: seen.at[4 + c], lambda to: seen.at[4 + c]))
    seen[y] = seen[4] + seen[5]
    copies = sent(send, recv, 1, Y, lambda to: seen.at[y], lambda to: seen.at[y])
    left[...] = dot3(p_ref[...], inv_ref[...], ((1,), (1,)))
    all_of(copies)
    total = jnp.sum((seen[0] + seen[1]) + (seen[2] + seen[3]), axis=0, keepdims=True)
    scale[...] = jnp.broadcast_to(jnp.sqrt(total) + EPSILON, (8, RANK))


def raw_factors(w, p, inv):
    return pl.pallas_call(
        raw_kernel,
        out_shape=(
            jax.ShapeDtypeStruct(w.shape, F32),
            jax.ShapeDtypeStruct(p.shape, F32),
            jax.ShapeDtypeStruct((8, RANK), F32),
        ),
        in_specs=[VMEM] * 3,
        out_specs=(VMEM,) * 3,
        scratch_shapes=[
            pltpu.VMEM((6, 8, RANK), F32),
            pltpu.SemaphoreType.DMA((2, 3)),
            pltpu.SemaphoreType.DMA((2, 3)),
        ],
        compiler_params=pltpu.CompilerParams(
            collective_id=3, has_side_effects=True, vmem_limit_bytes=40 << 20
        ),
        cost_estimate=pl.CostEstimate(flops=1 << 30, bytes_accessed=16 << 20, transcendentals=0),
    )(w, p, inv)


def sent_to_all(array, axis):
    devices = lax.axis_size(axis)
    return lax.all_to_all(
        jnp.broadcast_to(array[None], (devices, *array.shape)), axis, 0, 0, tiled=True
    )


def gathered_by_axis(array, axes):
    far, near = axes
    tiles = sent_to_all(sent_to_all(array, far), near)
    return tiles.swapaxes(0, 1).reshape(-1, *array.shape[1:])


def body(activations, grad_out, momentum, right_factor):
    high = lax.Precision.HIGH
    out_rows = gathered_by_axis(grad_out, NARROW)
    gradient = lax.dot_general(
        out_rows,
        lax.all_gather(activations, WIDE, axis=0, tiled=True),
        (((0,), (0,)), ((), ())),
        preferred_element_type=F32,
    )
    buffer = momentum + gradient
    part = jnp.dot(buffer, right_factor, precision=high, preferred_element_type=F32)
    left_factor, gram_matrix = left_and_gram(part)
    inverse = inverse_factor(gram_matrix)
    right_part = lax.dot_general(
        buffer, left_factor, (((0,), (0,)), ((), ())), precision=high, preferred_element_type=F32
    )
    unscaled = right_sum(right_part)
    right_raw, ortho_left, norms = raw_factors(unscaled, left_factor, inverse)
    feedback = lax.dot_general(
        ortho_left.astype(BF16),
        right_raw.astype(BF16),
        (((1,), (1,)), ((), ())),
        preferred_element_type=F32,
    )
    new_momentum = buffer - FEEDBACK * feedback
    new_right = right_raw / norms[:1]
    update_scale = math.sqrt(DOUT * DIN / RANK)
    product = lax.dot_general(
        ortho_left,
        new_right,
        (((1,), (1,)), ((), ())),
        precision=high,
        preferred_element_type=F32,
    )
    update = (update_scale * product).astype(BF16)
    return (new_momentum, new_right, update)


def solution(mesh):
    finer = Mesh(mesh.devices.reshape(4, 4, 4, 2), (X, Z, Y, C))
    in_specs = (P(WIDE, NARROW), P(NARROW, WIDE), P(WIDE, NARROW), P(NARROW, None))
    out_specs = (P(WIDE, NARROW), P(NARROW, None), P(WIDE, NARROW))
    return jax.shard_map(body, mesh=finer, in_specs=in_specs, out_specs=out_specs, check_vma=False)
```

time: 536 us -> 316 us (0.59); the launches traced: 525 us -> 316 us
  Pallas kernels: 0 us -> 143 us
  other arithmetic: 123 us -> 0.55 us
  waiting for transfers between devices: 184 us -> 74.7 us
  blocking collectives: 131 us -> 38.8 us
  matrix products: 50.7 us -> 31.7 us
    pallas_call x0 -> x4, Pallas kernels: none -> 143 us  [the longest x1 65.9 us: right_sum(): pl.pallas_call(right_kernel, out_shape=jax.ShapeDtypeStruct((4, 4, 2, 64,...]
    another operation x17 -> x0, other arithmetic: 118 us -> none  [the longest x14 78.8 us: body(): lower_factor = jnp.linalg.cholesky(gram_matrix)]
    reduce_scatter x2 -> x0, waiting for transfers between devices: 67.2 us -> none  [own_rows(): total = lax.psum_scatter(total, axis, scatter_dimension=0, tiled=True)]
    all_to_all x6 -> x2, blocking collectives: 87.2 us -> 38.8 us  [sent_to_all(): lax.all_to_all(jnp.broadcast_to(array[None], (devices, *array.shape)), ax...]
    all_to_all x3 -> x0, blocking collectives: 43.4 us -> none  [the longest x2 25.1 us: summed_on_arrival(): lax.all_to_all(tiles, axis, split_axis=0, concat_axis=0, tiled=True)]
    all_gather x1 -> x0, waiting for transfers between devices: 31 us -> none  [body(): right_raw = lax.all_gather(right_share, WIDE, axis=0, tiled=True)]
    dot_general x4 -> x3, matrix products: 24.7 us -> 12.7 us  [the longest x1 5.67 us: body(): lax.dot_general(buffer, left_factor, (((0,), (0,)), ((), ())), precision=...]
    all_to_all x1 -> x0, waiting for transfers between devices: 10.7 us -> none  [sent_to_all(): lax.all_to_all(jnp.broadcast_to(array[None], (devices, *array.shape)), ax...]
  transfers between devices with their start and end apart: 5 -> 1, of which waited for: 5 -> 1; matrix products, arithmetic and copies ran while one was open for 1% -> 1% of each run, Pallas kernels for 0% -> 0%
where the time goes in v1:
time: 316 us
  Pallas kernels  143 us (45%)
  waiting for transfers between devices  74.7 us (24%)
  blocking collectives  38.8 us (12%)
  matrix products  31.7 us (10%)
  between operations  14.2 us (4%)
  local copies, waits for them, and re-layouts  12.5 us (4%)
    all_gather x1, waiting for transfers between devices, body(): lax.all_gather(activations, WIDE, axis=0, tiled=True)  74 us
    pallas_call x1, Pallas kernels, right_sum(): pl.pallas_call(right_kernel, out_shape=jax.ShapeDtypeStruct((4, 4, 2, 64,...  65.9 us
    pallas_call x1, Pallas kernels, left_and_gram(): pl.pallas_call(left_kernel, out_shape=(jax.ShapeDtypeStruct((2, 4, 64, RA...  45.8 us
    all_to_all x2, blocking collectives, sent_to_all(): lax.all_to_all(jnp.broadcast_to(array[None], (devices, *array.shape)), ax...  38.8 us
    pallas_call x1, Pallas kernels, inverse_factor(): pl.pallas_call(factor_kernel, out_shape=jax.ShapeDtypeStruct((512, 512),...  20.3 us
    dot_general x1, matrix products, body(): lax.dot_general(out_rows, lax.all_gather(activations, WIDE, axis=0, tiled...  14.4 us
    pallas_call x1, Pallas kernels, raw_factors(): pl.pallas_call(raw_kernel, out_shape=(jax.ShapeDtypeStruct(w.shape, F32),...  11 us
  transfers between devices with their start and end apart: 1, of which 1 were waited for; matrix products, arithmetic and copies ran while one was open for 1% of the time, Pallas kernels for 0%

profile of v1, /device:TPU:1, one launch (start us, length us, event | category | flops | bytes accessed | tf_op | source)
XLA Modules:
  0.0 315.5 jit_solution(805907188310195732)
XLA Ops:
  7.2 0.0 all-gather.2.cloned.1.call-start
  7.2 0.7 all-gather.2.cloned.1.call-update
  7.9 1.2 broadcast_in_dim.4
  9.1 30.2 %all_to_all.10 = bf16[4,512,512]{2,1,0:T(8,128)(2,1)S(1)} all-to-all(bf16[4,512,512]{2,1,0:T(8,128)(2,1)S(1)} %broadcast_in_dim.4), channel_id=1, replica_groups=mesh['wide_0'=4,'wide_1'=4,'narrow_0'=4,'narrow_1'=2] {'narrow_0'}, dimensions={0} | all-to-all | bytes 4194304 | tf_op jit(solution)/shard_map/all_to_all | solution.py:296
  39.3 0.4 broadcast_in_dim.5
  39.7 8.6 %all_to_all.11 = bf16[2,4,512,512]{3,2,1,0:T(8,128)(2,1)S(1)} all-to-all(bf16[2,4,512,512]{3,2,1,0:T(8,128)(2,1)S(1)} %broadcast_in_dim.5), channel_id=1, replica_groups=mesh['wide_0'=4,'wide_1'=4,'narrow_0'=4,'narrow_1'=2] {'narrow_1'}, dimensions={0} | all-to-all | bytes 8388608 | tf_op jit(solution)/shard_map/all_to_all | solution.py:296
  48.3 2.5 copy.9
  50.8 74.0 %all-gather.2.cloned.1.call-done = bf16[4096,2048]{1,0:T(8,128)(2,1)} async-done(((bf16[256,2048]{1,0:T(8,128)(2,1)}), bf16[4096,2048]{1,0:T(8,128)(2,1)}) %all-gather.2.cloned.1.call-update) | async-done | bytes 16777232 | tf_op jit(solution)/shard_map/all_gather | solution.py:312
  124.8 0.0 copy-start.3
  124.8 14.4 %convolution_add_fusion = f32[512,2048]{1,0:T(8,128)S(1)} fusion(f32[512,2048]{1,0:T(8,128)} %param.6, bf16[4096,512]{1,0:T(8,128)(2,1)} %bitcast.29, bf16[4096,2048]{1,0:T(8,128)(2,1)} %all-gather.2.cloned.1.call-done), kind=kOutput, calls=%fused_computation.2 | convolution fusion | flops 8590983168 | bytes 29360128 | tf_op jit(solution)/shard_map/dot_general | solution.py:310
  139.2 0.0 copy-done.3
  139.2 0.0 copy-start
  139.2 3.7 %fusion.2 = f32[512,512]{1,0:T(8,128)S(1)} fusion(f32[512,2048]{1,0:T(8,128)S(1)} %convolution_add_fusion, f32[2048,512]{1,0:T(8,128)S(1)} %copy-done.3), kind=kOutput, calls=%fused_computation.6 | convolution fusion | flops 3221225472 | bytes 9437184 | tf_op jit(solution)/shard_map/dot_general | solution.py:317
  142.9 0.0 copy-done
  143.0 45.8 %shard_map.67 = (f32[2,4,64,512]{3,2,1,0:T(8,128)S(1)}, f32[4,2,4,16,512]{4,3,2,1,0:T(8,128)S(1)}) custom-call(f32[2,4,64,512]{3,2,1,0:T(8,128)S(1)} %bitcast.23), custom_call_target="tpu_custom_call" | custom-call | flops 67108864 | bytes 67108864 | tf_op jit(solution)/shard_map/pallas_call | solution.py:178
  188.8 5.3 %copy.10 = f32[2048,512]{1,0:T(8,128)} copy(f32[2048,512]{0,1:T(8,128)} %bitcast.27) | data formatting | bytes 8388608 | tf_op jit(solution)/shard_map/dot_general | solution.py:320
  194.1 5.7 %fusion.3.part = f32[4,4,2,64,512]{4,3,2,1,0:T(8,128)S(1)} fusion(f32[4,4,2,64,512]{4,3,2,1,0:T(8,128)} %bitcast.28, f32[512,512,1,1,1]{1,0,4,3,2:T(8,128)S(1)} %bitcast.24), kind=kOutput, calls=%fused_computation.7 | convolution fusion | flops 3221225472 | bytes 9437184 | tf_op jit(solution)/shard_map/dot_general | solution.py:320
  199.8 65.9 %shard_map.68 = f32[4,4,2,64,512]{4,3,2,1,0:T(8,128)S(1)} custom-call(f32[4,4,2,64,512]{4,3,2,1,0:T(8,128)S(1)} %fusion.3.part), custom_call_target="tpu_custom_call" | custom-call | flops 4194304 | bytes 134217728 | tf_op jit(solution)/shard_map/pallas_call | solution.py:234
  265.7 20.3 %shard_map.69.inv_ref = f32[512,512]{1,0:T(8,128)S(1)} custom-call(f32[512,512]{1,0:T(8,128)S(1)} %bitcast.26), custom_call_target="tpu_custom_call" | custom-call | tf_op jit(solution)/shard_map/pallas_call | solution.py:89
  286.0 11.0 %shard_map.70 = (f32[2048,512]{1,0:T(8,128)S(1)}, f32[512,512]{1,0:T(8,128)S(1)}, f32[8,512]{1,0:T(8,128)S(1)}) custom-call(f32[2048,512]{1,0:T(8,128)S(1)} %bitcast.22, f32[512,512]{1,0:T(8,128)S(1)} %bitcast.25, f32[512,512]{1,0:T(8,128)S(1)} %shard_map.69.inv_ref), custom_call_target="tpu_custom_call" | custom-call | flops 1073741824 | bytes 16777216 | tf_op jit(solution)/shard_map/pallas_call | solution.py:273
  297.0 0.0 copy-start.1
  297.0 0.6 broadcast_divide_fusion
  297.5 0.0 copy-start.2
  297.6 3.1 copy-done.1
  300.7 3.3 %multiply_subtract_fusion = f32[512,2048]{1,0:T(8,128)} fusion(f32[512,2048]{1,0:T(8,128)S(1)} %copy-done.1, f32[2048,512]{1,0:T(8,128)S(1)} %get-tuple-element.11, f32[512,512]{1,0:T(8,128)S(1)} %get-tuple-element.10), kind=kOutput, calls=%fused_computation.1 | convolution fusion | flops 1077149696 | bytes 13631488 | tf_op jit(solution)/shard_map/dot_general | solution.py:325
  304.0 0.0 copy-done.2
  304.0 4.7 %multiply_convert_fusion = bf16[512,2048]{1,0:T(8,128)(2,1)} fusion(f32[512,512]{1,0:T(8,128)S(1)} %get-tuple-element.10, f32[2048,512]{1,0:T(8,128)S(1)} %broadcast_divide_fusion), kind=kOutput, calls=%fused_computation | convolution fusion | flops 3223322624 | bytes 7340032 | tf_op jit(solution)/shard_map/dot_general | solution.py:334
  (1 shorter events, 0.0 us)
Async XLA Ops:
  7.2 117.7 %all-gather.2.cloned.1.call-start = ((), (), s32[]{:S(2)}) async-start(), calls=%async_computation.2 | async-start | bytes 17825792 | tf_op jit(solution)/shard_map/all_gather | solution.py:312
  124.8 14.4 %copy-start.3 = (f32[2048,512]{1,0:T(8,128)S(1)}, f32[2048,512]{1,0:T(8,128)}, u32[]{:S(2)}) copy-start(f32[2048,512]{1,0:T(8,128)} %param.7) | copy-start | bytes 12582916
  139.2 3.7 %copy-start = (f32[512,2048]{1,0:T(8,128)}, f32[512,2048]{1,0:T(8,128)S(1)}, u32[]{:S(2)}) copy-start(f32[512,2048]{1,0:T(8,128)S(1)} %convolution_add_fusion) | copy-start | bytes 12582916
  297.0 3.7 %copy-start.1 = (f32[512,2048]{1,0:T(8,128)S(1)}, f32[512,2048]{1,0:T(8,128)}, u32[]{:S(2)}) copy-start(f32[512,2048]{1,0:T(8,128)} %copy-done) | copy-start | bytes 12582916
  297.5 6.4 %copy-start.2 = (f32[2048,512]{1,0:T(8,128)}, f32[2048,512]{1,0:T(8,128)S(1)}, u32[]{:S(2)}) copy-start(f32[2048,512]{1,0:T(8,128)S(1)} %broadcast_divide_fusion) | copy-start | bytes 12582916
Sparse Core Ops, SparseCore 0:
  10.1 114.6 all-gather.1

commit v2 on v1

v2 whole, which is shorter than its diff:
```python
import math

import jax
import jax.numpy as jnp
from jax import lax
from jax.experimental import pallas as pl
from jax.experimental.pallas import tpu as pltpu
from jax.sharding import Mesh
from jax.sharding import PartitionSpec as P

DOUT = 8192
DIN = 16384
RANK = 512
X, Z, Y, C = "wide_0", "wide_1", "narrow_0", "narrow_1"
NARROW = (Y, C)
WIDE = (X, Z)
FEEDBACK = 0.05
EPSILON = 1e-06
F32 = jnp.float32
BF16 = jnp.bfloat16
VMEM = pl.BlockSpec(memory_space=pltpu.VMEM)
MESH = pl.DeviceIdType.MESH

def eliminated(rows):
    lane = lax.broadcasted_iota(jnp.int32, (8, 128), 1)
    sub = lax.broadcasted_iota(jnp.int32, (8, 128), 0)
    groups = len(rows)
    for p in range(groups):
        here = rows[p]
        cols = [jnp.broadcast_to(here[:, 8 * p + k : 8 * p + k + 1], (8, 128)) for k in range(8)]
        a = [[jnp.broadcast_to(cols[k][i : i + 1, :], (8, 128)) if k <= i else None for k in range(8)] for i in range(8)]
        low = [[None] * 8 for _ in range(8)]
        root = [None] * 8
        for k in range(8):
            root[k] = lax.rsqrt(a[k][k])
            for i in range(k + 1, 8):
                low[i][k] = a[i][k] * root[k]
            for i in range(k + 1, 8):
                for j in range(k + 1, i + 1):
                    a[i][j] = a[i][j] - low[i][k] * low[j][k]
        inside = (lane >= 8 * p) & (lane < 8 * p + 8)
        unit = jnp.where(lane == sub + 8 * p, 1.0, 0.0).astype(F32)
        source = jnp.where(inside, unit, here)
        y = []
        for k in range(8):
            value = jnp.broadcast_to(source[k : k + 1, :], (8, 128))
            for m in range(k):
                value = value - low[k][m] * y[m]
            y.append(value * root[k])
        done = y[0]
        for k in range(1, 8):
            done = jnp.where(sub == k, y[k], done)
        rows[p] = done
        for g in range(p + 1, groups):
            c = []
            total = jnp.where(inside, 0.0, rows[g])
            for k in range(8):
                value = jnp.broadcast_to(rows[g][:, 8 * p + k : 8 * p + k + 1], (8, 128))
                for m in range(k):
                    value = value - low[k][m] * c[m]
                c.append(value * root[k])
                total = total - c[k] * y[k]
            rows[g] = total
    return rows

def factor_kernel(c_ref, out_ref, s_ref):
    hi = lax.Precision.HIGHEST
    s_ref[...] = c_ref[...]
    row = lax.broadcasted_iota(jnp.int32, (128, 128), 0)
    col = lax.broadcasted_iota(jnp.int32, (128, 128), 1)
    for b in range(4):
        o = 128 * b
        rows = [s_ref[o + 8 * g : o + 8 * g + 8, o : o + 128] for g in range(16)]
        inv = jnp.concatenate(eliminated(rows), axis=0)
        inv = jnp.where(row >= col, inv, 0.0)
        s_ref[o : o + 128, o : o + 128] = jnp.where(row == col, 1.0, 0.0).astype(F32)
        y = jnp.dot(inv, s_ref[o : o + 128, :], precision=hi, preferred_element_type=F32)
        s_ref[o : o + 128, :] = y
        if b < 3:
            rest = y[:, o + 128 :]
            s_ref[o + 128 :, o : o + 128] = jnp.zeros((384 - o, 128), F32)
            s_ref[o + 128 :, :] = s_ref[o + 128 :, :] - lax.dot_general(
                rest, y, (((0,), (0,)), ((), ())), precision=hi, preferred_element_type=F32)
    row = lax.broadcasted_iota(jnp.int32, (512, 512), 0)
    col = lax.broadcasted_iota(jnp.int32, (512, 512), 1)
    out_ref[...] = jnp.where(row >= col, s_ref[...], 0.0)

def inverse_factor(c):
    return pl.pallas_call(factor_kernel, out_shape=jax.ShapeDtypeStruct((512,512),F32),
        in_specs=[pl.BlockSpec(memory_space=pltpu.VMEM)], out_specs=pl.BlockSpec(memory_space=pltpu.VMEM),
        scratch_shapes=[pltpu.VMEM((512,512),F32)],
        compiler_params=pltpu.CompilerParams(vmem_limit_bytes=32<<20))(c)


def halves(value):
    high = value.astype(BF16)
    return high, (value - high.astype(F32)).astype(BF16)


def one(left, right, dims=((1,), (0,))):
    return lax.dot_general(left, right, (dims, ((), ())), preferred_element_type=F32)


def dot3(left, right, dims=((1,), (0,))):
    a, b = halves(left)
    c, d = halves(right)
    return one(a, c, dims) + (one(a, d, dims) + one(b, c, dims))


def partner(axis, step):
    size = 2 if axis == C else 4
    return lax.rem(lax.axis_index(axis) + step, size)


def line_peers(axes):
    peers = []
    for axis in axes:
        for step in range(1, 2 if axis == C else 4):
            peers.append({axis: partner(axis, step)})
    return peers


def hail(peer):
    pl.semaphore_signal(
        pltpu.get_barrier_semaphore(), inc=1, device_id=peer, device_id_type=MESH
    )


def greet(peers):
    for peer in peers:
        hail(peer)
    pl.semaphore_wait(pltpu.get_barrier_semaphore(), len(peers))


def sent(send, recv, phase, axis, source, target):
    copies = []
    for step in range(1, 2 if axis == C else 4):
        to = partner(axis, step)
        copy = pltpu.make_async_remote_copy(
            src_ref=source(to),
            dst_ref=target(to),
            send_sem=send.at[phase, step - 1],
            recv_sem=recv.at[phase, step - 1],
            device_id={axis: to},
            device_id_type=MESH,
        )
        copy.start()
        copies.append(copy)
    return copies


def all_of(copies):
    for copy in copies:
        copy.wait()


def sum4(ref):
    return (ref[0] + ref[1]) + (ref[2] + ref[3])


def chain_kernel(
    a_ref, g_ref, m_ref, q_ref,
    wt, left, gram,
    q_hi, q_lo, z_part, z_pair, z_half, z_seen, z_own, z_all,
    part, pair, half, share,
    block, gx, gz,
    v_part, v_x, v_z, v_sx, v_sz, v_ex, v_ez, v_own, v_all,
    send, recv, z_send, z_recv, v_send, v_recv,
):
    x, z, y, c = (lax.axis_index(a) for a in (X, Z, Y, C))
    z_self = (x == y) & (lax.div(z, 2) == c)
    v_self = (x == y) & (z == 2 * c + lax.div(x, 2))
    barrier = pltpu.get_barrier_semaphore()

    def apart(first, alone, there, here):
        if not first:
            there()
            return
        pl.when(jnp.logical_not(alone))(there)
        pl.when(alone)(here)

    def z_sources(act):
        for dz in range(2):
            for dy in range(4):
                for dc in range(2):
                    act(dz == dy == dc == 0, lax.rem(z + dz, 2), partner(C, dc), partner(Y, dy))

    def v_sources(act):
        for dx in range(2):
            for dz in range(4):
                act(dx == dz == 0, lax.rem(x + dx, 2), partner(Z, dz))

    for peer in line_peers((X, Z, Y, C)):
        hail(peer)

    def nothing():
        pass

    z_sources(
        lambda first, zz, cc, yy: apart(
            first, z_self, lambda: hail({X: y, Z: 2 * c + zz, Y: yy, C: cc}), nothing
        )
    )
    v_sources(
        lambda first, xx, zz: apart(
            first,
            v_self,
            lambda: hail({X: 2 * lax.rem(z, 2) + xx, Z: zz, Y: x, C: lax.div(z, 2)}),
            nothing,
        )
    )

    @pl.loop(0, 4)
    def _(i):
        rows = pl.ds(pl.multiple_of(512 * i, 512), 512)
        q_hi[rows, :], q_lo[rows, :] = halves(q_ref[rows, :])

    z_part[...] = (one(a_ref[...], q_hi[...]) + one(a_ref[...], q_lo[...])).reshape(2, 4, 32, RANK)
    pl.semaphore_wait(barrier, 34 - z_self.astype(jnp.int32) - v_self.astype(jnp.int32))
    all_of(sent(send, recv, 0, C, lambda to: z_part.at[to], lambda to: z_pair))
    z_half[...] = z_part[c] + z_pair[...]
    copies = sent(send, recv, 1, Y, lambda to: z_half.at[to], lambda to: z_seen.at[y])
    z_seen[y] = z_half[y]
    all_of(copies)
    z_own[...] = sum4(z_seen)

    def z_copy(dx, dz):
        return pltpu.make_async_remote_copy(
            src_ref=z_own,
            dst_ref=z_all.at[lax.rem(z, 2), c, y],
            send_sem=z_send.at[dx, dz],
            recv_sem=z_recv.at[lax.rem(z, 2), c, y],
            device_id={X: partner(X, dx), Z: partner(Z, dz), Y: x, C: lax.div(z, 2)},
            device_id_type=MESH,
        )

    def z_keep():
        z_all[lax.rem(z, 2), c, y] = z_own[...]

    def z_arrived(first, zz, cc, yy):
        copy = pltpu.make_async_remote_copy(
            src_ref=z_own,
            dst_ref=z_all.at[zz, cc, yy],
            send_sem=z_send.at[0, 0],
            recv_sem=z_recv.at[zz, cc, yy],
            device_id={X: y, Z: 2 * c + zz, Y: yy, C: cc},
            device_id_type=MESH,
        )
        apart(first, z_self, copy.wait_recv, nothing)

    for dx in range(4):
        for dz in range(4):
            apart(dx == dz == 0, z_self, z_copy(dx, dz).start, z_keep)

    @pl.loop(0, 4)
    def _(i):
        rows = pl.ds(pl.multiple_of(128 * i, 128), 128)
        high, low = halves(m_ref[rows, :])
        total = one(high, q_hi[...]) + (one(low, q_hi[...]) + one(high, q_lo[...]))
        part[lax.div(i, 2), pl.ds(2 * lax.rem(i, 2), 2)] = total.reshape(2, 64, RANK)

    z_sources(z_arrived)
    for dx in range(4):
        for dz in range(4):
            apart(dx == dz == 0, z_self, z_copy(dx, dz).wait_send, nothing)
    high, low = halves(z_all[...].reshape(RANK, RANK))
    first = ((0,), (0,))
    gz_product = one(g_ref[...], high, first) + one(g_ref[...], low, first)
    part[...] = part[...] + gz_product.reshape(2, 4, 64, RANK)

    all_of(sent(send, recv, 2, C, lambda to: part.at[to], lambda to: pair))
    half[...] = part[c] + pair[...]
    copies = sent(send, recv, 3, Y, lambda to: half.at[to], lambda to: share.at[y])
    share[y] = half[y]
    all_of(copies)
    left[c, y] = sum4(share)
    all_of(sent(send, recv, 4, Y, lambda to: left.at[c, y], lambda to: left.at[c, y]))
    all_of(sent(send, recv, 5, C, lambda to: left.at[c], lambda to: left.at[c]))
    whole = left[...].reshape(RANK, RANK)
    p_hi, p_lo = halves(whole)

    for index in range(4):
        @pl.when(y == index)
        def _():
            own = whole[:, 128 * index : 128 * index + 128]
            block[...] = dot3(own, whole, first).reshape(2, 4, 16, RANK)
    g = sent(send, recv, 6, X, lambda to: block.at[c, to], lambda to: gx.at[x])
    gx[x] = block[c, x]
    v_part[...] = (one(g_ref[...], p_hi) + one(g_ref[...], p_lo)).reshape(4, 4, 2, 16, RANK)
    va = sent(send, recv, 11, X, lambda to: v_part.at[to, :, 0], lambda to: v_x.at[x])
    vb = sent(send, recv, 12, Z, lambda to: v_part.at[:, to, 1], lambda to: v_z.at[z])
    v_x[x] = v_part[x, :, 0]
    v_z[z] = v_part[:, z, 1]
    all_of(g)
    gz[z] = sum4(gx)
    g = sent(send, recv, 7, Z, lambda to: gz.at[z], lambda to: gz.at[z])
    turned = whole.T
    t_hi, t_lo = halves(turned)
    q_hi[0:RANK, :] = t_hi
    q_lo[0:RANK, :] = t_lo

    def momentum_part(begin, end):
        @pl.loop(begin, end)
        def _(j):
            columns = pl.ds(pl.multiple_of(256 * j, 256), 256)
            high, low = halves(m_ref[:, columns])
            left_hi, left_lo = q_hi[0:RANK, :], q_lo[0:RANK, :]
            total = one(left_hi, high) + (one(left_lo, high) + one(left_hi, low))
            for k in range(2):
                piece = total[:, 128 * k : 128 * k + 128].reshape(2, 256, 128)
                wt[lax.div(j, 2), 2 * lax.rem(j, 2) + k] = piece

    momentum_part(0, 2)
    all_of(va)
    v_sx[...] = sum4(v_x)
    va = sent(send, recv, 13, Z, lambda to: v_sx.at[to], lambda to: v_ez.at[z])
    all_of(vb)
    v_sz[...] = sum4(v_z)
    vb = sent(send, recv, 14, X, lambda to: v_sz.at[to], lambda to: v_ex.at[x])
    v_ez[z] = v_sx[z]
    v_ex[x] = v_sz[x]
    all_of(g)
    gram[y, c, x] = sum4(gz)
    g = sent(send, recv, 8, X, lambda to: gram.at[y, c, x], lambda to: gram.at[y, c, x])
    all_of(va)
    v_own[0] = sum4(v_ez)
    all_of(vb)
    v_own[1] = sum4(v_ex)

    def v_copy(dy, dc):
        return pltpu.make_async_remote_copy(
            src_ref=v_own,
            dst_ref=v_all.at[lax.rem(x, 2), z],
            send_sem=v_send.at[dy, dc],
            recv_sem=v_recv.at[lax.rem(x, 2), z],
            device_id={X: y, Z: 2 * c + lax.div(x, 2), Y: partner(Y, dy), C: partner(C, dc)},
            device_id_type=MESH,
        )

    def v_keep():
        v_all[lax.rem(x, 2), z] = v_own[...]

    def v_arrived(first, xx, zz):
        copy = pltpu.make_async_remote_copy(
            src_ref=v_own,
            dst_ref=v_all.at[xx, zz],
            send_sem=v_send.at[0, 0],
            recv_sem=v_recv.at[xx, zz],
            device_id={X: 2 * lax.rem(z, 2) + xx, Z: zz, Y: x, C: lax.div(z, 2)},
            device_id_type=MESH,
        )
        apart(first, v_self, copy.wait_recv, nothing)

    for dy in range(4):
        for dc in range(2):
            apart(dy == dc == 0, v_self, v_copy(dy, dc).start, v_keep)
    all_of(g)
    g = sent(send, recv, 9, Y, lambda to: gram.at[y, c], lambda to: gram.at[y, c])
    momentum_part(2, 8)
    all_of(g)
    g = sent(send, recv, 10, C, lambda to: gram.at[:, c], lambda to: gram.at[:, c])
    v_sources(v_arrived)
    for dy in range(4):
        for dc in range(2):
            apart(dy == dc == 0, v_self, v_copy(dy, dc).wait_send, nothing)
    t_hi, t_lo = halves(v_all[...].reshape(256, RANK).T)
    q_hi[RANK : 2 * RANK, 0:256] = t_hi
    q_lo[RANK : 2 * RANK, 0:256] = t_lo

    @pl.loop(0, 8)
    def _(j):
        columns = pl.ds(pl.multiple_of(256 * j, 256), 256)
        tokens = a_ref[:, columns]
        high, low = q_hi[RANK : 2 * RANK, 0:256], q_lo[RANK : 2 * RANK, 0:256]
        total = one(high, tokens) + one(low, tokens)
        for k in range(2):
            piece = total[:, 128 * k : 128 * k + 128].reshape(2, 256, 128)
            at = (lax.div(j, 2), 2 * lax.rem(j, 2) + k)
            wt[at] = wt[at] + piece

    all_of(g)


def chain(activations, grad_out, momentum, right_factor):
    shapes = [
        ((2048, RANK), BF16), ((2048, RANK), BF16),
        ((2, 4, 32, RANK), F32), ((4, 32, RANK), F32), ((4, 32, RANK), F32), ((4, 32, RANK), F32),
        ((32, RANK), F32), ((2, 2, 4, 32, RANK), F32),
        ((2, 4, 64, RANK), F32), ((4, 64, RANK), F32), ((4, 64, RANK), F32), ((4, 64, RANK), F32),
        ((2, 4, 16, RANK), F32), ((4, 16, RANK), F32), ((4, 16, RANK), F32),
        ((4, 4, 2, 16, RANK), F32), ((4, 4, 16, RANK), F32), ((4, 4, 16, RANK), F32),
        ((4, 16, RANK), F32), ((4, 16, RANK), F32), ((4, 16, RANK), F32), ((4, 16, RANK), F32),
        ((2, 16, RANK), F32), ((2, 4, 2, 16, RANK), F32),
    ]
    semaphores = [(15, 3), (15, 3), (4, 4), (2, 2, 4), (4, 2), (2, 4)]
    return pl.pallas_call(
        chain_kernel,
        out_shape=(
            jax.ShapeDtypeStruct((4, 4, 2, 256, 128), F32),
            jax.ShapeDtypeStruct((2, 4, 64, RANK), F32),
            jax.ShapeDtypeStruct((4, 2, 4, 16, RANK), F32),
        ),
        in_specs=[VMEM] * 4,
        out_specs=(VMEM,) * 3,
        scratch_shapes=[pltpu.VMEM(*s) for s in shapes]
        + [pltpu.SemaphoreType.DMA(s) for s in semaphores],
        compiler_params=pltpu.CompilerParams(
            collective_id=1, has_side_effects=True, vmem_limit_bytes=48 << 20
        ),
        cost_estimate=pl.CostEstimate(flops=1 << 34, bytes_accessed=128 << 20, transcendentals=0),
    )(activations, grad_out, momentum, right_factor)


def right_kernel(part, out, from_x, from_z, sum_x, sum_z, end_x, end_z, send, recv):
    x, z = lax.axis_index(X), lax.axis_index(Z)
    greet(line_peers((X, Z)))
    a = sent(send, recv, 0, X, lambda to: part.at[to, :, 0], lambda to: from_x.at[x])
    b = sent(send, recv, 1, Z, lambda to: part.at[:, to, 1], lambda to: from_z.at[z])
    from_x[x] = part[x, :, 0]
    from_z[z] = part[:, z, 1]
    all_of(a)
    sum_x[...] = sum4(from_x)
    a = sent(send, recv, 2, Z, lambda to: sum_x.at[to], lambda to: end_z.at[z])
    all_of(b)
    sum_z[...] = sum4(from_z)
    b = sent(send, recv, 3, X, lambda to: sum_z.at[to], lambda to: end_x.at[x])
    end_z[z] = sum_x[z]
    end_x[x] = sum_z[x]
    all_of(a)
    out[x, z, 0] = sum4(end_z)
    a = sent(send, recv, 4, Z, lambda to: out.at[x, z, 0], lambda to: out.at[x, z, 0])
    all_of(b)
    out[x, z, 1] = sum4(end_x)
    b = sent(send, recv, 5, X, lambda to: out.at[x, z, 1], lambda to: out.at[x, z, 1])
    all_of(a)
    a = sent(send, recv, 6, X, lambda to: out.at[x, :, 0], lambda to: out.at[x, :, 0])
    all_of(b)
    b = sent(send, recv, 7, Z, lambda to: out.at[:, z, 1], lambda to: out.at[:, z, 1])
    all_of(a)
    all_of(b)


def right_sum(part):
    return pl.pallas_call(
        right_kernel,
        out_shape=jax.ShapeDtypeStruct((4, 4, 2, 256, 128), F32),
        in_specs=[VMEM],
        out_specs=VMEM,
        scratch_shapes=[pltpu.VMEM((4, 4, 256, 128), F32)] * 2
        + [pltpu.VMEM((4, 256, 128), F32)] * 4
        + [pltpu.SemaphoreType.DMA((8, 3))] * 2,
        compiler_params=pltpu.CompilerParams(
            collective_id=2, has_side_effects=True, vmem_limit_bytes=40 << 20
        ),
        cost_estimate=pl.CostEstimate(flops=1 << 22, bytes_accessed=128 << 20, transcendentals=0),
    )(part)


def raw_kernel(w_ref, p_ref, inv_ref, right_t, left, scale, squares, seen, send, recv):
    y, c = lax.axis_index(Y), lax.axis_index(C)
    for peer in line_peers((Y, C)):
        hail(peer)
    squares[...] = jnp.zeros_like(squares)
    inv_hi, inv_lo = halves(inv_ref[...])

    @pl.loop(0, 8)
    def _(j):
        at = 2 * lax.rem(j, 2)
        pieces = [w_ref[lax.div(j, 2), at + k].reshape(RANK, 128) for k in range(2)]
        high, low = halves(jnp.concatenate(pieces, axis=1))
        total = one(inv_hi, high) + (one(inv_hi, low) + one(inv_lo, high))
        right_t[:, pl.ds(pl.multiple_of(256 * j, 256), 256)] = total
        square = total * total
        squares[...] += square[:, :128] + square[:, 128:]

    ones = jnp.ones((8, 128), F32)
    seen[4 + c] = lax.dot_general(
        ones, squares[...], (((1,), (1,)), ((), ())),
        precision=lax.Precision.HIGHEST, preferred_element_type=F32,
    )
    pl.semaphore_wait(pltpu.get_barrier_semaphore(), 4)
    all_of(sent(send, recv, 0, C, lambda to: seen.at[4 + c], lambda to: seen.at[4 + c]))
    seen[y] = seen[4] + seen[5]
    copies = sent(send, recv, 1, Y, lambda to: seen.at[y], lambda to: seen.at[y])
    left[...] = dot3(p_ref[...].reshape(RANK, RANK), inv_ref[...], ((1,), (1,)))
    all_of(copies)
    scale[...] = jnp.sqrt(sum4(seen)) + EPSILON


def raw_factors(w, p, inv):
    return pl.pallas_call(
        raw_kernel,
        out_shape=(
            jax.ShapeDtypeStruct((RANK, 2048), F32),
            jax.ShapeDtypeStruct((RANK, RANK), F32),
            jax.ShapeDtypeStruct((8, RANK), F32),
        ),
        in_specs=[VMEM] * 3,
        out_specs=(VMEM,) * 3,
        scratch_shapes=[
            pltpu.VMEM((RANK, 128), F32),
            pltpu.VMEM((6, 8, RANK), F32),
            pltpu.SemaphoreType.DMA((2, 3)),
            pltpu.SemaphoreType.DMA((2, 3)),
        ],
        compiler_params=pltpu.CompilerParams(
            collective_id=3, has_side_effects=True, vmem_limit_bytes=40 << 20
        ),
        cost_estimate=pl.CostEstimate(flops=1 << 30, bytes_accessed=16 << 20, transcendentals=0),
    )(w, p, inv)


def final_kernel(b_ref, r_ref, l_ref, n_ref, momentum, right, update):
    norms = n_ref[0:1, :]
    raw = r_ref[...]
    ortho = l_ref[...]
    r_hi, r_lo = halves(raw)
    momentum[...] = b_ref[...] - FEEDBACK * one(ortho.astype(BF16), r_hi)
    s_hi, s_lo = halves(ortho * (math.sqrt(DOUT * DIN / RANK) / norms))
    update[...] = (one(s_hi, r_hi) + (one(s_hi, r_lo) + one(s_lo, r_hi))).astype(BF16)
    right[...] = raw.T / norms


def final(buffer, right_t, left, norms):
    wide = 256
    return pl.pallas_call(
        final_kernel,
        grid=(2048 // wide,),
        in_specs=[
            pl.BlockSpec((RANK, wide), lambda j: (0, j)),
            pl.BlockSpec((RANK, wide), lambda j: (0, j)),
            pl.BlockSpec((RANK, RANK), lambda j: (0, 0)),
            pl.BlockSpec((8, RANK), lambda j: (0, 0)),
        ],
        out_specs=(
            pl.BlockSpec((RANK, wide), lambda j: (0, j)),
            pl.BlockSpec((wide, RANK), lambda j: (j, 0)),
            pl.BlockSpec((RANK, wide), lambda j: (0, j)),
        ),
        out_shape=(
            jax.ShapeDtypeStruct((RANK, 2048), F32),
            jax.ShapeDtypeStruct((2048, RANK), F32),
            jax.ShapeDtypeStruct((RANK, 2048), BF16),
        ),
        compiler_params=pltpu.CompilerParams(vmem_limit_bytes=40 << 20),
        cost_estimate=pl.CostEstimate(flops=1 << 32, bytes_accessed=20 << 20, transcendentals=0),
    )(buffer, right_t, left, norms)


def body(activations, grad_out, momentum, right_factor):
    all_activations = lax.all_gather(activations, WIDE, axis=0, tiled=True)
    all_grads = lax.all_gather(grad_out, NARROW, axis=0, tiled=True)
    part, left_factor, gram_matrix = chain(activations, grad_out, momentum, right_factor)
    inverse = inverse_factor(gram_matrix.reshape(RANK, RANK))
    unscaled = right_sum(part)
    gradient = lax.dot_general(
        all_grads, all_activations, (((0,), (0,)), ((), ())), preferred_element_type=F32
    )
    buffer = momentum + gradient
    right_t, ortho_left, norms = raw_factors(unscaled, left_factor, inverse)
    return final(buffer, right_t, ortho_left, norms)


def solution(mesh):
    finer = Mesh(mesh.devices.reshape(4, 4, 4, 2), (X, Z, Y, C))
    in_specs = (P(WIDE, NARROW), P(NARROW, WIDE), P(WIDE, NARROW), P(NARROW, None))
    out_specs = (P(WIDE, NARROW), P(NARROW, None), P(WIDE, NARROW))
    return jax.shard_map(body, mesh=finer, in_specs=in_specs, out_specs=out_specs, check_vma=False)
```

time: 316 us -> 299 us (0.946)
  Pallas kernels: 143 us -> 262 us
  waiting for transfers between devices: 74.7 us -> 1.38 us
  blocking collectives: 38.8 us -> 0 us
  matrix products: 31.7 us -> 14.4 us
  local copies, waits for them, and re-layouts: 12.5 us -> 6.63 us
    pallas_call x3 -> x4, Pallas kernels: 123 us -> 242 us  [the longest x1 122 us: chain(): pl.pallas_call(chain_kernel, out_shape=(jax.ShapeDtypeStruct((4, 4, 2, 25...]
    all_gather x1 -> x2, waiting for transfers between devices: 74 us -> 0.01 us  [the longest x1 0.01 us: body(): all_grads = lax.all_gather(grad_out, NARROW, axis=0, tiled=True)]
    all_to_all x2 -> x0, blocking collectives: 38.8 us -> none  [sent_to_all(): lax.all_to_all(jnp.broadcast_to(array[None], (devices, *array.shape)), ax...]
    dot_general x5 -> x1, matrix products: 31.7 us -> 14.4 us  [body(): lax.dot_general(all_grads, all_activations, (((0,), (0,)), ((), ())), pre...]
    dot_general x1 -> x0, local copies, waits for them, and re-layouts: 5.35 us -> none  [body(): lax.dot_general(buffer, left_factor, (((0,), (0,)), ((), ())), precision=...]
    unnamed x8 -> x10, local copies, waits for them, and re-layouts: 3.14 us -> 6.63 us
  transfers between devices with their start and end apart: 1 -> 2, of which waited for: 1 -> 0; matrix products, arithmetic and copies ran while one was open for 1% -> 0% of each run, Pallas kernels for 0% -> 85%
where the time goes in v2:
time: 299 us
  Pallas kernels  262 us (88%)
  matrix products  14.4 us (5%)
  between operations  14.1 us (5%)
  local copies, waits for them, and re-layouts  6.63 us (2%)
    pallas_call x1, Pallas kernels, chain(): pl.pallas_call(chain_kernel, out_shape=(jax.ShapeDtypeStruct((4, 4, 2, 25...  122 us
    pallas_call x1, Pallas kernels, right_sum(): pl.pallas_call(right_kernel, out_shape=jax.ShapeDtypeStruct((4, 4, 2, 256...  99.3 us
    pallas_call x1, Pallas kernels, inverse_factor(): pl.pallas_call(factor_kernel, out_shape=jax.ShapeDtypeStruct((512, 512),...  20.2 us
    dot_general x1, matrix products, body(): lax.dot_general(all_grads, all_activations, (((0,), (0,)), ((), ())), pre...  14.4 us
    pallas_call x1, Pallas kernels, raw_factors(): pl.pallas_call(raw_kernel, out_shape=(jax.ShapeDtypeStruct((RANK, 2048),...  12.7 us
    pallas_call x1, Pallas kernels, final(): pl.pallas_call(final_kernel, grid=(2048 // wide,), in_specs=[pl.BlockSpec...  7.93 us
    unnamed x10, local copies, waits for them, and re-layouts  6.63 us
  transfers between devices with their start and end apart: 2, of which 0 were waited for; matrix products, arithmetic and copies ran while one was open for 0% of the time, Pallas kernels for 85%

profile of v2, /device:TPU:1, one launch (start us, length us, event | category | flops | bytes accessed | tf_op | source)
XLA Modules:
  0.0 298.9 jit_solution(10191213829597389483)
XLA Ops:
  7.2 0.0 all-gather.3.cloned.1.call-start
  7.2 0.7 all-gather.3.cloned.1.call-update
  7.9 0.0 all-gather.5.cloned.1.call-start
  7.9 0.7 all-gather.5.cloned.1.call-update
  8.6 0.0 copy-start.1
  8.7 1.2 copy-done.1
  9.9 0.0 copy-start.2
  9.9 1.0 copy-done.2
  10.9 122.2 %shard_map.67 = (f32[4,4,2,256,128]{4,3,2,1,0:T(8,128)}, f32[2,4,64,512]{3,2,1,0:T(8,128)S(1)}, f32[4,2,4,16,512]{4,3,2,1,0:T(8,128)S(1)}) custom-call(bf16[256,2048]{1,0:T(8,128)(2,1)S(1)} %copy-done.1, bf16[512,512]{1,0:T(8,128)(2,1)S(1)} %copy-done.2, f32[512,2048]{1,0:T(8,128)} %m_ref.1, f32[2048,512]{1,0:T(8,128)} %q_ref.1), custom_call_target="tpu_custom_call" | custom-call | flops 17179869184 | bytes 134217728 | tf_op jit(solution)/shard_map/pallas_call | solution.py:396
  133.1 20.2 %shard_map.69.inv_ref = f32[512,512]{1,0:T(8,128)S(1)} custom-call(f32[512,512]{1,0:T(8,128)S(1)} %bitcast.3), custom_call_target="tpu_custom_call" | custom-call | tf_op jit(solution)/shard_map/pallas_call | solution.py:89
  153.3 0.0 copy-start
  153.3 2.4 copy-done
  155.7 99.3 %shard_map.68.w_ref = f32[4,4,2,256,128]{4,3,2,1,0:T(8,128)S(1)} custom-call(f32[4,4,2,256,128]{4,3,2,1,0:T(8,128)S(1)} %copy-done), custom_call_target="tpu_custom_call" | custom-call | flops 4194304 | bytes 134217728 | tf_op jit(solution)/shard_map/pallas_call | solution.py:444
  255.0 12.7 %shard_map.70 = (f32[512,2048]{1,0:T(8,128)S(1)}, f32[512,512]{1,0:T(8,128)S(1)}, f32[8,512]{1,0:T(8,128)S(1)}) custom-call(f32[4,4,2,256,128]{4,3,2,1,0:T(8,128)S(1)} %shard_map.68.w_ref, f32[2,4,64,512]{3,2,1,0:T(8,128)S(1)} %get-tuple-element.10.p_ref, f32[512,512]{1,0:T(8,128)S(1)} %shard_map.69.inv_ref), custom_call_target="tpu_custom_call" | custom-call | flops 1073741824 | bytes 16777216 | tf_op jit(solution)/shard_map/pallas_call | solution.py:491
  267.7 0.0 copy-start.3
  267.7 2.0 copy-done.3
  269.7 0.0 all-gather.3.cloned.1.call-done
  269.7 0.0 all-gather.5.cloned.1.call-done
  269.7 0.0 copy-start.4
  269.7 14.4 %convolution_add_fusion.b_ref = f32[512,2048]{1,0:T(8,128)S(1)} fusion(f32[512,2048]{1,0:T(8,128)} %m_ref.1, bf16[4096,512]{1,0:T(8,128)(2,1)} %all-gather.3.cloned.1.call-done, bf16[4096,2048]{1,0:T(8,128)(2,1)} %all-gather.5.cloned.1.call-done), kind=kOutput, calls=%fused_computation | convolution fusion | flops 8590983168 | bytes 29360128 | tf_op jit(solution)/shard_map/dot_general | solution.py:556
  284.1 0.0 copy-done.4
  284.1 7.9 %shard_map.71 = (f32[512,2048]{1,0:T(8,128)}, f32[2048,512]{1,0:T(8,128)}, bf16[512,2048]{1,0:T(8,128)(2,1)}) custom-call(f32[512,2048]{1,0:T(8,128)S(1)} %convolution_add_fusion.b_ref, f32[512,2048]{1,0:T(8,128)S(1)} %copy-done.4, f32[512,512]{1,0:T(8,128)S(1)} %get-tuple-element.13.l_ref, f32[8,512]{1,0:T(8,128)S(1)} %get-tuple-element.14.n_ref), custom_call_target="tpu_custom_call" | custom-call | flops 4294967296 | bytes 20971520 | tf_op jit(solution)/shard_map/pallas_call | solution.py:526
Async XLA Ops:
  7.2 262.5 %all-gather.3.cloned.1.call-start = ((), (), s32[]{:S(2)}) async-start(), calls=%async_computation | async-start | bytes 4718592 | tf_op jit(solution)/shard_map/all_gather | solution.py:552
  7.9 261.8 %all-gather.5.cloned.1.call-start = ((), (), s32[]{:S(2)}) async-start(), calls=%async_computation.1 | async-start | bytes 17825792 | tf_op jit(solution)/shard_map/all_gather | solution.py:551
  8.6 1.2 copy-start.1
  9.9 1.0 copy-start.2
  153.3 2.4 copy-start
  267.7 2.0 copy-start.3
  269.7 14.4 %copy-start.4 = (f32[512,2048]{1,0:T(8,128)S(1)}, f32[512,2048]{1,0:T(8,128)}, u32[]{:S(2)}) copy-start(f32[512,2048]{1,0:T(8,128)} %copy-done.3) | copy-start | bytes 12582916
Sparse Core Ops, SparseCore 0:
  9.7 51.9 all-gather.2
  63.9 162.6 all-gather.4

commit v3 on v2

--- a/solution.py
+++ b/solution.py
@@ -411,13 +411,30 @@
     )(activations, grad_out, momentum, right_factor)
 
 
-def right_kernel(part, out, from_x, from_z, sum_x, sum_z, end_x, end_z, send, recv):
-    x, z = lax.axis_index(X), lax.axis_index(Z)
-    greet(line_peers((X, Z)))
+def right_kernel(
+    part, g_ref, a_all, m_ref, inv_ref, p_ref,
+    right_t, left, scale, buffer,
+    from_x, from_z, sum_x, sum_z, end_x, end_z, out,
+    g_all, g_turned, tokens, squares, seen, send, recv, tile_sem,
+):
+    x, z, y, c = (lax.axis_index(a) for a in (X, Z, Y, C))
+
+    def tile(j):
+        slot = lax.rem(j, 2)
+        columns = pl.ds(pl.multiple_of(256 * j, 256), 256)
+        return pltpu.make_async_copy(a_all.at[:, columns], tokens.at[slot], tile_sem.at[slot])
+
+    tile(0).start()
+    tile(1).start()
+    greet(line_peers((X, Z, Y, C)))
     a = sent(send, recv, 0, X, lambda to: part.at[to, :, 0], lambda to: from_x.at[x])
     b = sent(send, recv, 1, Z, lambda to: part.at[:, to, 1], lambda to: from_z.at[z])
+    g = sent(send, recv, 8, Y, lambda to: g_ref, lambda to: g_all.at[y, c])
     from_x[x] = part[x, :, 0]
     from_z[z] = part[:, z, 1]
+    g_all[y, c] = g_ref[...]
+    left[...] = dot3(p_ref[...].reshape(RANK, RANK), inv_ref[...], ((1,), (1,)))
+    squares[...] = jnp.zeros_like(squares)
     all_of(a)
     sum_x[...] = sum4(from_x)
     a = sent(send, recv, 2, Z, lambda to: sum_x.at[to], lambda to: end_z.at[z])
@@ -426,6 +443,8 @@
     b = sent(send, recv, 3, X, lambda to: sum_z.at[to], lambda to: end_x.at[x])
     end_z[z] = sum_x[z]
     end_x[x] = sum_z[x]
+    all_of(g)
+    g = sent(send, recv, 9, C, lambda to: g_all.at[:, c], lambda to: g_all.at[:, c])
     all_of(a)
     out[x, z, 0] = sum4(end_z)
     a = sent(send, recv, 4, Z, lambda to: out.at[x, z, 0], lambda to: out.at[x, z, 0])
@@ -436,37 +455,28 @@
     a = sent(send, recv, 6, X, lambda to: out.at[x, :, 0], lambda to: out.at[x, :, 0])
     all_of(b)
     b = sent(send, recv, 7, Z, lambda to: out.at[:, z, 1], lambda to: out.at[:, z, 1])
+    all_of(g)
+    for n in range(8):
+        g_turned[:, 512 * n : 512 * n + 512] = g_all[n // 2, n % 2].T
+
+    @pl.loop(0, 8)
+    def _(j):
+        tile(j).wait()
+        columns = pl.ds(pl.multiple_of(256 * j, 256), 256)
+        buffer[:, columns] = m_ref[:, columns] + one(g_turned[...], tokens[lax.rem(j, 2)])
+
+        @pl.when(j < 6)
+        def _():
+            tile(j + 2).start()
+
     all_of(a)
     all_of(b)
-
-
-def right_sum(part):
-    return pl.pallas_call(
-        right_kernel,
-        out_shape=jax.ShapeDtypeStruct((4, 4, 2, 256, 128), F32),
-        in_specs=[VMEM],
-        out_specs=VMEM,
-        scratch_shapes=[pltpu.VMEM((4, 4, 256, 128), F32)] * 2
-        + [pltpu.VMEM((4, 256, 128), F32)] * 4
-        + [pltpu.SemaphoreType.DMA((8, 3))] * 2,
-        compiler_params=pltpu.CompilerParams(
-            collective_id=2, has_side_effects=True, vmem_limit_bytes=40 << 20
-        ),
-        cost_estimate=pl.CostEstimate(flops=1 << 22, bytes_accessed=128 << 20, transcendentals=0),
-    )(part)
-
-
-def raw_kernel(w_ref, p_ref, inv_ref, right_t, left, scale, squares, seen, send, recv):
-    y, c = lax.axis_index(Y), lax.axis_index(C)
-    for peer in line_peers((Y, C)):
-        hail(peer)
-    squares[...] = jnp.zeros_like(squares)
     inv_hi, inv_lo = halves(inv_ref[...])
 
     @pl.loop(0, 8)
     def _(j):
         at = 2 * lax.rem(j, 2)
-        pieces = [w_ref[lax.div(j, 2), at + k].reshape(RANK, 128) for k in range(2)]
+        pieces = [out[lax.div(j, 2), at + k].reshape(RANK, 128) for k in range(2)]
         high, low = halves(jnp.concatenate(pieces, axis=1))
         total = one(inv_hi, high) + (one(inv_hi, low) + one(inv_lo, high))
         right_t[:, pl.ds(pl.multiple_of(256 * j, 256), 256)] = total
@@ -478,36 +488,41 @@
         ones, squares[...], (((1,), (1,)), ((), ())),
         precision=lax.Precision.HIGHEST, preferred_element_type=F32,
     )
-    pl.semaphore_wait(pltpu.get_barrier_semaphore(), 4)
-    all_of(sent(send, recv, 0, C, lambda to: seen.at[4 + c], lambda to: seen.at[4 + c]))
+    all_of(sent(send, recv, 10, C, lambda to: seen.at[4 + c], lambda to: seen.at[4 + c]))
     seen[y] = seen[4] + seen[5]
-    copies = sent(send, recv, 1, Y, lambda to: seen.at[y], lambda to: seen.at[y])
-    left[...] = dot3(p_ref[...].reshape(RANK, RANK), inv_ref[...], ((1,), (1,)))
-    all_of(copies)
+    all_of(sent(send, recv, 11, Y, lambda to: seen.at[y], lambda to: seen.at[y]))
     scale[...] = jnp.sqrt(sum4(seen)) + EPSILON
 
 
-def raw_factors(w, p, inv):
+def right_factors(part, grad_out, all_activations, momentum, inverse, left):
     return pl.pallas_call(
-        raw_kernel,
+        right_kernel,
         out_shape=(
             jax.ShapeDtypeStruct((RANK, 2048), F32),
             jax.ShapeDtypeStruct((RANK, RANK), F32),
             jax.ShapeDtypeStruct((8, RANK), F32),
+            jax.ShapeDtypeStruct((RANK, 2048), F32),
         ),
-        in_specs=[VMEM] * 3,
-        out_specs=(VMEM,) * 3,
-        scratch_shapes=[
+        in_specs=[VMEM, VMEM, pl.BlockSpec(memory_space=pl.ANY), VMEM, VMEM, VMEM],
+        out_specs=(VMEM,) * 4,
+        scratch_shapes=[pltpu.VMEM((4, 4, 256, 128), F32)] * 2
+        + [pltpu.VMEM((4, 256, 128), F32)] * 4
+        + [
+            pltpu.VMEM((4, 4, 2, 256, 128), F32),
+            pltpu.VMEM((4, 2, 512, 512), BF16),
+            pltpu.VMEM((512, 4096), BF16),
+            pltpu.VMEM((2, 4096, 256), BF16),
             pltpu.VMEM((RANK, 128), F32),
             pltpu.VMEM((6, 8, RANK), F32),
-            pltpu.SemaphoreType.DMA((2, 3)),
-            pltpu.SemaphoreType.DMA((2, 3)),
+            pltpu.SemaphoreType.DMA((12, 3)),
+            pltpu.SemaphoreType.DMA((12, 3)),
+            pltpu.SemaphoreType.DMA((2,)),
         ],
         compiler_params=pltpu.CompilerParams(
-            collective_id=3, has_side_effects=True, vmem_limit_bytes=40 << 20
+            collective_id=2, has_side_effects=True, vmem_limit_bytes=56 << 20
         ),
-        cost_estimate=pl.CostEstimate(flops=1 << 30, bytes_accessed=16 << 20, transcendentals=0),
-    )(w, p, inv)
+        cost_estimate=pl.CostEstimate(flops=1 << 34, bytes_accessed=128 << 20, transcendentals=0),
+    )(part, grad_out, all_activations, momentum, inverse, left)
 
 
 def final_kernel(b_ref, r_ref, l_ref, n_ref, momentum, right, update):
@@ -542,22 +557,18 @@
             jax.ShapeDtypeStruct((2048, RANK), F32),
             jax.ShapeDtypeStruct((RANK, 2048), BF16),
         ),
-        compiler_params=pltpu.CompilerParams(vmem_limit_bytes=40 << 20),
+        compiler_params=pltpu.CompilerParams(vmem_limit_bytes=60 << 20),
         cost_estimate=pl.CostEstimate(flops=1 << 32, bytes_accessed=20 << 20, transcendentals=0),
     )(buffer, right_t, left, norms)
 
 
 def body(activations, grad_out, momentum, right_factor):
     all_activations = lax.all_gather(activations, WIDE, axis=0, tiled=True)
-    all_grads = lax.all_gather(grad_out, NARROW, axis=0, tiled=True)
     part, left_factor, gram_matrix = chain(activations, grad_out, momentum, right_factor)
     inverse = inverse_factor(gram_matrix.reshape(RANK, RANK))
-    unscaled = right_sum(part)
-    gradient = lax.dot_general(
-        all_grads, all_activations, (((0,), (0,)), ((), ())), preferred_element_type=F32
+    right_t, ortho_left, norms, buffer = right_factors(
+        part, grad_out, all_activations, momentum, inverse, left_factor
     )
-    buffer = momentum + gradient
-    right_t, ortho_left, norms = raw_factors(unscaled, left_factor, inverse)
     return final(buffer, right_t, ortho_left, norms)
 
 

time: 299 us -> 278 us (0.930)
  Pallas kernels: 262 us -> 243 us
  matrix products: 14.4 us -> 0 us
  waiting for transfers between devices: 1.38 us -> 14.7 us
    pallas_call x2 -> x1, Pallas kernels: 112 us -> 85 us  [right_factors(): pl.pallas_call(right_kernel, out_shape=(jax.ShapeDtypeStruct((RANK, 2048)...]
    dot_general x1 -> x0, matrix products: 14.4 us -> none  [body(): lax.dot_general(all_grads, all_activations, (((0,), (0,)), ((), ())), pre...]
    all_gather x1, waiting for transfers between devices: 0.01 us -> 14 us  [body(): all_activations = lax.all_gather(activations, WIDE, axis=0, tiled=True)]
    pallas_call x1, Pallas kernels: 122 us -> 126 us  [chain(): pl.pallas_call(chain_kernel, out_shape=(jax.ShapeDtypeStruct((4, 4, 2, 25...]
    pallas_call x1, Pallas kernels: 7.93 us -> 11.3 us  [final(): pl.pallas_call(final_kernel, grid=(2048 // wide,), in_specs=[pl.BlockSpec...]
    unnamed x10 -> x8, local copies, waits for them, and re-layouts: 6.63 us -> 4.19 us
  transfers between devices with their start and end apart: 2 -> 1, of which waited for: 0 -> 1; matrix products, arithmetic and copies ran while one was open for 0% -> 0% of each run, Pallas kernels for 85% -> 53%
where the time goes in v3:
time: 278 us; the launch traced here: 276 us
  Pallas kernels  243 us (87%)
  waiting for transfers between devices  14.7 us (5%)
  between operations  14.1 us (5%)
  local copies, waits for them, and re-layouts  4.19 us (2%)
    pallas_call x1, Pallas kernels, chain(): pl.pallas_call(chain_kernel, out_shape=(jax.ShapeDtypeStruct((4, 4, 2, 25...  126 us
    pallas_call x1, Pallas kernels, right_factors(): pl.pallas_call(right_kernel, out_shape=(jax.ShapeDtypeStruct((RANK, 2048)...  85 us
    pallas_call x1, Pallas kernels, inverse_factor(): pl.pallas_call(factor_kernel, out_shape=jax.ShapeDtypeStruct((512, 512),...  20.2 us
    all_gather x1, waiting for transfers between devices, body(): all_activations = lax.all_gather(activations, WIDE, axis=0, tiled=True)  14 us
    pallas_call x1, Pallas kernels, final(): pl.pallas_call(final_kernel, grid=(2048 // wide,), in_specs=[pl.BlockSpec...  11.3 us
  transfers between devices with their start and end apart: 1, of which 1 were waited for; matrix products, arithmetic and copies ran while one was open for 0% of the time, Pallas kernels for 53%

profile of v3, /device:TPU:1, one launch (start us, length us, event | category | flops | bytes accessed | tf_op | source)
XLA Modules:
  0.0 275.8 jit_solution(17689203553582198374)
XLA Ops:
  7.2 0.0 all-gather.2.cloned.1.call-start
  7.2 0.7 all-gather.2.cloned.1.call-update
  7.9 0.0 copy-start
  7.9 1.2 copy-done
  9.1 0.0 copy-start.2
  9.1 1.0 copy-done.2
  10.2 126.2 %shard_map.67 = (f32[4,4,2,256,128]{4,3,2,1,0:T(8,128)}, f32[2,4,64,512]{3,2,1,0:T(8,128)S(1)}, f32[4,2,4,16,512]{4,3,2,1,0:T(8,128)S(1)}) custom-call(bf16[256,2048]{1,0:T(8,128)(2,1)S(1)} %copy-done, bf16[512,512]{1,0:T(8,128)(2,1)S(1)} %copy-done.2, f32[512,2048]{1,0:T(8,128)} %m_ref.3, f32[2048,512]{1,0:T(8,128)} %q_ref.1), custom_call_target="tpu_custom_call" | custom-call | flops 17179869184 | bytes 134217728 | tf_op jit(solution)/shard_map/pallas_call | solution.py:396
  136.4 0.0 copy-start.3
  136.4 1.0 copy-done.3
  137.4 20.2 %shard_map.68.inv_ref = f32[512,512]{1,0:T(8,128)S(1)} custom-call(f32[512,512]{1,0:T(8,128)S(1)} %bitcast.1), custom_call_target="tpu_custom_call" | custom-call | tf_op jit(solution)/shard_map/pallas_call | solution.py:89
  157.6 0.0 copy-start.1
  157.6 1.0 copy-done.1
  158.6 14.0 %all-gather.2.cloned.1.call-done.a_all = bf16[4096,2048]{1,0:T(8,128)(2,1)} async-done(((bf16[256,2048]{1,0:T(8,128)(2,1)}), bf16[4096,2048]{1,0:T(8,128)(2,1)}) %all-gather.2.cloned.1.call-update) | async-done | bytes 16777232 | tf_op jit(solution)/shard_map/all_gather | solution.py:566
  172.6 85.0 %shard_map.69 = (f32[512,2048]{1,0:T(8,128)}, f32[512,512]{1,0:T(8,128)}, f32[8,512]{1,0:T(8,128)}, f32[512,2048]{1,0:T(8,128)}) custom-call(f32[4,4,2,256,128]{4,3,2,1,0:T(8,128)} %get-tuple-element.10.part, bf16[512,512]{1,0:T(8,128)(2,1)} %g_ref.3, bf16[4096,2048]{1,0:T(8,128)(2,1)} %all-gather.2.cloned.1.call-done.a_all, f32[512,2048]{1,0:T(8,128)} %m_ref.3, ...), custom_call_target="tpu_custom_call" | custom-call | flops 17179869184 | bytes 134217728 | tf_op jit(solution)/shard_map/pallas_call | solution.py:498
  257.7 11.3 %shard_map.70 = (f32[512,2048]{1,0:T(8,128)}, f32[2048,512]{1,0:T(8,128)}, bf16[512,2048]{1,0:T(8,128)(2,1)}) custom-call(f32[512,2048]{1,0:T(8,128)} %get-tuple-element.13.b_ref, f32[512,2048]{1,0:T(8,128)} %get-tuple-element.14.r_ref, f32[512,512]{1,0:T(8,128)} %get-tuple-element.15.l_ref, f32[8,512]{1,0:T(8,128)} %get-tuple-element.16.n_ref), custom_call_target="tpu_custom_call" | custom-call | flops 4294967296 | bytes 20971520 | tf_op jit(solution)/shard_map/pallas_call | solution.py:541
Async XLA Ops:
  7.2 165.5 %all-gather.2.cloned.1.call-start = ((), (), s32[]{:S(2)}) async-start(), calls=%async_computation | async-start | bytes 17825792 | tf_op jit(solution)/shard_map/all_gather | solution.py:566
  7.9 1.2 copy-start
  9.1 1.0 copy-start.2
  136.4 1.0 copy-start.3
  157.6 1.0 copy-start.1
Sparse Core Ops, SparseCore 0:
  10.1 162.4 all-gather.1

commit v4 on v3

--- a/solution.py
+++ b/solution.py
@@ -161,54 +161,33 @@
 def chain_kernel(
     a_ref, g_ref, m_ref, q_ref,
     wt, left, gram,
-    q_hi, q_lo, z_part, z_pair, z_half, z_seen, z_own, z_all,
+    q_hi, q_lo, g_mine, z_part, z_pair, z_half, z_seen, z_all,
     part, pair, half, share,
     block, gx, gz,
-    v_part, v_x, v_z, v_sx, v_sz, v_ex, v_ez, v_own, v_all,
-    send, recv, z_send, z_recv, v_send, v_recv,
+    v_part, v_x, v_z, v_sx, v_sz, v_ex, v_ez, v_all,
+    send, recv, g_send, g_recv,
 ):
     x, z, y, c = (lax.axis_index(a) for a in (X, Z, Y, C))
-    z_self = (x == y) & (lax.div(z, 2) == c)
-    v_self = (x == y) & (z == 2 * c + lax.div(x, 2))
-    barrier = pltpu.get_barrier_semaphore()
-
-    def apart(first, alone, there, here):
-        if not first:
-            there()
-            return
-        pl.when(jnp.logical_not(alone))(there)
-        pl.when(alone)(here)
-
-    def z_sources(act):
-        for dz in range(2):
-            for dy in range(4):
-                for dc in range(2):
-                    act(dz == dy == dc == 0, lax.rem(z + dz, 2), partner(C, dc), partner(Y, dy))
-
-    def v_sources(act):
-        for dx in range(2):
-            for dz in range(4):
-                act(dx == dz == 0, lax.rem(x + dx, 2), partner(Z, dz))
-
-    for peer in line_peers((X, Z, Y, C)):
-        hail(peer)
-
-    def nothing():
-        pass
-
-    z_sources(
-        lambda first, zz, cc, yy: apart(
-            first, z_self, lambda: hail({X: y, Z: 2 * c + zz, Y: yy, C: cc}), nothing
+    first = ((0,), (0,))
+    others = [(dy, dc) for dy in range(4) for dc in range(2) if dy or dc]
+    greet(line_peers((X, Z)) + [{Y: partner(Y, dy), C: partner(C, dc)} for dy, dc in others])
+
+    deals = []
+    mine = pl.ds(2 * (2 * y + c), 2)
+    for dy, dc in others:
+        to_y, to_c = partner(Y, dy), partner(C, dc)
+        deals.append(
+            pltpu.make_async_remote_copy(
+                src_ref=g_ref.at[:, to_c, to_y],
+                dst_ref=g_mine.at[mine],
+                send_sem=g_send.at[dy, dc],
+                recv_sem=g_recv.at[dy, dc],
+                device_id={Y: to_y, C: to_c},
+                device_id_type=MESH,
+            )
         )
-    )
-    v_sources(
-        lambda first, xx, zz: apart(
-            first,
-            v_self,
-            lambda: hail({X: 2 * lax.rem(z, 2) + xx, Z: zz, Y: x, C: lax.div(z, 2)}),
-            nothing,
-        )
-    )
+        deals[-1].start()
+    g_mine[mine] = g_ref[:, c, y]
 
     @pl.loop(0, 4)
     def _(i):
@@ -216,56 +195,36 @@
         q_hi[rows, :], q_lo[rows, :] = halves(q_ref[rows, :])
 
     z_part[...] = (one(a_ref[...], q_hi[...]) + one(a_ref[...], q_lo[...])).reshape(2, 4, 32, RANK)
-    pl.semaphore_wait(barrier, 34 - z_self.astype(jnp.int32) - v_self.astype(jnp.int32))
     all_of(sent(send, recv, 0, C, lambda to: z_part.at[to], lambda to: z_pair))
     z_half[...] = z_part[c] + z_pair[...]
     copies = sent(send, recv, 1, Y, lambda to: z_half.at[to], lambda to: z_seen.at[y])
     z_seen[y] = z_half[y]
     all_of(copies)
-    z_own[...] = sum4(z_seen)
-
-    def z_copy(dx, dz):
-        return pltpu.make_async_remote_copy(
-            src_ref=z_own,
-            dst_ref=z_all.at[lax.rem(z, 2), c, y],
-            send_sem=z_send.at[dx, dz],
-            recv_sem=z_recv.at[lax.rem(z, 2), c, y],
-            device_id={X: partner(X, dx), Z: partner(Z, dz), Y: x, C: lax.div(z, 2)},
-            device_id_type=MESH,
-        )
-
-    def z_keep():
-        z_all[lax.rem(z, 2), c, y] = z_own[...]
-
-    def z_arrived(first, zz, cc, yy):
-        copy = pltpu.make_async_remote_copy(
-            src_ref=z_own,
-            dst_ref=z_all.at[zz, cc, yy],
-            send_sem=z_send.at[0, 0],
-            recv_sem=z_recv.at[zz, cc, yy],
-            device_id={X: y, Z: 2 * c + zz, Y: yy, C: cc},
-            device_id_type=MESH,
-        )
-        apart(first, z_self, copy.wait_recv, nothing)
-
-    for dx in range(4):
-        for dz in range(4):
-            apart(dx == dz == 0, z_self, z_copy(dx, dz).start, z_keep)
-
-    @pl.loop(0, 4)
-    def _(i):
-        rows = pl.ds(pl.multiple_of(128 * i, 128), 128)
-        high, low = halves(m_ref[rows, :])
-        total = one(high, q_hi[...]) + (one(low, q_hi[...]) + one(high, q_lo[...]))
-        part[lax.div(i, 2), pl.ds(2 * lax.rem(i, 2), 2)] = total.reshape(2, 64, RANK)
-
-    z_sources(z_arrived)
-    for dx in range(4):
-        for dz in range(4):
-            apart(dx == dz == 0, z_self, z_copy(dx, dz).wait_send, nothing)
+    z_all[x, z] = sum4(z_seen).reshape(2, 16, RANK)
+    za = sent(send, recv, 15, Z, lambda to: z_all.at[x, z, 0], lambda to: z_all.at[x, z, 0])
+    zb = sent(send, recv, 16, X, lambda to: z_all.at[x, z, 1], lambda to: z_all.at[x, z, 1])
+
+    def momentum_left(begin, end):
+        @pl.loop(begin, end)
+        def _(i):
+            rows = pl.ds(pl.multiple_of(128 * i, 128), 128)
+            high, low = halves(m_ref[rows, :])
+            total = one(high, q_hi[...]) + (one(low, q_hi[...]) + one(high, q_lo[...]))
+            part[lax.div(i, 2), pl.ds(2 * lax.rem(i, 2), 2)] = total.reshape(2, 64, RANK)
+
+    momentum_left(0, 1)
+    all_of(za)
+    za = sent(send, recv, 17, X, lambda to: z_all.at[x, :, 0], lambda to: z_all.at[x, :, 0])
+    all_of(zb)
+    zb = sent(send, recv, 18, Z, lambda to: z_all.at[:, z, 1], lambda to: z_all.at[:, z, 1])
+    momentum_left(1, 4)
+    for deal in deals:
+        deal.wait()
+    all_of(za)
+    all_of(zb)
     high, low = halves(z_all[...].reshape(RANK, RANK))
-    first = ((0,), (0,))
-    gz_product = one(g_ref[...], high, first) + one(g_ref[...], low, first)
+    grads = g_mine[...].reshape(512, 512)
+    gz_product = one(grads, high, first) + one(grads, low, first)
     part[...] = part[...] + gz_product.reshape(2, 4, 64, RANK)
 
     all_of(sent(send, recv, 2, C, lambda to: part.at[to], lambda to: pair))
@@ -279,6 +238,9 @@
     whole = left[...].reshape(RANK, RANK)
     p_hi, p_lo = halves(whole)
 
+    v_part[...] = (one(grads, p_hi) + one(grads, p_lo)).reshape(4, 4, 2, 16, RANK)
+    va = sent(send, recv, 11, X, lambda to: v_part.at[to, :, 0], lambda to: v_x.at[x])
+    vb = sent(send, recv, 12, Z, lambda to: v_part.at[:, to, 1], lambda to: v_z.at[z])
     for index in range(4):
         @pl.when(y == index)
         def _():
@@ -286,20 +248,13 @@
             block[...] = dot3(own, whole, first).reshape(2, 4, 16, RANK)
     g = sent(send, recv, 6, X, lambda to: block.at[c, to], lambda to: gx.at[x])
     gx[x] = block[c, x]
-    v_part[...] = (one(g_ref[...], p_hi) + one(g_ref[...], p_lo)).reshape(4, 4, 2, 16, RANK)
-    va = sent(send, recv, 11, X, lambda to: v_part.at[to, :, 0], lambda to: v_x.at[x])
-    vb = sent(send, recv, 12, Z, lambda to: v_part.at[:, to, 1], lambda to: v_z.at[z])
     v_x[x] = v_part[x, :, 0]
     v_z[z] = v_part[:, z, 1]
-    all_of(g)
-    gz[z] = sum4(gx)
-    g = sent(send, recv, 7, Z, lambda to: gz.at[z], lambda to: gz.at[z])
-    turned = whole.T
-    t_hi, t_lo = halves(turned)
+    t_hi, t_lo = halves(whole.T)
     q_hi[0:RANK, :] = t_hi
     q_lo[0:RANK, :] = t_lo
 
-    def momentum_part(begin, end):
+    def momentum_right(begin, end):
         @pl.loop(begin, end)
         def _(j):
             columns = pl.ds(pl.multiple_of(256 * j, 256), 256)
@@ -310,7 +265,7 @@
                 piece = total[:, 128 * k : 128 * k + 128].reshape(2, 256, 128)
                 wt[lax.div(j, 2), 2 * lax.rem(j, 2) + k] = piece
 
-    momentum_part(0, 2)
+    momentum_right(0, 2)
     all_of(va)
     v_sx[...] = sum4(v_x)
     va = sent(send, recv, 13, Z, lambda to: v_sx.at[to], lambda to: v_ez.at[z])
@@ -320,52 +275,29 @@
     v_ez[z] = v_sx[z]
     v_ex[x] = v_sz[x]
     all_of(g)
+    gz[z] = sum4(gx)
+    g = sent(send, recv, 7, Z, lambda to: gz.at[z], lambda to: gz.at[z])
+    momentum_right(2, 3)
+    all_of(va)
+    v_all[c, y, 0] = sum4(v_ez)
+    all_of(vb)
+    v_all[c, y, 1] = sum4(v_ex)
+    v = sent(send, recv, 19, Y, lambda to: v_all.at[c, y], lambda to: v_all.at[c, y])
+    all_of(g)
     gram[y, c, x] = sum4(gz)
     g = sent(send, recv, 8, X, lambda to: gram.at[y, c, x], lambda to: gram.at[y, c, x])
-    all_of(va)
-    v_own[0] = sum4(v_ez)
-    all_of(vb)
-    v_own[1] = sum4(v_ex)
-
-    def v_copy(dy, dc):
-        return pltpu.make_async_remote_copy(
-            src_ref=v_own,
-            dst_ref=v_all.at[lax.rem(x, 2), z],
-            send_sem=v_send.at[dy, dc],
-            recv_sem=v_recv.at[lax.rem(x, 2), z],
-            device_id={X: y, Z: 2 * c + lax.div(x, 2), Y: partner(Y, dy), C: partner(C, dc)},
-            device_id_type=MESH,
-        )
-
-    def v_keep():
-        v_all[lax.rem(x, 2), z] = v_own[...]
-
-    def v_arrived(first, xx, zz):
-        copy = pltpu.make_async_remote_copy(
-            src_ref=v_own,
-            dst_ref=v_all.at[xx, zz],
-            send_sem=v_send.at[0, 0],
-            recv_sem=v_recv.at[xx, zz],
-            device_id={X: 2 * lax.rem(z, 2) + xx, Z: zz, Y: x, C: lax.div(z, 2)},
-            device_id_type=MESH,
-        )
-        apart(first, v_self, copy.wait_recv, nothing)
-
-    for dy in range(4):
-        for dc in range(2):
-            apart(dy == dc == 0, v_self, v_copy(dy, dc).start, v_keep)
+    momentum_right(3, 5)
+    all_of(v)
+    v = sent(send, recv, 20, C, lambda to: v_all.at[c], lambda to: v_all.at[c])
     all_of(g)
     g = sent(send, recv, 9, Y, lambda to: gram.at[y, c], lambda to: gram.at[y, c])
-    momentum_part(2, 8)
-    all_of(g)
-    g = sent(send, recv, 10, C, lambda to: gram.at[:, c], lambda to: gram.at[:, c])
-    v_sources(v_arrived)
-    for dy in range(4):
-        for dc in range(2):
-            apart(dy == dc == 0, v_self, v_copy(dy, dc).wait_send, nothing)
+    momentum_right(5, 8)
+    all_of(v)
     t_hi, t_lo = halves(v_all[...].reshape(256, RANK).T)
     q_hi[RANK : 2 * RANK, 0:256] = t_hi
     q_lo[RANK : 2 * RANK, 0:256] = t_lo
+    all_of(g)
+    g = sent(send, recv, 10, C, lambda to: gram.at[:, c], lambda to: gram.at[:, c])
 
     @pl.loop(0, 8)
     def _(j):
@@ -383,16 +315,16 @@
 
 def chain(activations, grad_out, momentum, right_factor):
     shapes = [
-        ((2048, RANK), BF16), ((2048, RANK), BF16),
+        ((2048, RANK), BF16), ((2048, RANK), BF16), ((16, 32, 512), BF16),
         ((2, 4, 32, RANK), F32), ((4, 32, RANK), F32), ((4, 32, RANK), F32), ((4, 32, RANK), F32),
-        ((32, RANK), F32), ((2, 2, 4, 32, RANK), F32),
+        ((4, 4, 2, 16, RANK), F32),
         ((2, 4, 64, RANK), F32), ((4, 64, RANK), F32), ((4, 64, RANK), F32), ((4, 64, RANK), F32),
         ((2, 4, 16, RANK), F32), ((4, 16, RANK), F32), ((4, 16, RANK), F32),
         ((4, 4, 2, 16, RANK), F32), ((4, 4, 16, RANK), F32), ((4, 4, 16, RANK), F32),
         ((4, 16, RANK), F32), ((4, 16, RANK), F32), ((4, 16, RANK), F32), ((4, 16, RANK), F32),
-        ((2, 16, RANK), F32), ((2, 4, 2, 16, RANK), F32),
+        ((2, 4, 2, 16, RANK), F32),
     ]
-    semaphores = [(15, 3), (15, 3), (4, 4), (2, 2, 4), (4, 2), (2, 4)]
+    semaphores = [(21, 3), (21, 3), (4, 2), (4, 2)]
     return pl.pallas_call(
         chain_kernel,
         out_shape=(
@@ -405,27 +337,19 @@
         scratch_shapes=[pltpu.VMEM(*s) for s in shapes]
         + [pltpu.SemaphoreType.DMA(s) for s in semaphores],
         compiler_params=pltpu.CompilerParams(
-            collective_id=1, has_side_effects=True, vmem_limit_bytes=48 << 20
+            collective_id=1, has_side_effects=True, vmem_limit_bytes=58 << 20
         ),
         cost_estimate=pl.CostEstimate(flops=1 << 34, bytes_accessed=128 << 20, transcendentals=0),
-    )(activations, grad_out, momentum, right_factor)
+    )(activations, grad_out.reshape(2, 2, 4, 32, 512), momentum, right_factor)
 
 
 def right_kernel(
-    part, g_ref, a_all, m_ref, inv_ref, p_ref,
-    right_t, left, scale, buffer,
+    part, g_ref, inv_ref, p_ref,
+    right_t, left, scale, g_turned,
     from_x, from_z, sum_x, sum_z, end_x, end_z, out,
-    g_all, g_turned, tokens, squares, seen, send, recv, tile_sem,
+    g_all, squares, seen, send, recv,
 ):
     x, z, y, c = (lax.axis_index(a) for a in (X, Z, Y, C))
-
-    def tile(j):
-        slot = lax.rem(j, 2)
-        columns = pl.ds(pl.multiple_of(256 * j, 256), 256)
-        return pltpu.make_async_copy(a_all.at[:, columns], tokens.at[slot], tile_sem.at[slot])
-
-    tile(0).start()
-    tile(1).start()
     greet(line_peers((X, Z, Y, C)))
     a = sent(send, recv, 0, X, lambda to: part.at[to, :, 0], lambda to: from_x.at[x])
     b = sent(send, recv, 1, Z, lambda to: part.at[:, to, 1], lambda to: from_z.at[z])
@@ -458,17 +382,6 @@
     all_of(g)
     for n in range(8):
         g_turned[:, 512 * n : 512 * n + 512] = g_all[n // 2, n % 2].T
-
-    @pl.loop(0, 8)
-    def _(j):
-        tile(j).wait()
-        columns = pl.ds(pl.multiple_of(256 * j, 256), 256)
-        buffer[:, columns] = m_ref[:, columns] + one(g_turned[...], tokens[lax.rem(j, 2)])
-
-        @pl.when(j < 6)
-        def _():
-            tile(j + 2).start()
-
     all_of(a)
     all_of(b)
     inv_hi, inv_lo = halves(inv_ref[...])
@@ -494,82 +407,83 @@
     scale[...] = jnp.sqrt(sum4(seen)) + EPSILON
 
 
-def right_factors(part, grad_out, all_activations, momentum, inverse, left):
+def right_factors(part, grad_out, inverse, left):
     return pl.pallas_call(
         right_kernel,
         out_shape=(
             jax.ShapeDtypeStruct((RANK, 2048), F32),
             jax.ShapeDtypeStruct((RANK, RANK), F32),
             jax.ShapeDtypeStruct((8, RANK), F32),
-            jax.ShapeDtypeStruct((RANK, 2048), F32),
+            jax.ShapeDtypeStruct((512, 4096), BF16),
         ),
-        in_specs=[VMEM, VMEM, pl.BlockSpec(memory_space=pl.ANY), VMEM, VMEM, VMEM],
+        in_specs=[VMEM] * 4,
         out_specs=(VMEM,) * 4,
         scratch_shapes=[pltpu.VMEM((4, 4, 256, 128), F32)] * 2
         + [pltpu.VMEM((4, 256, 128), F32)] * 4
         + [
             pltpu.VMEM((4, 4, 2, 256, 128), F32),
             pltpu.VMEM((4, 2, 512, 512), BF16),
-            pltpu.VMEM((512, 4096), BF16),
-            pltpu.VMEM((2, 4096, 256), BF16),
             pltpu.VMEM((RANK, 128), F32),
             pltpu.VMEM((6, 8, RANK), F32),
             pltpu.SemaphoreType.DMA((12, 3)),
             pltpu.SemaphoreType.DMA((12, 3)),
-            pltpu.SemaphoreType.DMA((2,)),
         ],
         compiler_params=pltpu.CompilerParams(
-            collective_id=2, has_side_effects=True, vmem_limit_bytes=56 << 20
+            collective_id=2, has_side_effects=True, vmem_limit_bytes=58 << 20
         ),
         cost_estimate=pl.CostEstimate(flops=1 << 34, bytes_accessed=128 << 20, transcendentals=0),
-    )(part, grad_out, all_activations, momentum, inverse, left)
-
-
-def final_kernel(b_ref, r_ref, l_ref, n_ref, momentum, right, update):
+    )(part, grad_out, inverse, left)
+
+
+def final_kernel(a_ref, g_ref, m_ref, r_ref, l_ref, n_ref, momentum, right, update, low_ref, s_hi, s_lo):
     norms = n_ref[0:1, :]
+
+    @pl.when(pl.program_id(0) == 0)
+    def _():
+        ortho = l_ref[...]
+        low_ref[...] = (FEEDBACK * ortho).astype(BF16)
+        s_hi[...], s_lo[...] = halves(ortho * (math.sqrt(DOUT * DIN / RANK) / norms))
+
     raw = r_ref[...]
-    ortho = l_ref[...]
     r_hi, r_lo = halves(raw)
-    momentum[...] = b_ref[...] - FEEDBACK * one(ortho.astype(BF16), r_hi)
-    s_hi, s_lo = halves(ortho * (math.sqrt(DOUT * DIN / RANK) / norms))
-    update[...] = (one(s_hi, r_hi) + (one(s_hi, r_lo) + one(s_lo, r_hi))).astype(BF16)
+    buffer = m_ref[...] + one(g_ref[...], a_ref[...])
+    momentum[...] = buffer - one(low_ref[...], r_hi)
+    update[...] = (one(s_hi[...], r_hi) + (one(s_hi[...], r_lo) + one(s_lo[...], r_hi))).astype(BF16)
     right[...] = raw.T / norms
 
 
-def final(buffer, right_t, left, norms):
+def final(activations, grads, momentum, right_t, left, norms):
     wide = 256
+    tile = pl.BlockSpec((RANK, wide), lambda j: (0, j))
     return pl.pallas_call(
         final_kernel,
         grid=(2048 // wide,),
         in_specs=[
-            pl.BlockSpec((RANK, wide), lambda j: (0, j)),
-            pl.BlockSpec((RANK, wide), lambda j: (0, j)),
+            pl.BlockSpec((4096, wide), lambda j: (0, j)),
+            pl.BlockSpec((512, 4096), lambda j: (0, 0), pipeline_mode=pl.Buffered(1)),
+            tile,
+            tile,
             pl.BlockSpec((RANK, RANK), lambda j: (0, 0)),
             pl.BlockSpec((8, RANK), lambda j: (0, 0)),
         ],
-        out_specs=(
-            pl.BlockSpec((RANK, wide), lambda j: (0, j)),
-            pl.BlockSpec((wide, RANK), lambda j: (j, 0)),
-            pl.BlockSpec((RANK, wide), lambda j: (0, j)),
-        ),
+        out_specs=(tile, pl.BlockSpec((wide, RANK), lambda j: (j, 0)), tile),
         out_shape=(
             jax.ShapeDtypeStruct((RANK, 2048), F32),
             jax.ShapeDtypeStruct((2048, RANK), F32),
             jax.ShapeDtypeStruct((RANK, 2048), BF16),
         ),
+        scratch_shapes=[pltpu.VMEM((RANK, RANK), BF16)] * 3,
         compiler_params=pltpu.CompilerParams(vmem_limit_bytes=60 << 20),
-        cost_estimate=pl.CostEstimate(flops=1 << 32, bytes_accessed=20 << 20, transcendentals=0),
-    )(buffer, right_t, left, norms)
+        cost_estimate=pl.CostEstimate(flops=1 << 34, bytes_accessed=40 << 20, transcendentals=0),
+    )(activations, grads, momentum, right_t, left, norms)
 
 
 def body(activations, grad_out, momentum, right_factor):
     all_activations = lax.all_gather(activations, WIDE, axis=0, tiled=True)
     part, left_factor, gram_matrix = chain(activations, grad_out, momentum, right_factor)
     inverse = inverse_factor(gram_matrix.reshape(RANK, RANK))
-    right_t, ortho_left, norms, buffer = right_factors(
-        part, grad_out, all_activations, momentum, inverse, left_factor
-    )
-    return final(buffer, right_t, ortho_left, norms)
+    right_t, ortho_left, norms, grads = right_factors(part, grad_out, inverse, left_factor)
+    return final(all_activations, grads, momentum, right_t, ortho_left, norms)
 
 
 def solution(mesh):

time: 278 us -> 248 us (0.89)
  waiting for transfers between devices: 14.7 us -> 0.7 us
  Pallas kernels: 243 us -> 231 us
    pallas_call x1, Pallas kernels: 126 us -> 105 us  [chain(): pl.pallas_call(chain_kernel, out_shape=(jax.ShapeDtypeStruct((4, 4, 2, 25...]
    all_gather x1, waiting for transfers between devices: 14 us -> 0.02 us  [body(): all_activations = lax.all_gather(activations, WIDE, axis=0, tiled=True)]
    pallas_call x1, Pallas kernels: 11.3 us -> 21.4 us  [final(): pl.pallas_call(final_kernel, grid=(2048 // wide,), in_specs=[pl.BlockSpec...]
  transfers between devices with their start and end apart: 1 -> 1, of which waited for: 1 -> 0; matrix products, arithmetic and copies ran while one was open for 0% -> 0% of each run, Pallas kernels for 53% -> 85%
where the time goes in v4:
time: 248 us
  Pallas kernels  231 us (93%)
  between operations  14.1 us (6%)
    pallas_call x1, Pallas kernels, chain(): pl.pallas_call(chain_kernel, out_shape=(jax.ShapeDtypeStruct((4, 4, 2, 25...  105 us
    pallas_call x1, Pallas kernels, right_factors(): pl.pallas_call(right_kernel, out_shape=(jax.ShapeDtypeStruct((RANK, 2048)...  83.8 us
    pallas_call x1, Pallas kernels, final(): pl.pallas_call(final_kernel, grid=(2048 // wide,), in_specs=[pl.BlockSpec...  21.4 us
    pallas_call x1, Pallas kernels, inverse_factor(): pl.pallas_call(factor_kernel, out_shape=jax.ShapeDtypeStruct((512, 512),...  20.2 us
  transfers between devices with their start and end apart: 1, of which 0 were waited for; matrix products, arithmetic and copies ran while one was open for 0% of the time, Pallas kernels for 85%

profile of v4, /device:TPU:1, one launch (start us, length us, event | category | flops | bytes accessed | tf_op | source)
XLA Modules:
  0.0 247.6 jit_solution(6581942777495555413)
XLA Ops:
  7.2 0.0 all-gather.2.cloned.1.call-start
  7.2 0.7 all-gather.2.cloned.1.call-update
  7.9 105.2 %shard_map.67 = (f32[4,4,2,256,128]{4,3,2,1,0:T(8,128)}, f32[2,4,64,512]{3,2,1,0:T(8,128)}, f32[4,2,4,16,512]{4,3,2,1,0:T(8,128)}) custom-call(bf16[256,2048]{1,0:T(8,128)(2,1)} %a_ref.1, bf16[2,2,4,32,512]{4,3,2,1,0:T(8,128)(2,1)} %bitcast.3, f32[512,2048]{1,0:T(8,128)} %m_ref.3, f32[2048,512]{1,0:T(8,128)} %q_ref.1), custom_call_target="tpu_custom_call" | custom-call | flops 17179869184 | bytes 134217728 | tf_op jit(solution)/shard_map/pallas_call | solution.py:328
  113.1 0.0 copy-start.1
  113.1 1.2 copy-done.1
  114.4 20.2 %shard_map.68.inv_ref = f32[512,512]{1,0:T(8,128)S(1)} custom-call(f32[512,512]{1,0:T(8,128)S(1)} %bitcast.2), custom_call_target="tpu_custom_call" | custom-call | tf_op jit(solution)/shard_map/pallas_call | solution.py:89
  134.6 0.0 copy-start
  134.6 1.0 copy-done
  135.6 83.8 %shard_map.69 = (f32[512,2048]{1,0:T(8,128)}, f32[512,512]{1,0:T(8,128)}, f32[8,512]{1,0:T(8,128)}, bf16[512,4096]{1,0:T(8,128)(2,1)}) custom-call(f32[4,4,2,256,128]{4,3,2,1,0:T(8,128)} %get-tuple-element.10.part, bf16[512,512]{1,0:T(8,128)(2,1)} %g_ref.1, f32[512,512]{1,0:T(8,128)} %copy-done, f32[2,4,64,512]{3,2,1,0:T(8,128)} %get-tuple-element.12.p_ref), custom_call_target="tpu_custom_call" | custom-call | flops 17179869184 | bytes 134217728 | tf_op jit(solution)/shard_map/pallas_call | solution.py:411
  219.4 0.0 all-gather.2.cloned.1.call-done.a_ref
  219.4 21.4 %shard_map.70 = (f32[512,2048]{1,0:T(8,128)}, f32[2048,512]{1,0:T(8,128)}, bf16[512,2048]{1,0:T(8,128)(2,1)}) custom-call(bf16[4096,2048]{1,0:T(8,128)(2,1)} %all-gather.2.cloned.1.call-done.a_ref, bf16[512,4096]{1,0:T(8,128)(2,1)} %get-tuple-element.13.g_ref, f32[512,2048]{1,0:T(8,128)} %m_ref.3, f32[512,2048]{1,0:T(8,128)} %get-tuple-element.14.r_ref, ...), custom_call_target="tpu_custom_call" | custom-call | flops 17179869184 | bytes 41943040 | tf_op jit(solution)/shard_map/pallas_call | solution.py:458
Async XLA Ops:
  7.2 212.3 %all-gather.2.cloned.1.call-start = ((), (), s32[]{:S(2)}) async-start(), calls=%async_computation | async-start | bytes 17825792 | tf_op jit(solution)/shard_map/all_gather | solution.py:482
  113.1 1.3 copy-start.1
  134.6 1.0 copy-start
Sparse Core Ops, SparseCore 0:
  10.1 131.2 all-gather.1

commit v5 on v4

--- a/solution.py
+++ b/solution.py
@@ -63,33 +63,32 @@
             rows[g] = total
     return rows
 
-def factor_kernel(c_ref, out_ref, s_ref):
-    hi = lax.Precision.HIGHEST
-    s_ref[...] = c_ref[...]
+
+def inverse_factor(s_ref, out_ref):
+    highest = lax.Precision.HIGHEST
     row = lax.broadcasted_iota(jnp.int32, (128, 128), 0)
     col = lax.broadcasted_iota(jnp.int32, (128, 128), 1)
-    for b in range(4):
-        o = 128 * b
-        rows = [s_ref[o + 8 * g : o + 8 * g + 8, o : o + 128] for g in range(16)]
-        inv = jnp.concatenate(eliminated(rows), axis=0)
-        inv = jnp.where(row >= col, inv, 0.0)
-        s_ref[o : o + 128, o : o + 128] = jnp.where(row == col, 1.0, 0.0).astype(F32)
-        y = jnp.dot(inv, s_ref[o : o + 128, :], precision=hi, preferred_element_type=F32)
-        s_ref[o : o + 128, :] = y
-        if b < 3:
-            rest = y[:, o + 128 :]
-            s_ref[o + 128 :, o : o + 128] = jnp.zeros((384 - o, 128), F32)
-            s_ref[o + 128 :, :] = s_ref[o + 128 :, :] - lax.dot_general(
-                rest, y, (((0,), (0,)), ((), ())), precision=hi, preferred_element_type=F32)
-    row = lax.broadcasted_iota(jnp.int32, (512, 512), 0)
-    col = lax.broadcasted_iota(jnp.int32, (512, 512), 1)
+    tall = lax.broadcasted_iota(jnp.int32, (RANK, 128), 0)
+    wide = lax.broadcasted_iota(jnp.int32, (128, RANK), 1)
+
+    @pl.loop(0, 4)
+    def _(b):
+        o = pl.multiple_of(128 * b, 128)
+        here = pl.ds(o, 128)
+        rows = [s_ref[pl.ds(pl.multiple_of(o + 8 * g, 8), 8), here] for g in range(16)]
+        inv = jnp.where(row >= col, jnp.concatenate(eliminated(rows), axis=0), 0.0)
+        s_ref[here, here] = jnp.where(row == col, 1.0, 0.0).astype(F32)
+        y = jnp.dot(inv, s_ref[here, :], precision=highest, preferred_element_type=F32)
+        s_ref[here, :] = y
+        s_ref[:, here] = jnp.where(tall >= o + 128, 0.0, s_ref[:, here])
+        rest = jnp.where(wide >= o + 128, y, 0.0)
+        s_ref[...] = s_ref[...] - lax.dot_general(
+            rest, y, (((0,), (0,)), ((), ())), precision=highest, preferred_element_type=F32
+        )
+
+    row = lax.broadcasted_iota(jnp.int32, (RANK, RANK), 0)
+    col = lax.broadcasted_iota(jnp.int32, (RANK, RANK), 1)
     out_ref[...] = jnp.where(row >= col, s_ref[...], 0.0)
-
-def inverse_factor(c):
-    return pl.pallas_call(factor_kernel, out_shape=jax.ShapeDtypeStruct((512,512),F32),
-        in_specs=[pl.BlockSpec(memory_space=pltpu.VMEM)], out_specs=pl.BlockSpec(memory_space=pltpu.VMEM),
-        scratch_shapes=[pltpu.VMEM((512,512),F32)],
-        compiler_params=pltpu.CompilerParams(vmem_limit_bytes=32<<20))(c)
 
 
 def halves(value):
@@ -344,10 +343,10 @@
 
 
 def right_kernel(
-    part, g_ref, inv_ref, p_ref,
-    right_t, left, scale, g_turned,
-    from_x, from_z, sum_x, sum_z, end_x, end_z, out,
-    g_all, squares, seen, send, recv,
+    part, g_ref, gram_ref, p_ref,
+    out, left, scale, g_turned,
+    from_x, from_z, sum_x, sum_z, end_x, end_z,
+    g_all, factor, inverse, seen, send, recv,
 ):
     x, z, y, c = (lax.axis_index(a) for a in (X, Z, Y, C))
     greet(line_peers((X, Z, Y, C)))
@@ -357,8 +356,9 @@
     from_x[x] = part[x, :, 0]
     from_z[z] = part[:, z, 1]
     g_all[y, c] = g_ref[...]
-    left[...] = dot3(p_ref[...].reshape(RANK, RANK), inv_ref[...], ((1,), (1,)))
-    squares[...] = jnp.zeros_like(squares)
+    factor[...] = gram_ref[...].reshape(RANK, RANK)
+    inverse_factor(factor, inverse)
+    inv_hi, inv_lo = halves(inverse[...])
     all_of(a)
     sum_x[...] = sum4(from_x)
     a = sent(send, recv, 2, Z, lambda to: sum_x.at[to], lambda to: end_z.at[z])
@@ -370,48 +370,45 @@
     all_of(g)
     g = sent(send, recv, 9, C, lambda to: g_all.at[:, c], lambda to: g_all.at[:, c])
     all_of(a)
-    out[x, z, 0] = sum4(end_z)
+    all_of(b)
+
+    high, low = halves(jnp.concatenate([sum4(end_z), sum4(end_x)], axis=0))
+    share = one(inv_hi, high) + (one(inv_hi, low) + one(inv_lo, high))
+    out[x, z] = share.reshape(2, 256, 128)
     a = sent(send, recv, 4, Z, lambda to: out.at[x, z, 0], lambda to: out.at[x, z, 0])
-    all_of(b)
-    out[x, z, 1] = sum4(end_x)
     b = sent(send, recv, 5, X, lambda to: out.at[x, z, 1], lambda to: out.at[x, z, 1])
+    seen[0, c] = lax.dot_general(
+        jnp.ones((8, 128), F32), share * share, (((1,), (1,)), ((), ())),
+        precision=lax.Precision.HIGHEST, preferred_element_type=F32,
+    )
+    all_of(sent(send, recv, 10, C, lambda to: seen.at[0, c], lambda to: seen.at[0, c]))
+    seen[1, x] = seen[0, 0] + seen[0, 1]
+    q = sent(send, recv, 11, X, lambda to: seen.at[1, x], lambda to: seen.at[1, x])
     all_of(a)
     a = sent(send, recv, 6, X, lambda to: out.at[x, :, 0], lambda to: out.at[x, :, 0])
     all_of(b)
     b = sent(send, recv, 7, Z, lambda to: out.at[:, z, 1], lambda to: out.at[:, z, 1])
+    all_of(q)
+    seen[2, z] = sum4(seen.at[1])
+    q = sent(send, recv, 12, Z, lambda to: seen.at[2, z], lambda to: seen.at[2, z])
+    left[...] = dot3(p_ref[...].reshape(RANK, RANK), inverse[...], ((1,), (1,)))
+    all_of(q)
+    seen[3, y] = sum4(seen.at[2])
+    q = sent(send, recv, 13, Y, lambda to: seen.at[3, y], lambda to: seen.at[3, y])
     all_of(g)
     for n in range(8):
         g_turned[:, 512 * n : 512 * n + 512] = g_all[n // 2, n % 2].T
+    all_of(q)
+    scale[...] = jnp.sqrt(sum4(seen.at[3])) + EPSILON
     all_of(a)
     all_of(b)
-    inv_hi, inv_lo = halves(inv_ref[...])
-
-    @pl.loop(0, 8)
-    def _(j):
-        at = 2 * lax.rem(j, 2)
-        pieces = [out[lax.div(j, 2), at + k].reshape(RANK, 128) for k in range(2)]
-        high, low = halves(jnp.concatenate(pieces, axis=1))
-        total = one(inv_hi, high) + (one(inv_hi, low) + one(inv_lo, high))
-        right_t[:, pl.ds(pl.multiple_of(256 * j, 256), 256)] = total
-        square = total * total
-        squares[...] += square[:, :128] + square[:, 128:]
-
-    ones = jnp.ones((8, 128), F32)
-    seen[4 + c] = lax.dot_general(
-        ones, squares[...], (((1,), (1,)), ((), ())),
-        precision=lax.Precision.HIGHEST, preferred_element_type=F32,
-    )
-    all_of(sent(send, recv, 10, C, lambda to: seen.at[4 + c], lambda to: seen.at[4 + c]))
-    seen[y] = seen[4] + seen[5]
-    all_of(sent(send, recv, 11, Y, lambda to: seen.at[y], lambda to: seen.at[y]))
-    scale[...] = jnp.sqrt(sum4(seen)) + EPSILON
-
-
-def right_factors(part, grad_out, inverse, left):
+
+
+def right_factors(part, grad_out, gram, left):
     return pl.pallas_call(
         right_kernel,
         out_shape=(
-            jax.ShapeDtypeStruct((RANK, 2048), F32),
+            jax.ShapeDtypeStruct((4, 4, 2, 256, 128), F32),
             jax.ShapeDtypeStruct((RANK, RANK), F32),
             jax.ShapeDtypeStruct((8, RANK), F32),
             jax.ShapeDtypeStruct((512, 4096), BF16),
@@ -421,18 +418,18 @@
         scratch_shapes=[pltpu.VMEM((4, 4, 256, 128), F32)] * 2
         + [pltpu.VMEM((4, 256, 128), F32)] * 4
         + [
-            pltpu.VMEM((4, 4, 2, 256, 128), F32),
             pltpu.VMEM((4, 2, 512, 512), BF16),
-            pltpu.VMEM((RANK, 128), F32),
-            pltpu.VMEM((6, 8, RANK), F32),
-            pltpu.SemaphoreType.DMA((12, 3)),
-            pltpu.SemaphoreType.DMA((12, 3)),
+            pltpu.VMEM((RANK, RANK), F32),
+            pltpu.VMEM((RANK, RANK), F32),
+            pltpu.VMEM((4, 4, 8, RANK), F32),
+            pltpu.SemaphoreType.DMA((14, 3)),
+            pltpu.SemaphoreType.DMA((14, 3)),
         ],
         compiler_params=pltpu.CompilerParams(
             collective_id=2, has_side_effects=True, vmem_limit_bytes=58 << 20
         ),
         cost_estimate=pl.CostEstimate(flops=1 << 34, bytes_accessed=128 << 20, transcendentals=0),
-    )(part, grad_out, inverse, left)
+    )(part, grad_out, gram, left)
 
 
 def final_kernel(a_ref, g_ref, m_ref, r_ref, l_ref, n_ref, momentum, right, update, low_ref, s_hi, s_lo):
@@ -444,7 +441,7 @@
         low_ref[...] = (FEEDBACK * ortho).astype(BF16)
         s_hi[...], s_lo[...] = halves(ortho * (math.sqrt(DOUT * DIN / RANK) / norms))
 
-    raw = r_ref[...]
+    raw = jnp.concatenate([r_ref[0, k].reshape(RANK, 128) for k in range(2)], axis=1)
     r_hi, r_lo = halves(raw)
     buffer = m_ref[...] + one(g_ref[...], a_ref[...])
     momentum[...] = buffer - one(low_ref[...], r_hi)
@@ -462,7 +459,7 @@
             pl.BlockSpec((4096, wide), lambda j: (0, j)),
             pl.BlockSpec((512, 4096), lambda j: (0, 0), pipeline_mode=pl.Buffered(1)),
             tile,
-            tile,
+            pl.BlockSpec((1, 2, 2, 256, 128), lambda j: (j // 2, j % 2, 0, 0, 0)),
             pl.BlockSpec((RANK, RANK), lambda j: (0, 0)),
             pl.BlockSpec((8, RANK), lambda j: (0, 0)),
         ],
@@ -481,8 +478,7 @@
 def body(activations, grad_out, momentum, right_factor):
     all_activations = lax.all_gather(activations, WIDE, axis=0, tiled=True)
     part, left_factor, gram_matrix = chain(activations, grad_out, momentum, right_factor)
-    inverse = inverse_factor(gram_matrix.reshape(RANK, RANK))
-    right_t, ortho_left, norms, grads = right_factors(part, grad_out, inverse, left_factor)
+    right_t, ortho_left, norms, grads = right_factors(part, grad_out, gram_matrix, left_factor)
     return final(all_activations, grads, momentum, right_t, ortho_left, norms)
 
 

time: 248 us -> 242 us (0.976)
  Pallas kernels: 231 us -> 226 us
    pallas_call x2 -> x1, Pallas kernels: 104 us -> 99.2 us  [right_factors(): pl.pallas_call(right_kernel, out_shape=(jax.ShapeDtypeStruct((4, 4, 2, 25...]
where the time goes in v5:
time: 242 us; the launch traced here: 241 us
  Pallas kernels  226 us (93%)
  between operations  14.1 us (6%)
    pallas_call x1, Pallas kernels, chain(): pl.pallas_call(chain_kernel, out_shape=(jax.ShapeDtypeStruct((4, 4, 2, 25...  105 us
    pallas_call x1, Pallas kernels, right_factors(): pl.pallas_call(right_kernel, out_shape=(jax.ShapeDtypeStruct((4, 4, 2, 25...  99.2 us
    pallas_call x1, Pallas kernels, final(): pl.pallas_call(final_kernel, grid=(2048 // wide,), in_specs=[pl.BlockSpec...  21.4 us
  transfers between devices with their start and end apart: 1, of which 0 were waited for; matrix products, arithmetic and copies ran while one was open for 0% of the time, Pallas kernels for 85%

profile of v5, /device:TPU:1, one launch (start us, length us, event | category | flops | bytes accessed | tf_op | source)
XLA Modules:
  0.0 240.6 jit_solution(13098529430663743522)
XLA Ops:
  7.2 0.0 all-gather.2.cloned.1.call-start
  7.2 0.7 all-gather.2.cloned.1.call-update
  7.9 105.2 %shard_map.67 = (f32[4,4,2,256,128]{4,3,2,1,0:T(8,128)}, f32[2,4,64,512]{3,2,1,0:T(8,128)}, f32[4,2,4,16,512]{4,3,2,1,0:T(8,128)}) custom-call(bf16[256,2048]{1,0:T(8,128)(2,1)} %a_ref.1, bf16[2,2,4,32,512]{4,3,2,1,0:T(8,128)(2,1)} %bitcast.1, f32[512,2048]{1,0:T(8,128)} %m_ref.3, f32[2048,512]{1,0:T(8,128)} %q_ref.1), custom_call_target="tpu_custom_call" | custom-call | flops 17179869184 | bytes 134217728 | tf_op jit(solution)/shard_map/pallas_call | solution.py:327
  113.1 99.2 %shard_map.68 = (f32[4,4,2,256,128]{4,3,2,1,0:T(8,128)}, f32[512,512]{1,0:T(8,128)}, f32[8,512]{1,0:T(8,128)}, bf16[512,4096]{1,0:T(8,128)(2,1)}) custom-call(f32[4,4,2,256,128]{4,3,2,1,0:T(8,128)} %get-tuple-element.10.part, bf16[512,512]{1,0:T(8,128)(2,1)} %g_ref.1, f32[4,2,4,16,512]{4,3,2,1,0:T(8,128)} %get-tuple-element.11.gram_ref, ...), custom_call_target="tpu_custom_call" | custom-call | flops 17179869184 | bytes 134217728 | tf_op jit(solution)/shard_map/pallas_call | solution.py:408
  212.3 0.0 all-gather.2.cloned.1.call-done.a_ref
  212.4 21.4 %shard_map.69 = (f32[512,2048]{1,0:T(8,128)}, f32[2048,512]{1,0:T(8,128)}, bf16[512,2048]{1,0:T(8,128)(2,1)}) custom-call(bf16[4096,2048]{1,0:T(8,128)(2,1)} %all-gather.2.cloned.1.call-done.a_ref, bf16[512,4096]{1,0:T(8,128)(2,1)} %get-tuple-element.13.g_ref, f32[512,2048]{1,0:T(8,128)} %m_ref.3, f32[4,4,2,256,128]{4,3,2,1,0:T(8,128)} %get-tuple-element.14.r_ref, ...), custom_call_target="tpu_custom_call" | custom-call | flops 17179869184 | bytes 41943040 | tf_op jit(solution)/shard_map/pallas_call | solution.py:455
Async XLA Ops:
  7.2 205.2 %all-gather.2.cloned.1.call-start = ((), (), s32[]{:S(2)}) async-start(), calls=%async_computation | async-start | bytes 17825792 | tf_op jit(solution)/shard_map/all_gather | solution.py:479
Sparse Core Ops, SparseCore 0:
  10.1 151.1 all-gather.1

commit v6 on v5

--- a/solution.py
+++ b/solution.py
@@ -64,14 +64,14 @@
     return rows
 
 
-def inverse_factor(s_ref, out_ref):
+def factored(s_ref, begin, end):
     highest = lax.Precision.HIGHEST
     row = lax.broadcasted_iota(jnp.int32, (128, 128), 0)
     col = lax.broadcasted_iota(jnp.int32, (128, 128), 1)
     tall = lax.broadcasted_iota(jnp.int32, (RANK, 128), 0)
     wide = lax.broadcasted_iota(jnp.int32, (128, RANK), 1)
 
-    @pl.loop(0, 4)
+    @pl.loop(begin, end)
     def _(b):
         o = pl.multiple_of(128 * b, 128)
         here = pl.ds(o, 128)
@@ -86,9 +86,11 @@
             rest, y, (((0,), (0,)), ((), ())), precision=highest, preferred_element_type=F32
         )
 
-    row = lax.broadcasted_iota(jnp.int32, (RANK, RANK), 0)
-    col = lax.broadcasted_iota(jnp.int32, (RANK, RANK), 1)
-    out_ref[...] = jnp.where(row >= col, s_ref[...], 0.0)
+
+def lower_part(value):
+    row = lax.broadcasted_iota(jnp.int32, value.shape, 0)
+    col = lax.broadcasted_iota(jnp.int32, value.shape, 1)
+    return jnp.where(row >= col, value, 0.0)
 
 
 def halves(value):
@@ -109,6 +111,9 @@
 def partner(axis, step):
     size = 2 if axis == C else 4
     return lax.rem(lax.axis_index(axis) + step, size)
+
+
+ANY = pl.BlockSpec(memory_space=pl.ANY)
 
 
 def line_peers(axes):
@@ -157,14 +162,65 @@
     return (ref[0] + ref[1]) + (ref[2] + ref[3])
 
 
+def hop(send, recv, phase, axis, step, source, target):
+    copy = pltpu.make_async_remote_copy(
+        src_ref=source,
+        dst_ref=target,
+        send_sem=send.at[phase, 0],
+        recv_sem=recv.at[phase, 0],
+        device_id={axis: partner(axis, step)},
+        device_id_type=MESH,
+    )
+    copy.start()
+    return copy
+
+
+def sum_begun(send, recv, phase, axis, piece, relays, come):
+    right, left, far = partner(axis, 1), partner(axis, 3), partner(axis, 2)
+    return [
+        hop(send, recv, phase, axis, 1, piece(far, 0), relays.at[0]),
+        hop(send, recv, phase + 1, axis, 3, piece(far, 1), relays.at[1]),
+        hop(send, recv, phase + 2, axis, 1, piece(right, 1), come.at[0, 2:4]),
+        hop(send, recv, phase + 3, axis, 3, piece(left, 0), come.at[1, 0:2]),
+    ]
+
+
+def sum_relayed(send, recv, phase, axis, begun, piece, relays, passed, come):
+    right, left = partner(axis, 1), partner(axis, 3)
+    begun[0].wait()
+    passed[0] = relays[0] + piece(right, 0)[...]
+    first = hop(send, recv, phase + 4, axis, 1, passed.at[0], come.at[0, 0:2])
+    begun[1].wait()
+    passed[1] = relays[1] + piece(left, 1)[...]
+    return begun[2:] + [first, hop(send, recv, phase + 5, axis, 3, passed.at[1], come.at[1, 2:4])]
+
+
+def gather_begun(send, recv, phase, axis, piece):
+    me = lax.axis_index(axis)
+    return [
+        hop(send, recv, phase, axis, 1, piece(me), piece(me)),
+        hop(send, recv, phase + 1, axis, 3, piece(me), piece(me)),
+    ]
+
+
+def gather_relayed(send, recv, phase, axis, begun, part):
+    right, left = partner(axis, 1), partner(axis, 3)
+    begun[0].wait()
+    first = hop(send, recv, phase + 2, axis, 1, part(left, 0), part(left, 0))
+    begun[1].wait()
+    return [first, hop(send, recv, phase + 3, axis, 3, part(right, 1), part(right, 1))]
+
+
 def chain_kernel(
     a_ref, g_ref, m_ref, q_ref,
-    wt, left, gram,
-    q_hi, q_lo, g_mine, z_part, z_pair, z_half, z_seen, z_all,
+    solved, ortho, grads_out,
+    wt, left, gram, q_hi, q_lo, g_mine, z_part, z_pair, z_half, z_seen, z_all,
     part, pair, half, share,
     block, gx, gz,
     v_part, v_x, v_z, v_sx, v_sz, v_ex, v_ez, v_all,
-    send, recv, g_send, g_recv,
+    relay_x, relay_z, pass_x, pass_z, come_x, come_z, end_x, end_z,
+    g_all, g_turned, factor, inverse,
+    send, recv, g_send, g_recv, out_sem,
 ):
     x, z, y, c = (lax.axis_index(a) for a in (X, Z, Y, C))
     first = ((0,), (0,))
@@ -309,10 +365,55 @@
             at = (lax.div(j, 2), 2 * lax.rem(j, 2) + k)
             wt[at] = wt[at] + piece
 
+    def part_x(to, half):
+        return wt.at[to, 2 * half : 2 * half + 2, 0]
+
+    def part_z(to, half):
+        return wt.at[2 * half : 2 * half + 2, to, 1]
+
+    a = sum_begun(send, recv, 21, X, part_x, relay_x, come_x)
+    b = sum_begun(send, recv, 27, Z, part_z, relay_z, come_z)
     all_of(g)
+    g = sent(send, recv, 33, Y, lambda to: g_ref, lambda to: g_all.at[y, c])
+    g_all[y, c] = g_ref[...]
+    factor[...] = gram[...].reshape(RANK, RANK)
+    factored(factor, 0, 2)
+    a = sum_relayed(send, recv, 21, X, a, part_x, relay_x, pass_x, come_x)
+    b = sum_relayed(send, recv, 27, Z, b, part_z, relay_z, pass_z, come_z)
+    factored(factor, 2, 4)
+    inverse[...] = lower_part(factor[...])
+    all_of(a)
+    sum_x = wt.at[x, :, 0]
+    sum_x[...] = sum_x[...] + (come_x[0] + come_x[1])
+    a = sent(send, recv, 34, Z, lambda to: wt.at[x, to, 0], lambda to: end_z.at[z])
+    all_of(b)
+    sum_z = wt.at[:, z, 1]
+    sum_z[...] = sum_z[...] + (come_z[0] + come_z[1])
+    b = sent(send, recv, 35, X, lambda to: wt.at[to, z, 1], lambda to: end_x.at[x])
+    end_z[z] = wt[x, z, 0]
+    end_x[x] = wt[x, z, 1]
+    all_of(g)
+    g = sent(send, recv, 36, C, lambda to: g_all.at[:, c], lambda to: g_all.at[:, c])
+    inv_hi, inv_lo = halves(inverse[...])
+    last = ((1,), (1,))
+    ortho[...] = one(p_hi, inv_hi, last) + (one(p_hi, inv_lo, last) + one(p_lo, inv_hi, last))
+    all_of(g)
+
+    @pl.loop(0, 8)
+    def _(n):
+        g_turned[n] = g_all[lax.div(n, 2), lax.rem(n, 2)].reshape(512, 512).T
+
+    copy = pltpu.make_async_copy(g_turned, grads_out, out_sem)
+    copy.start()
+    all_of(a)
+    all_of(b)
+    high, low = halves(jnp.concatenate([sum4(end_z), sum4(end_x)], axis=0))
+    solved[...] = one(inv_hi, high) + (one(inv_hi, low) + one(inv_lo, high))
+    copy.wait()
 
 
 def chain(activations, grad_out, momentum, right_factor):
+    big = [((4, 4, 2, 256, 128), F32), ((2, 4, 64, RANK), F32), ((4, 2, 4, 16, RANK), F32)]
     shapes = [
         ((2048, RANK), BF16), ((2048, RANK), BF16), ((16, 32, 512), BF16),
         ((2, 4, 32, RANK), F32), ((4, 32, RANK), F32), ((4, 32, RANK), F32), ((4, 32, RANK), F32),
@@ -322,18 +423,24 @@
         ((4, 4, 2, 16, RANK), F32), ((4, 4, 16, RANK), F32), ((4, 4, 16, RANK), F32),
         ((4, 16, RANK), F32), ((4, 16, RANK), F32), ((4, 16, RANK), F32), ((4, 16, RANK), F32),
         ((2, 4, 2, 16, RANK), F32),
+        ((2, 2, 256, 128), F32), ((2, 2, 256, 128), F32),
+        ((2, 2, 256, 128), F32), ((2, 2, 256, 128), F32),
+        ((2, 4, 256, 128), F32), ((2, 4, 256, 128), F32),
+        ((4, 256, 128), F32), ((4, 256, 128), F32),
+        ((4, 2, 2, 2, 4, 32, 512), BF16), ((8, 512, 512), BF16),
+        ((RANK, RANK), F32), ((RANK, RANK), F32),
     ]
-    semaphores = [(21, 3), (21, 3), (4, 2), (4, 2)]
+    semaphores = [(37, 3), (37, 3), (4, 2), (4, 2), ()]
     return pl.pallas_call(
         chain_kernel,
         out_shape=(
-            jax.ShapeDtypeStruct((4, 4, 2, 256, 128), F32),
-            jax.ShapeDtypeStruct((2, 4, 64, RANK), F32),
-            jax.ShapeDtypeStruct((4, 2, 4, 16, RANK), F32),
+            jax.ShapeDtypeStruct((RANK, 128), F32),
+            jax.ShapeDtypeStruct((RANK, RANK), F32),
+            jax.ShapeDtypeStruct((8, 512, 512), BF16),
         ),
         in_specs=[VMEM] * 4,
-        out_specs=(VMEM,) * 3,
-        scratch_shapes=[pltpu.VMEM(*s) for s in shapes]
+        out_specs=(VMEM, VMEM, ANY),
+        scratch_shapes=[pltpu.VMEM(*s) for s in big + shapes]
         + [pltpu.SemaphoreType.DMA(s) for s in semaphores],
         compiler_params=pltpu.CompilerParams(
             collective_id=1, has_side_effects=True, vmem_limit_bytes=58 << 20
@@ -342,122 +449,137 @@
     )(activations, grad_out.reshape(2, 2, 4, 32, 512), momentum, right_factor)
 
 
-def right_kernel(
-    part, g_ref, gram_ref, p_ref,
-    out, left, scale, g_turned,
-    from_x, from_z, sum_x, sum_z, end_x, end_z,
-    g_all, factor, inverse, seen, send, recv,
+def gather_kernel(
+    share, tokens, turned, momentum,
+    out, buffer, scale,
+    g_all, m_all, slots, sums, seen, send, recv, load_sem, tile_sem, store_sem,
 ):
     x, z, y, c = (lax.axis_index(a) for a in (X, Z, Y, C))
+
+    def tile(j):
+        slot = lax.rem(j, 2)
+        columns = pl.ds(pl.multiple_of(256 * j, 256), 256)
+        return pltpu.make_async_copy(tokens.at[:, columns], slots.at[slot], tile_sem.at[slot])
+
+    def store(j):
+        slot = lax.rem(j, 2)
+        columns = pl.ds(pl.multiple_of(256 * j, 256), 256)
+        return pltpu.make_async_copy(sums.at[slot], buffer.at[:, columns], store_sem.at[slot])
+
+    loads = [
+        pltpu.make_async_copy(turned.at[n], g_all.at[:, 512 * n : 512 * n + 512], load_sem.at[n])
+        for n in range(8)
+    ]
+    loads.append(pltpu.make_async_copy(momentum, m_all, load_sem.at[8]))
+    for load in loads:
+        load.start()
+    tile(0).start()
+    tile(1).start()
     greet(line_peers((X, Z, Y, C)))
-    a = sent(send, recv, 0, X, lambda to: part.at[to, :, 0], lambda to: from_x.at[x])
-    b = sent(send, recv, 1, Z, lambda to: part.at[:, to, 1], lambda to: from_z.at[z])
-    g = sent(send, recv, 8, Y, lambda to: g_ref, lambda to: g_all.at[y, c])
-    from_x[x] = part[x, :, 0]
-    from_z[z] = part[:, z, 1]
-    g_all[y, c] = g_ref[...]
-    factor[...] = gram_ref[...].reshape(RANK, RANK)
-    inverse_factor(factor, inverse)
-    inv_hi, inv_lo = halves(inverse[...])
+    own = share[...]
+    out[x, z] = own.reshape(2, 256, 128)
+    a = sent(send, recv, 0, Z, lambda to: out.at[x, z, 0], lambda to: out.at[x, z, 0])
+    b = sent(send, recv, 1, X, lambda to: out.at[x, z, 1], lambda to: out.at[x, z, 1])
+    seen[0, c] = lax.dot_general(
+        jnp.ones((8, 128), F32), own * own, (((1,), (1,)), ((), ())),
+        precision=lax.Precision.HIGHEST, preferred_element_type=F32,
+    )
+    all_of(sent(send, recv, 2, C, lambda to: seen.at[0, c], lambda to: seen.at[0, c]))
+    seen[1, x] = seen[0, 0] + seen[0, 1]
+    q = sent(send, recv, 3, X, lambda to: seen.at[1, x], lambda to: seen.at[1, x])
+    for load in loads:
+        load.wait()
+    all_of(q)
+    seen[2, z] = sum4(seen.at[1])
+    q = sent(send, recv, 4, Z, lambda to: seen.at[2, z], lambda to: seen.at[2, z])
     all_of(a)
-    sum_x[...] = sum4(from_x)
-    a = sent(send, recv, 2, Z, lambda to: sum_x.at[to], lambda to: end_z.at[z])
+    a = gather_begun(send, recv, 6, X, lambda at: out.at[at, :, 0])
     all_of(b)
-    sum_z[...] = sum4(from_z)
-    b = sent(send, recv, 3, X, lambda to: sum_z.at[to], lambda to: end_x.at[x])
-    end_z[z] = sum_x[z]
-    end_x[x] = sum_z[x]
-    all_of(g)
-    g = sent(send, recv, 9, C, lambda to: g_all.at[:, c], lambda to: g_all.at[:, c])
+    b = gather_begun(send, recv, 10, Z, lambda at: out.at[:, at, 1])
+    all_of(q)
+    seen[3, y] = sum4(seen.at[2])
+    q = sent(send, recv, 5, Y, lambda to: seen.at[3, y], lambda to: seen.at[3, y])
+
+    def gradient(begin, end):
+        @pl.loop(begin, end)
+        def _(j):
+            slot = lax.rem(j, 2)
+            columns = pl.ds(pl.multiple_of(256 * j, 256), 256)
+            tile(j).wait()
+
+            @pl.when(j >= 2)
+            def _():
+                store(j - 2).wait()
+
+            sums[slot] = m_all[:, columns] + one(g_all[...], slots[slot])
+            store(j).start()
+
+            @pl.when(j < 6)
+            def _():
+                tile(j + 2).start()
+
+    gradient(0, 8)
+    a = gather_relayed(send, recv, 6, X, a, lambda at, h: out.at[at, 2 * h : 2 * h + 2, 0])
+    b = gather_relayed(send, recv, 10, Z, b, lambda at, h: out.at[2 * h : 2 * h + 2, at, 1])
+    all_of(q)
+    scale[...] = jnp.sqrt(sum4(seen.at[3])) + EPSILON
+    store(6).wait()
+    store(7).wait()
     all_of(a)
     all_of(b)
 
-    high, low = halves(jnp.concatenate([sum4(end_z), sum4(end_x)], axis=0))
-    share = one(inv_hi, high) + (one(inv_hi, low) + one(inv_lo, high))
-    out[x, z] = share.reshape(2, 256, 128)
-    a = sent(send, recv, 4, Z, lambda to: out.at[x, z, 0], lambda to: out.at[x, z, 0])
-    b = sent(send, recv, 5, X, lambda to: out.at[x, z, 1], lambda to: out.at[x, z, 1])
-    seen[0, c] = lax.dot_general(
-        jnp.ones((8, 128), F32), share * share, (((1,), (1,)), ((), ())),
-        precision=lax.Precision.HIGHEST, preferred_element_type=F32,
-    )
-    all_of(sent(send, recv, 10, C, lambda to: seen.at[0, c], lambda to: seen.at[0, c]))
-    seen[1, x] = seen[0, 0] + seen[0, 1]
-    q = sent(send, recv, 11, X, lambda to: seen.at[1, x], lambda to: seen.at[1, x])
-    all_of(a)
-    a = sent(send, recv, 6, X, lambda to: out.at[x, :, 0], lambda to: out.at[x, :, 0])
-    all_of(b)
-    b = sent(send, recv, 7, Z, lambda to: out.at[:, z, 1], lambda to: out.at[:, z, 1])
-    all_of(q)
-    seen[2, z] = sum4(seen.at[1])
-    q = sent(send, recv, 12, Z, lambda to: seen.at[2, z], lambda to: seen.at[2, z])
-    left[...] = dot3(p_ref[...].reshape(RANK, RANK), inverse[...], ((1,), (1,)))
-    all_of(q)
-    seen[3, y] = sum4(seen.at[2])
-    q = sent(send, recv, 13, Y, lambda to: seen.at[3, y], lambda to: seen.at[3, y])
-    all_of(g)
-    for n in range(8):
-        g_turned[:, 512 * n : 512 * n + 512] = g_all[n // 2, n % 2].T
-    all_of(q)
-    scale[...] = jnp.sqrt(sum4(seen.at[3])) + EPSILON
-    all_of(a)
-    all_of(b)
-
-
-def right_factors(part, grad_out, gram, left):
+
+def gathered(share, activations, grads, momentum):
     return pl.pallas_call(
-        right_kernel,
+        gather_kernel,
         out_shape=(
             jax.ShapeDtypeStruct((4, 4, 2, 256, 128), F32),
-            jax.ShapeDtypeStruct((RANK, RANK), F32),
+            jax.ShapeDtypeStruct((RANK, 2048), F32),
             jax.ShapeDtypeStruct((8, RANK), F32),
-            jax.ShapeDtypeStruct((512, 4096), BF16),
         ),
-        in_specs=[VMEM] * 4,
-        out_specs=(VMEM,) * 4,
-        scratch_shapes=[pltpu.VMEM((4, 4, 256, 128), F32)] * 2
-        + [pltpu.VMEM((4, 256, 128), F32)] * 4
-        + [
-            pltpu.VMEM((4, 2, 512, 512), BF16),
-            pltpu.VMEM((RANK, RANK), F32),
-            pltpu.VMEM((RANK, RANK), F32),
+        in_specs=[VMEM, ANY, ANY, ANY],
+        out_specs=(VMEM, ANY, VMEM),
+        scratch_shapes=[
+            pltpu.VMEM((512, 4096), BF16),
+            pltpu.VMEM((RANK, 2048), F32),
+            pltpu.VMEM((2, 4096, 256), BF16),
+            pltpu.VMEM((2, RANK, 256), F32),
             pltpu.VMEM((4, 4, 8, RANK), F32),
             pltpu.SemaphoreType.DMA((14, 3)),
             pltpu.SemaphoreType.DMA((14, 3)),
+            pltpu.SemaphoreType.DMA((9,)),
+            pltpu.SemaphoreType.DMA((2,)),
+            pltpu.SemaphoreType.DMA((2,)),
         ],
         compiler_params=pltpu.CompilerParams(
             collective_id=2, has_side_effects=True, vmem_limit_bytes=58 << 20
         ),
         cost_estimate=pl.CostEstimate(flops=1 << 34, bytes_accessed=128 << 20, transcendentals=0),
-    )(part, grad_out, gram, left)
-
-
-def final_kernel(a_ref, g_ref, m_ref, r_ref, l_ref, n_ref, momentum, right, update, low_ref, s_hi, s_lo):
-    norms = n_ref[0:1, :]
-
+    )(share, activations, grads, momentum)
+
+
+def final_kernel(b_ref, r_ref, l_ref, n_ref, momentum, right, update, low_ref, s_hi, s_lo, inv_ref):
     @pl.when(pl.program_id(0) == 0)
     def _():
         ortho = l_ref[...]
+        inv_ref[...] = 1.0 / n_ref[...]
         low_ref[...] = (FEEDBACK * ortho).astype(BF16)
-        s_hi[...], s_lo[...] = halves(ortho * (math.sqrt(DOUT * DIN / RANK) / norms))
+        s_hi[...], s_lo[...] = halves(ortho * (math.sqrt(DOUT * DIN / RANK) * inv_ref[0:1, :]))
 
     raw = jnp.concatenate([r_ref[0, k].reshape(RANK, 128) for k in range(2)], axis=1)
     r_hi, r_lo = halves(raw)
-    buffer = m_ref[...] + one(g_ref[...], a_ref[...])
-    momentum[...] = buffer - one(low_ref[...], r_hi)
+    momentum[...] = b_ref[...] - one(low_ref[...], r_hi)
     update[...] = (one(s_hi[...], r_hi) + (one(s_hi[...], r_lo) + one(s_lo[...], r_hi))).astype(BF16)
-    right[...] = raw.T / norms
-
-
-def final(activations, grads, momentum, right_t, left, norms):
+    right[...] = raw.T * inv_ref[0:1, :]
+
+
+def final(buffer, right_t, left, norms):
     wide = 256
     tile = pl.BlockSpec((RANK, wide), lambda j: (0, j))
     return pl.pallas_call(
         final_kernel,
         grid=(2048 // wide,),
         in_specs=[
-            pl.BlockSpec((4096, wide), lambda j: (0, j)),
-            pl.BlockSpec((512, 4096), lambda j: (0, 0), pipeline_mode=pl.Buffered(1)),
             tile,
             pl.BlockSpec((1, 2, 2, 256, 128), lambda j: (j // 2, j % 2, 0, 0, 0)),
             pl.BlockSpec((RANK, RANK), lambda j: (0, 0)),
@@ -469,17 +591,17 @@
             jax.ShapeDtypeStruct((2048, RANK), F32),
             jax.ShapeDtypeStruct((RANK, 2048), BF16),
         ),
-        scratch_shapes=[pltpu.VMEM((RANK, RANK), BF16)] * 3,
+        scratch_shapes=[pltpu.VMEM((RANK, RANK), BF16)] * 3 + [pltpu.VMEM((8, RANK), F32)],
         compiler_params=pltpu.CompilerParams(vmem_limit_bytes=60 << 20),
-        cost_estimate=pl.CostEstimate(flops=1 << 34, bytes_accessed=40 << 20, transcendentals=0),
-    )(activations, grads, momentum, right_t, left, norms)
+        cost_estimate=pl.CostEstimate(flops=1 << 32, bytes_accessed=20 << 20, transcendentals=0),
+    )(buffer, right_t, left, norms)
 
 
 def body(activations, grad_out, momentum, right_factor):
     all_activations = lax.all_gather(activations, WIDE, axis=0, tiled=True)
-    part, left_factor, gram_matrix = chain(activations, grad_out, momentum, right_factor)
-    right_t, ortho_left, norms, grads = right_factors(part, grad_out, gram_matrix, left_factor)
-    return final(all_activations, grads, momentum, right_t, ortho_left, norms)
+    share, ortho_left, grads = chain(activations, grad_out, momentum, right_factor)
+    right_t, buffer, norms = gathered(share, all_activations, grads, momentum)
+    return final(buffer, right_t, ortho_left, norms)
 
 
 def solution(mesh):

time: 242 us -> 220 us (0.909)
  Pallas kernels: 226 us -> 201 us
  waiting for transfers between devices: 0.7 us -> 4.26 us
    pallas_call x3, Pallas kernels: 226 us -> 201 us  [the longest x1 152 us: chain(): pl.pallas_call(chain_kernel, out_shape=(jax.ShapeDtypeStruct((RANK, 128),...]
    all_gather x1, waiting for transfers between devices: 0.02 us -> 3.58 us  [body(): all_activations = lax.all_gather(activations, WIDE, axis=0, tiled=True)]
  transfers between devices with their start and end apart: 1 -> 1, of which waited for: 0 -> 1; matrix products, arithmetic and copies ran while one was open for 0% -> 0% of each run, Pallas kernels for 85% -> 70%
where the time goes in v6:
time: 220 us; the launch traced here: 219 us
  Pallas kernels  201 us (91%)
  between operations  14 us (6%)
  waiting for transfers between devices  4.26 us (2%)
    pallas_call x1, Pallas kernels, chain(): pl.pallas_call(chain_kernel, out_shape=(jax.ShapeDtypeStruct((RANK, 128),...  152 us
    pallas_call x1, Pallas kernels, gathered(): pl.pallas_call(gather_kernel, out_shape=(jax.ShapeDtypeStruct((4, 4, 2, 2...  36.5 us
    pallas_call x1, Pallas kernels, final(): pl.pallas_call(final_kernel, grid=(2048 // wide,), in_specs=[tile, pl.Blo...  11.7 us
  transfers between devices with their start and end apart: 1, of which 1 were waited for; matrix products, arithmetic and copies ran while one was open for 0% of the time, Pallas kernels for 70%

profile of v6, /device:TPU:1, one launch (start us, length us, event | category | flops | bytes accessed | tf_op | source)
XLA Modules:
  0.0 219.0 jit_solution(2624604645304405354)
XLA Ops:
  7.2 0.0 all-gather.2.cloned.1.call-start
  7.2 0.7 all-gather.2.cloned.1.call-update
  7.9 152.4 %shard_map.67 = (f32[512,128]{1,0:T(8,128)}, f32[512,512]{1,0:T(8,128)}, bf16[8,512,512]{2,1,0:T(8,128)(2,1)}) custom-call(bf16[256,2048]{1,0:T(8,128)(2,1)} %a_ref.1, bf16[2,2,4,32,512]{4,3,2,1,0:T(8,128)(2,1)} %bitcast.1, f32[512,2048]{1,0:T(8,128)} %momentum.1, f32[2048,512]{1,0:T(8,128)} %q_ref.1), custom_call_target="tpu_custom_call" | custom-call | flops 17179869184 | bytes 134217728 | tf_op jit(solution)/shard_map/pallas_call | solution.py:434
  160.3 3.6 %all-gather.2.cloned.1.call-done.tokens = bf16[4096,2048]{1,0:T(8,128)(2,1)} async-done(((bf16[256,2048]{1,0:T(8,128)(2,1)}), bf16[4096,2048]{1,0:T(8,128)(2,1)}) %all-gather.2.cloned.1.call-update) | async-done | bytes 16777232 | tf_op jit(solution)/shard_map/all_gather | solution.py:601
  163.9 36.5 %shard_map.68 = (f32[4,4,2,256,128]{4,3,2,1,0:T(8,128)}, f32[512,2048]{1,0:T(8,128)}, f32[8,512]{1,0:T(8,128)}) custom-call(f32[512,128]{1,0:T(8,128)} %get-tuple-element.9.share, bf16[4096,2048]{1,0:T(8,128)(2,1)} %all-gather.2.cloned.1.call-done.tokens, bf16[8,512,512]{2,1,0:T(8,128)(2,1)} %get-tuple-element.10.turned, f32[512,2048]{1,0:T(8,128)} %momentum.1), custom_call_target="tpu_custom_call" | custom-call | flops 17179869184 | bytes 134217728 | tf_op jit(solution)/shard_map/pallas_call | solution.py:533
  200.4 11.7 %shard_map.69 = (f32[512,2048]{1,0:T(8,128)}, f32[2048,512]{1,0:T(8,128)}, bf16[512,2048]{1,0:T(8,128)(2,1)}) custom-call(f32[512,2048]{1,0:T(8,128)} %get-tuple-element.11.b_ref, f32[4,4,2,256,128]{4,3,2,1,0:T(8,128)} %get-tuple-element.12.r_ref, f32[512,512]{1,0:T(8,128)} %get-tuple-element.13.l_ref, f32[8,512]{1,0:T(8,128)} %get-tuple-element.14.n_ref), custom_call_target="tpu_custom_call" | custom-call | flops 4294967296 | bytes 20971520 | tf_op jit(solution)/shard_map/pallas_call | solution.py:579
Async XLA Ops:
  7.2 156.8 %all-gather.2.cloned.1.call-start = ((), (), s32[]{:S(2)}) async-start(), calls=%async_computation | async-start | bytes 17825792 | tf_op jit(solution)/shard_map/all_gather | solution.py:601
Sparse Core Ops, SparseCore 0:
  10.1 153.7 all-gather.1

commit v7 on v6

--- a/solution.py
+++ b/solution.py
@@ -213,13 +213,13 @@
 
 def chain_kernel(
     a_ref, g_ref, m_ref, q_ref,
-    solved, ortho, grads_out,
+    out, ortho, grads_out, scale,
     wt, left, gram, q_hi, q_lo, g_mine, z_part, z_pair, z_half, z_seen, z_all,
     part, pair, half, share,
     block, gx, gz,
     v_part, v_x, v_z, v_sx, v_sz, v_ex, v_ez, v_all,
     relay_x, relay_z, pass_x, pass_z, come_x, come_z, end_x, end_z,
-    g_all, g_turned, factor, inverse,
+    g_all, g_turned, factor, inverse, seen,
     send, recv, g_send, g_recv, out_sem,
 ):
     x, z, y, c = (lax.axis_index(a) for a in (X, Z, Y, C))
@@ -396,7 +396,6 @@
     g = sent(send, recv, 36, C, lambda to: g_all.at[:, c], lambda to: g_all.at[:, c])
     inv_hi, inv_lo = halves(inverse[...])
     last = ((1,), (1,))
-    ortho[...] = one(p_hi, inv_hi, last) + (one(p_hi, inv_lo, last) + one(p_lo, inv_hi, last))
     all_of(g)
 
     @pl.loop(0, 8)
@@ -408,8 +407,35 @@
     all_of(a)
     all_of(b)
     high, low = halves(jnp.concatenate([sum4(end_z), sum4(end_x)], axis=0))
-    solved[...] = one(inv_hi, high) + (one(inv_hi, low) + one(inv_lo, high))
+    own = one(inv_hi, high) + (one(inv_hi, low) + one(inv_lo, high))
+    out[x, z] = own.reshape(2, 256, 128)
+    a = sent(send, recv, 37, Z, lambda to: out.at[x, z, 0], lambda to: out.at[x, z, 0])
+    b = sent(send, recv, 38, X, lambda to: out.at[x, z, 1], lambda to: out.at[x, z, 1])
+    seen[0, c] = lax.dot_general(
+        jnp.ones((8, 128), F32), own * own, (((1,), (1,)), ((), ())),
+        precision=lax.Precision.HIGHEST, preferred_element_type=F32,
+    )
+    all_of(sent(send, recv, 39, C, lambda to: seen.at[0, c], lambda to: seen.at[0, c]))
+    seen[1, x] = seen[0, 0] + seen[0, 1]
+    q = sent(send, recv, 40, X, lambda to: seen.at[1, x], lambda to: seen.at[1, x])
+    all_of(q)
+    seen[2, z] = sum4(seen.at[1])
+    q = sent(send, recv, 41, Z, lambda to: seen.at[2, z], lambda to: seen.at[2, z])
+    all_of(a)
+    a = gather_begun(send, recv, 43, X, lambda at: out.at[at, :, 0])
+    all_of(b)
+    b = gather_begun(send, recv, 47, Z, lambda at: out.at[:, at, 1])
+    all_of(q)
+    seen[3, y] = sum4(seen.at[2])
+    q = sent(send, recv, 42, Y, lambda to: seen.at[3, y], lambda to: seen.at[3, y])
+    ortho[...] = one(p_hi, inv_hi, last) + (one(p_hi, inv_lo, last) + one(p_lo, inv_hi, last))
+    a = gather_relayed(send, recv, 43, X, a, lambda at, h: out.at[at, 2 * h : 2 * h + 2, 0])
+    b = gather_relayed(send, recv, 47, Z, b, lambda at, h: out.at[2 * h : 2 * h + 2, at, 1])
+    all_of(q)
+    scale[...] = jnp.sqrt(sum4(seen.at[3])) + EPSILON
     copy.wait()
+    all_of(a)
+    all_of(b)
 
 
 def chain(activations, grad_out, momentum, right_factor):
@@ -428,18 +454,19 @@
         ((2, 4, 256, 128), F32), ((2, 4, 256, 128), F32),
         ((4, 256, 128), F32), ((4, 256, 128), F32),
         ((4, 2, 2, 2, 4, 32, 512), BF16), ((8, 512, 512), BF16),
-        ((RANK, RANK), F32), ((RANK, RANK), F32),
+        ((RANK, RANK), F32), ((RANK, RANK), F32), ((4, 4, 8, RANK), F32),
     ]
-    semaphores = [(37, 3), (37, 3), (4, 2), (4, 2), ()]
+    semaphores = [(51, 3), (51, 3), (4, 2), (4, 2), ()]
     return pl.pallas_call(
         chain_kernel,
         out_shape=(
-            jax.ShapeDtypeStruct((RANK, 128), F32),
+            jax.ShapeDtypeStruct((4, 4, 2, 256, 128), F32),
             jax.ShapeDtypeStruct((RANK, RANK), F32),
             jax.ShapeDtypeStruct((8, 512, 512), BF16),
+            jax.ShapeDtypeStruct((8, RANK), F32),
         ),
         in_specs=[VMEM] * 4,
-        out_specs=(VMEM, VMEM, ANY),
+        out_specs=(VMEM, VMEM, ANY, VMEM),
         scratch_shapes=[pltpu.VMEM(*s) for s in big + shapes]
         + [pltpu.SemaphoreType.DMA(s) for s in semaphores],
         compiler_params=pltpu.CompilerParams(
@@ -449,116 +476,7 @@
     )(activations, grad_out.reshape(2, 2, 4, 32, 512), momentum, right_factor)
 
 
-def gather_kernel(
-    share, tokens, turned, momentum,
-    out, buffer, scale,
-    g_all, m_all, slots, sums, seen, send, recv, load_sem, tile_sem, store_sem,
-):
-    x, z, y, c = (lax.axis_index(a) for a in (X, Z, Y, C))
-
-    def tile(j):
-        slot = lax.rem(j, 2)
-        columns = pl.ds(pl.multiple_of(256 * j, 256), 256)
-        return pltpu.make_async_copy(tokens.at[:, columns], slots.at[slot], tile_sem.at[slot])
-
-    def store(j):
-        slot = lax.rem(j, 2)
-        columns = pl.ds(pl.multiple_of(256 * j, 256), 256)
-        return pltpu.make_async_copy(sums.at[slot], buffer.at[:, columns], store_sem.at[slot])
-
-    loads = [
-        pltpu.make_async_copy(turned.at[n], g_all.at[:, 512 * n : 512 * n + 512], load_sem.at[n])
-        for n in range(8)
-    ]
-    loads.append(pltpu.make_async_copy(momentum, m_all, load_sem.at[8]))
-    for load in loads:
-        load.start()
-    tile(0).start()
-    tile(1).start()
-    greet(line_peers((X, Z, Y, C)))
-    own = share[...]
-    out[x, z] = own.reshape(2, 256, 128)
-    a = sent(send, recv, 0, Z, lambda to: out.at[x, z, 0], lambda to: out.at[x, z, 0])
-    b = sent(send, recv, 1, X, lambda to: out.at[x, z, 1], lambda to: out.at[x, z, 1])
-    seen[0, c] = lax.dot_general(
-        jnp.ones((8, 128), F32), own * own, (((1,), (1,)), ((), ())),
-        precision=lax.Precision.HIGHEST, preferred_element_type=F32,
-    )
-    all_of(sent(send, recv, 2, C, lambda to: seen.at[0, c], lambda to: seen.at[0, c]))
-    seen[1, x] = seen[0, 0] + seen[0, 1]
-    q = sent(send, recv, 3, X, lambda to: seen.at[1, x], lambda to: seen.at[1, x])
-    for load in loads:
-        load.wait()
-    all_of(q)
-    seen[2, z] = sum4(seen.at[1])
-    q = sent(send, recv, 4, Z, lambda to: seen.at[2, z], lambda to: seen.at[2, z])
-    all_of(a)
-    a = gather_begun(send, recv, 6, X, lambda at: out.at[at, :, 0])
-    all_of(b)
-    b = gather_begun(send, recv, 10, Z, lambda at: out.at[:, at, 1])
-    all_of(q)
-    seen[3, y] = sum4(seen.at[2])
-    q = sent(send, recv, 5, Y, lambda to: seen.at[3, y], lambda to: seen.at[3, y])
-
-    def gradient(begin, end):
-        @pl.loop(begin, end)
-        def _(j):
-            slot = lax.rem(j, 2)
-            columns = pl.ds(pl.multiple_of(256 * j, 256), 256)
-            tile(j).wait()
-
-            @pl.when(j >= 2)
-            def _():
-                store(j - 2).wait()
-
-            sums[slot] = m_all[:, columns] + one(g_all[...], slots[slot])
-            store(j).start()
-
-            @pl.when(j < 6)
-            def _():
-                tile(j + 2).start()
-
-    gradient(0, 8)
-    a = gather_relayed(send, recv, 6, X, a, lambda at, h: out.at[at, 2 * h : 2 * h + 2, 0])
-    b = gather_relayed(send, recv, 10, Z, b, lambda at, h: out.at[2 * h : 2 * h + 2, at, 1])
-    all_of(q)
-    scale[...] = jnp.sqrt(sum4(seen.at[3])) + EPSILON
-    store(6).wait()
-    store(7).wait()
-    all_of(a)
-    all_of(b)
-
-
-def gathered(share, activations, grads, momentum):
-    return pl.pallas_call(
-        gather_kernel,
-        out_shape=(
-            jax.ShapeDtypeStruct((4, 4, 2, 256, 128), F32),
-            jax.ShapeDtypeStruct((RANK, 2048), F32),
-            jax.ShapeDtypeStruct((8, RANK), F32),
-        ),
-        in_specs=[VMEM, ANY, ANY, ANY],
-        out_specs=(VMEM, ANY, VMEM),
-        scratch_shapes=[
-            pltpu.VMEM((512, 4096), BF16),
-            pltpu.VMEM((RANK, 2048), F32),
-            pltpu.VMEM((2, 4096, 256), BF16),
-            pltpu.VMEM((2, RANK, 256), F32),
-            pltpu.VMEM((4, 4, 8, RANK), F32),
-            pltpu.SemaphoreType.DMA((14, 3)),
-            pltpu.SemaphoreType.DMA((14, 3)),
-            pltpu.SemaphoreType.DMA((9,)),
-            pltpu.SemaphoreType.DMA((2,)),
-            pltpu.SemaphoreType.DMA((2,)),
-        ],
-        compiler_params=pltpu.CompilerParams(
-            collective_id=2, has_side_effects=True, vmem_limit_bytes=58 << 20
-        ),
-        cost_estimate=pl.CostEstimate(flops=1 << 34, bytes_accessed=128 << 20, transcendentals=0),
-    )(share, activations, grads, momentum)
-
-
-def final_kernel(b_ref, r_ref, l_ref, n_ref, momentum, right, update, low_ref, s_hi, s_lo, inv_ref):
+def final_kernel(a_ref, g_ref, m_ref, r_ref, l_ref, n_ref, momentum, right, update, low_ref, s_hi, s_lo, inv_ref):
     @pl.when(pl.program_id(0) == 0)
     def _():
         ortho = l_ref[...]
@@ -568,18 +486,23 @@
 
     raw = jnp.concatenate([r_ref[0, k].reshape(RANK, 128) for k in range(2)], axis=1)
     r_hi, r_lo = halves(raw)
-    momentum[...] = b_ref[...] - one(low_ref[...], r_hi)
+    buffer = m_ref[...] - one(low_ref[...], r_hi)
+    for n in range(8):
+        buffer = buffer + one(g_ref[n], a_ref[512 * n : 512 * n + 512, :])
+    momentum[...] = buffer
     update[...] = (one(s_hi[...], r_hi) + (one(s_hi[...], r_lo) + one(s_lo[...], r_hi))).astype(BF16)
     right[...] = raw.T * inv_ref[0:1, :]
 
 
-def final(buffer, right_t, left, norms):
+def final(activations, grads, momentum, right_t, left, norms):
     wide = 256
     tile = pl.BlockSpec((RANK, wide), lambda j: (0, j))
     return pl.pallas_call(
         final_kernel,
         grid=(2048 // wide,),
         in_specs=[
+            pl.BlockSpec((4096, wide), lambda j: (0, j)),
+            pl.BlockSpec((8, 512, 512), lambda j: (0, 0, 0), pipeline_mode=pl.Buffered(1)),
             tile,
             pl.BlockSpec((1, 2, 2, 256, 128), lambda j: (j // 2, j % 2, 0, 0, 0)),
             pl.BlockSpec((RANK, RANK), lambda j: (0, 0)),
@@ -594,14 +517,13 @@
         scratch_shapes=[pltpu.VMEM((RANK, RANK), BF16)] * 3 + [pltpu.VMEM((8, RANK), F32)],
         compiler_params=pltpu.CompilerParams(vmem_limit_bytes=60 << 20),
         cost_estimate=pl.CostEstimate(flops=1 << 32, bytes_accessed=20 << 20, transcendentals=0),
-    )(buffer, right_t, left, norms)
+    )(activations, grads, momentum, right_t, left, norms)
 
 
 def body(activations, grad_out, momentum, right_factor):
     all_activations = lax.all_gather(activations, WIDE, axis=0, tiled=True)
-    share, ortho_left, grads = chain(activations, grad_out, momentum, right_factor)
-    right_t, buffer, norms = gathered(share, all_activations, grads, momentum)
-    return final(buffer, right_t, ortho_left, norms)
+    right_t, ortho_left, grads, norms = chain(activations, grad_out, momentum, right_factor)
+    return final(all_activations, grads, momentum, right_t, ortho_left, norms)
 
 
 def solution(mesh):

time: 220 us -> 224 us (1.018)
  Pallas kernels: 201 us -> 206 us
  waiting for transfers between devices: 4.26 us -> 0.7 us
    pallas_call x3 -> x2, Pallas kernels: 201 us -> 206 us  [the longest x1 185 us: chain(): pl.pallas_call(chain_kernel, out_shape=(jax.ShapeDtypeStruct((4, 4, 2, 25...]
    all_gather x1, waiting for transfers between devices: 3.58 us -> 0.02 us  [body(): all_activations = lax.all_gather(activations, WIDE, axis=0, tiled=True)]
  transfers between devices with their start and end apart: 1 -> 1, of which waited for: 1 -> 0; matrix products, arithmetic and copies ran while one was open for 0% -> 0% of each run, Pallas kernels for 70% -> 84%
where the time goes in v7:
time: 224 us; the launch traced here: 221 us
  Pallas kernels  206 us (92%)
  between operations  14 us (6%)
    pallas_call x1, Pallas kernels, chain(): pl.pallas_call(chain_kernel, out_shape=(jax.ShapeDtypeStruct((4, 4, 2, 25...  185 us
    pallas_call x1, Pallas kernels, final(): pl.pallas_call(final_kernel, grid=(2048 // wide,), in_specs=[pl.BlockSpec...  21.2 us
  transfers between devices with their start and end apart: 1, of which 0 were waited for; matrix products, arithmetic and copies ran while one was open for 0% of the time, Pallas kernels for 84%

profile of v7, /device:TPU:1, one launch (start us, length us, event | category | flops | bytes accessed | tf_op | source)
XLA Modules:
  0.0 220.9 jit_solution(18016837013792076117)
XLA Ops:
  7.2 0.0 all-gather.2.cloned.1.call-start
  7.2 0.7 all-gather.2.cloned.1.call-update
  7.9 185.0 %shard_map.67 = (f32[4,4,2,256,128]{4,3,2,1,0:T(8,128)}, f32[512,512]{1,0:T(8,128)}, bf16[8,512,512]{2,1,0:T(8,128)(2,1)}, f32[8,512]{1,0:T(8,128)}) custom-call(bf16[256,2048]{1,0:T(8,128)(2,1)} %a_ref.1, bf16[2,2,4,32,512]{4,3,2,1,0:T(8,128)(2,1)} %bitcast.1, f32[512,2048]{1,0:T(8,128)} %m_ref.3, f32[2048,512]{1,0:T(8,128)} %q_ref.1), custom_call_target="tpu_custom_call" | custom-call | flops 17179869184 | bytes 134217728 | tf_op jit(solution)/shard_map/pallas_call | solution.py:460
  192.9 0.0 all-gather.2.cloned.1.call-done.a_ref
  192.9 21.2 %shard_map.68 = (f32[512,2048]{1,0:T(8,128)}, f32[2048,512]{1,0:T(8,128)}, bf16[512,2048]{1,0:T(8,128)(2,1)}) custom-call(bf16[4096,2048]{1,0:T(8,128)(2,1)} %all-gather.2.cloned.1.call-done.a_ref, bf16[8,512,512]{2,1,0:T(8,128)(2,1)} %get-tuple-element.7.g_ref, f32[512,2048]{1,0:T(8,128)} %m_ref.3, f32[4,4,2,256,128]{4,3,2,1,0:T(8,128)} %get-tuple-element.8.r_ref, ...), custom_call_target="tpu_custom_call" | custom-call | flops 4294967296 | bytes 20971520 | tf_op jit(solution)/shard_map/pallas_call | solution.py:500
Async XLA Ops:
  7.2 185.7 %all-gather.2.cloned.1.call-start = ((), (), s32[]{:S(2)}) async-start(), calls=%async_computation | async-start | bytes 17825792 | tf_op jit(solution)/shard_map/all_gather | solution.py:524
Sparse Core Ops, SparseCore 0:
  10.1 156.5 all-gather.1

commit v8 on v6

--- a/solution.py
+++ b/solution.py
@@ -114,6 +114,7 @@
 
 
 ANY = pl.BlockSpec(memory_space=pl.ANY)
+HBM = pl.BlockSpec(memory_space=pltpu.HBM)
 
 
 def line_peers(axes):
@@ -537,7 +538,7 @@
             jax.ShapeDtypeStruct((RANK, 2048), F32),
             jax.ShapeDtypeStruct((8, RANK), F32),
         ),
-        in_specs=[VMEM, ANY, ANY, ANY],
+        in_specs=[VMEM, HBM, HBM, HBM],
         out_specs=(VMEM, ANY, VMEM),
         scratch_shapes=[
             pltpu.VMEM((512, 4096), BF16),
@@ -552,7 +553,7 @@
             pltpu.SemaphoreType.DMA((2,)),
         ],
         compiler_params=pltpu.CompilerParams(
-            collective_id=2, has_side_effects=True, vmem_limit_bytes=58 << 20
+            collective_id=2, has_side_effects=True, vmem_limit_bytes=42 << 20
         ),
         cost_estimate=pl.CostEstimate(flops=1 << 34, bytes_accessed=128 << 20, transcendentals=0),
     )(share, activations, grads, momentum)
@@ -566,7 +567,7 @@
         low_ref[...] = (FEEDBACK * ortho).astype(BF16)
         s_hi[...], s_lo[...] = halves(ortho * (math.sqrt(DOUT * DIN / RANK) * inv_ref[0:1, :]))
 
-    raw = jnp.concatenate([r_ref[0, k].reshape(RANK, 128) for k in range(2)], axis=1)
+    raw = jnp.concatenate([r_ref[0, k].reshape(RANK, 128) for k in range(4)], axis=1)
     r_hi, r_lo = halves(raw)
     momentum[...] = b_ref[...] - one(low_ref[...], r_hi)
     update[...] = (one(s_hi[...], r_hi) + (one(s_hi[...], r_lo) + one(s_lo[...], r_hi))).astype(BF16)
@@ -574,14 +575,14 @@
 
 
 def final(buffer, right_t, left, norms):
-    wide = 256
+    wide = 512
     tile = pl.BlockSpec((RANK, wide), lambda j: (0, j))
     return pl.pallas_call(
         final_kernel,
         grid=(2048 // wide,),
         in_specs=[
             tile,
-            pl.BlockSpec((1, 2, 2, 256, 128), lambda j: (j // 2, j % 2, 0, 0, 0)),
+            pl.BlockSpec((1, 4, 2, 256, 128), lambda j: (j, 0, 0, 0, 0)),
             pl.BlockSpec((RANK, RANK), lambda j: (0, 0)),
             pl.BlockSpec((8, RANK), lambda j: (0, 0)),
         ],
@@ -592,7 +593,7 @@
             jax.ShapeDtypeStruct((RANK, 2048), BF16),
         ),
         scratch_shapes=[pltpu.VMEM((RANK, RANK), BF16)] * 3 + [pltpu.VMEM((8, RANK), F32)],
-        compiler_params=pltpu.CompilerParams(vmem_limit_bytes=60 << 20),
+        compiler_params=pltpu.CompilerParams(vmem_limit_bytes=24 << 20),
         cost_estimate=pl.CostEstimate(flops=1 << 32, bytes_accessed=20 << 20, transcendentals=0),
     )(buffer, right_t, left, norms)
 

time: 220 us -> 214 us (0.973)
  Pallas kernels: 201 us -> 194 us
    pallas_call x1, Pallas kernels: 11.7 us -> 7.15 us  [final(): pl.pallas_call(final_kernel, grid=(2048 // wide,), in_specs=[tile, pl.Blo...]
    pallas_call x1, Pallas kernels: 36.5 us -> 34.3 us  [gathered(): pl.pallas_call(gather_kernel, out_shape=(jax.ShapeDtypeStruct((4, 4, 2, 2...]
  transfers between devices with their start and end apart: 1 -> 1, of which waited for: 1 -> 1; matrix products, arithmetic and copies ran while one was open for 0% -> 0% of each run, Pallas kernels for 70% -> 71%
where the time goes in v8:
time: 214 us; the launch traced here: 213 us
  Pallas kernels  194 us (91%)
  between operations  14.1 us (7%)
  waiting for transfers between devices  4.33 us (2%)
    pallas_call x1, Pallas kernels, chain(): pl.pallas_call(chain_kernel, out_shape=(jax.ShapeDtypeStruct((RANK, 128),...  152 us
    pallas_call x1, Pallas kernels, gathered(): pl.pallas_call(gather_kernel, out_shape=(jax.ShapeDtypeStruct((4, 4, 2, 2...  34.3 us
    pallas_call x1, Pallas kernels, final(): pl.pallas_call(final_kernel, grid=(2048 // wide,), in_specs=[tile, pl.Blo...  7.15 us
  transfers between devices with their start and end apart: 1, of which 1 were waited for; matrix products, arithmetic and copies ran while one was open for 0% of the time, Pallas kernels for 71%

profile of v8, /device:TPU:1, one launch (start us, length us, event | category | flops | bytes accessed | tf_op | source)
XLA Modules:
  0.0 213.2 jit_solution(13119844452446710308)
XLA Ops:
  7.2 0.0 all-gather.2.cloned.1.call-start
  7.2 0.7 all-gather.2.cloned.1.call-update
  7.9 152.4 %shard_map.67 = (f32[512,128]{1,0:T(8,128)}, f32[512,512]{1,0:T(8,128)}, bf16[8,512,512]{2,1,0:T(8,128)(2,1)}) custom-call(bf16[256,2048]{1,0:T(8,128)(2,1)} %a_ref.1, bf16[2,2,4,32,512]{4,3,2,1,0:T(8,128)(2,1)} %bitcast.1, f32[512,2048]{1,0:T(8,128)} %momentum.1, f32[2048,512]{1,0:T(8,128)} %q_ref.1), custom_call_target="tpu_custom_call" | custom-call | flops 17179869184 | bytes 134217728 | tf_op jit(solution)/shard_map/pallas_call | solution.py:435
  160.3 3.6 %all-gather.2.cloned.1.call-done.tokens = bf16[4096,2048]{1,0:T(8,128)(2,1)} async-done(((bf16[256,2048]{1,0:T(8,128)(2,1)}), bf16[4096,2048]{1,0:T(8,128)(2,1)}) %all-gather.2.cloned.1.call-update) | async-done | bytes 16777232 | tf_op jit(solution)/shard_map/all_gather | solution.py:602
  163.9 0.0 copy-start.1
  163.9 0.9 copy-done.1
  164.9 0.0 copy-start
  164.9 34.3 %shard_map.68 = (f32[4,4,2,256,128]{4,3,2,1,0:T(8,128)S(1)}, f32[512,2048]{1,0:T(8,128)S(1)}, f32[8,512]{1,0:T(8,128)S(1)}) custom-call(f32[512,128]{1,0:T(8,128)S(1)} %copy-done.1, bf16[4096,2048]{1,0:T(8,128)(2,1)} %all-gather.2.cloned.1.call-done.tokens, bf16[8,512,512]{2,1,0:T(8,128)(2,1)} %get-tuple-element.10.turned, f32[512,2048]{1,0:T(8,128)} %momentum.1), custom_call_target="tpu_custom_call" | custom-call | flops 17179869184 | bytes 134217728 | tf_op jit(solution)/shard_map/pallas_call | solution.py:534
  199.2 0.0 copy-done
  199.2 7.1 %shard_map.69 = (f32[512,2048]{1,0:T(8,128)}, f32[2048,512]{1,0:T(8,128)}, bf16[512,2048]{1,0:T(8,128)(2,1)}) custom-call(f32[512,2048]{1,0:T(8,128)S(1)} %get-tuple-element.11.b_ref, f32[4,4,2,256,128]{4,3,2,1,0:T(8,128)S(1)} %get-tuple-element.12.r_ref, f32[512,512]{1,0:T(8,128)S(1)} %copy-done, f32[8,512]{1,0:T(8,128)S(1)} %get-tuple-element.14.n_ref), custom_call_target="tpu_custom_call" | custom-call | flops 4294967296 | bytes 20971520 | tf_op jit(solution)/shard_map/pallas_call | solution.py:580
Async XLA Ops:
  7.2 156.8 %all-gather.2.cloned.1.call-start = ((), (), s32[]{:S(2)}) async-start(), calls=%async_computation | async-start | bytes 17825792 | tf_op jit(solution)/shard_map/all_gather | solution.py:602
  163.9 0.9 copy-start.1
  164.9 34.3 %copy-start = (f32[512,512]{1,0:T(8,128)S(1)}, f32[512,512]{1,0:T(8,128)}, u32[]{:S(2)}) copy-start(f32[512,512]{1,0:T(8,128)} %get-tuple-element.13.l_ref) | copy-start | bytes 3145732
Sparse Core Ops, SparseCore 0:
  10.1 153.7 all-gather.1

commit v9 on v8

--- a/solution.py
+++ b/solution.py
@@ -519,9 +519,10 @@
             def _():
                 tile(j + 2).start()
 
-    gradient(0, 8)
+    gradient(0, 6)
     a = gather_relayed(send, recv, 6, X, a, lambda at, h: out.at[at, 2 * h : 2 * h + 2, 0])
     b = gather_relayed(send, recv, 10, Z, b, lambda at, h: out.at[2 * h : 2 * h + 2, at, 1])
+    gradient(6, 8)
     all_of(q)
     scale[...] = jnp.sqrt(sum4(seen.at[3])) + EPSILON
     store(6).wait()

time: 214 us -> 213 us (level)
  transfers between devices with their start and end apart: 1 -> 1, of which waited for: 1 -> 1; matrix products, arithmetic and copies ran while one was open for 0% -> 0% of each run, Pallas kernels for 71% -> 72%
where the time goes in v9:
time: 213 us; the launch traced here: 212 us
  Pallas kernels  193 us (91%)
  between operations  14.1 us (7%)
  waiting for transfers between devices  4.33 us (2%)
    pallas_call x1, Pallas kernels, chain(): pl.pallas_call(chain_kernel, out_shape=(jax.ShapeDtypeStruct((RANK, 128),...  152 us
    pallas_call x1, Pallas kernels, gathered(): pl.pallas_call(gather_kernel, out_shape=(jax.ShapeDtypeStruct((4, 4, 2, 2...  33.1 us
    pallas_call x1, Pallas kernels, final(): pl.pallas_call(final_kernel, grid=(2048 // wide,), in_specs=[tile, pl.Blo...  7.15 us
  transfers between devices with their start and end apart: 1, of which 1 were waited for; matrix products, arithmetic and copies ran while one was open for 0% of the time, Pallas kernels for 72%

profile of v9, /device:TPU:1, one launch (start us, length us, event | category | flops | bytes accessed | tf_op | source)
XLA Modules:
  0.0 211.9 jit_solution(9829054620587047774)
XLA Ops:
  7.2 0.0 all-gather.2.cloned.1.call-start
  7.2 0.7 all-gather.2.cloned.1.call-update
  7.9 152.4 %shard_map.67 = (f32[512,128]{1,0:T(8,128)}, f32[512,512]{1,0:T(8,128)}, bf16[8,512,512]{2,1,0:T(8,128)(2,1)}) custom-call(bf16[256,2048]{1,0:T(8,128)(2,1)} %a_ref.1, bf16[2,2,4,32,512]{4,3,2,1,0:T(8,128)(2,1)} %bitcast.1, f32[512,2048]{1,0:T(8,128)} %momentum.1, f32[2048,512]{1,0:T(8,128)} %q_ref.1), custom_call_target="tpu_custom_call" | custom-call | flops 17179869184 | bytes 134217728 | tf_op jit(solution)/shard_map/pallas_call | solution.py:435
  160.3 3.6 %all-gather.2.cloned.1.call-done.tokens = bf16[4096,2048]{1,0:T(8,128)(2,1)} async-done(((bf16[256,2048]{1,0:T(8,128)(2,1)}), bf16[4096,2048]{1,0:T(8,128)(2,1)}) %all-gather.2.cloned.1.call-update) | async-done | bytes 16777232 | tf_op jit(solution)/shard_map/all_gather | solution.py:603
  163.9 0.0 copy-start.1
  163.9 0.9 copy-done.1
  164.9 0.0 copy-start
  164.9 33.1 %shard_map.68 = (f32[4,4,2,256,128]{4,3,2,1,0:T(8,128)S(1)}, f32[512,2048]{1,0:T(8,128)S(1)}, f32[8,512]{1,0:T(8,128)S(1)}) custom-call(f32[512,128]{1,0:T(8,128)S(1)} %copy-done.1, bf16[4096,2048]{1,0:T(8,128)(2,1)} %all-gather.2.cloned.1.call-done.tokens, bf16[8,512,512]{2,1,0:T(8,128)(2,1)} %get-tuple-element.10.turned, f32[512,2048]{1,0:T(8,128)} %momentum.1), custom_call_target="tpu_custom_call" | custom-call | flops 17179869184 | bytes 134217728 | tf_op jit(solution)/shard_map/pallas_call | solution.py:535
  197.9 0.0 copy-done
  197.9 7.1 %shard_map.69 = (f32[512,2048]{1,0:T(8,128)}, f32[2048,512]{1,0:T(8,128)}, bf16[512,2048]{1,0:T(8,128)(2,1)}) custom-call(f32[512,2048]{1,0:T(8,128)S(1)} %get-tuple-element.11.b_ref, f32[4,4,2,256,128]{4,3,2,1,0:T(8,128)S(1)} %get-tuple-element.12.r_ref, f32[512,512]{1,0:T(8,128)S(1)} %copy-done, f32[8,512]{1,0:T(8,128)S(1)} %get-tuple-element.14.n_ref), custom_call_target="tpu_custom_call" | custom-call | flops 4294967296 | bytes 20971520 | tf_op jit(solution)/shard_map/pallas_call | solution.py:581
Async XLA Ops:
  7.2 156.8 %all-gather.2.cloned.1.call-start = ((), (), s32[]{:S(2)}) async-start(), calls=%async_computation | async-start | bytes 17825792 | tf_op jit(solution)/shard_map/all_gather | solution.py:603
  163.9 0.9 copy-start.1
  164.9 33.1 %copy-start = (f32[512,512]{1,0:T(8,128)S(1)}, f32[512,512]{1,0:T(8,128)}, u32[]{:S(2)}) copy-start(f32[512,512]{1,0:T(8,128)} %get-tuple-element.13.l_ref) | copy-start | bytes 3145732
Sparse Core Ops, SparseCore 0:
  10.1 153.7 all-gather.1
